TPU v7x, 128 devices: a whole 4x4x4 slice. The times are simulated.
128 devices in a mesh: seq: 4 (over y_lo, core), fsdp: 32 (over y_hi, x, z).
Axes of the slice: x: 4, y: 4 (y_hi: 2, y_lo: 2; y = y_hi * 2 + y_lo), z: 4, core: 2. Of those that a mesh axis runs over, the one named last changes fastest.
Arguments:
- tokens: bfloat16 [32, 1024, 1024], P('fsdp', 'seq'), may hold values from -6 to 6
- norm1_gain: bfloat16 [1024], P(('seq', 'fsdp')), may hold values from 0.099609375 to 1.8984375
- query_weight: bfloat16 [1024, 1024], P(('seq', 'fsdp')), may hold values from -0.1875 to 0.1875
- key_weight: bfloat16 [1024, 512], P(('seq', 'fsdp')), may hold values from -0.1875 to 0.1875
- value_weight: bfloat16 [1024, 512], P(('seq', 'fsdp')), may hold values from -0.1875 to 0.1875
- output_weight: bfloat16 [1024, 1024], P(('seq', 'fsdp')), may hold values from -1.5 to 1.5
- norm2_gain: bfloat16 [1024], P(('seq', 'fsdp')), may hold values from 0.099609375 to 1.8984375
- router_weight: bfloat16 [1024, 32], P(('seq', 'fsdp')), may hold values from -0.09375 to 0.09375
- expert_gate: bfloat16 [32, 1024, 512], P('fsdp', 'seq'), may hold values from -0.1875 to 0.1875
- expert_up: bfloat16 [32, 1024, 512], P('fsdp', 'seq'), may hold values from -0.1875 to 0.1875
- expert_down: bfloat16 [32, 512, 1024], P('fsdp', 'seq'), may hold values from -1 to 1
- routes: int32 [32, 1024, 8], P('fsdp', 'seq'), may hold values from 0 to 31, all different within a row; in each aligned block of 256 rows (0 to 255, 256 to 511, ..., all dimensions but the last counted through in order) at most 80 rows name the same one
- cotangent: bfloat16 [32, 1024, 1024], P('fsdp', 'seq'), may hold values from -6 to 6
Outputs:
- output: bfloat16 [32, 1024, 1024], P('fsdp', 'seq')
- grad_tokens: float32 [32, 1024, 1024], P('fsdp', 'seq')
- grad_norm1_gain: float32 [1024], P(('seq', 'fsdp'))
- grad_query_weight: float32 [1024, 1024], P(('seq', 'fsdp'))
- grad_key_weight: float32 [1024, 512], P(('seq', 'fsdp'))
- grad_value_weight: float32 [1024, 512], P(('seq', 'fsdp'))
- grad_output_weight: float32 [1024, 1024], P(('seq', 'fsdp'))
- grad_norm2_gain: float32 [1024], P(('seq', 'fsdp'))
- grad_router_weight: float32 [1024, 32], P(('seq', 'fsdp'))
- grad_expert_gate: float32 [32, 1024, 512], P('fsdp', 'seq')
- grad_expert_up: float32 [32, 1024, 512], P('fsdp', 'seq')
- grad_expert_down: float32 [32, 512, 1024], P('fsdp', 'seq')
Inputs may be any that keep to these rules, and one draw needn't show every extreme that they name: `routes`: each row names 8 different experts. In each aligned block of 256 rows (the tokens of one device) no expert is named by more than 80 rows, a bound that some block reaches.
All inputs are finite; a program needn't handle non-finite values.
Results may differ from a plain program's by a relative error of at most 0.02.
Values may be sent and summed in bfloat16 or wider, within the bound.
No kernel may reach another device: no remote copies, remote signals or barrier semaphores. Data moves between devices by JAX's collectives and lax.ppermute only.
A program may use at most 192 MiB of HBM per device.

v0:
```python
import jax
import jax.numpy as jnp
from jax import lax
from jax.sharding import PartitionSpec as P

HEADS = 16
KV_HEADS = 8
HEAD = 64
TOPK = 8
CAP = 80


epsilon = 1e-06
rope_base = 10000.0


def rope_angles(positions, head_size):
    half_size = head_size // 2
    freqs = rope_base ** (-2.0 * jnp.arange(half_size).astype(jnp.float32) / head_size)
    angles = positions.astype(jnp.float32)[:, None] * freqs[None, :]
    return (jnp.cos(angles), jnp.sin(angles))


def rotate(values, angle_cos, angle_sin):
    half_size = values.shape[-1] // 2
    first_half = values[..., :half_size]
    second_half = values[..., half_size:]
    cos_part = angle_cos[:, None, :]
    sin_part = angle_sin[:, None, :]
    return jnp.concatenate(
        [
            first_half * cos_part - second_half * sin_part,
            second_half * cos_part + first_half * sin_part,
        ],
        axis=-1,
    )


def unrotate(grads, angle_cos, angle_sin):
    half_size = grads.shape[-1] // 2
    first_half = grads[..., :half_size]
    second_half = grads[..., half_size:]
    cos_part = angle_cos[:, None, :]
    sin_part = angle_sin[:, None, :]
    return jnp.concatenate(
        [
            first_half * cos_part + second_half * sin_part,
            second_half * cos_part - first_half * sin_part,
        ],
        axis=-1,
    )


def norm_forward(values, gain_vec):
    factor = lax.rsqrt(jnp.mean(values * values, axis=-1, keepdims=True) + epsilon)
    normed = values * factor
    return (normed, factor, normed * gain_vec.astype(jnp.float32))


def norm_backward(grad_out, normed, factor, gain_vec):
    grad_normed = grad_out * gain_vec.astype(jnp.float32)
    grad_gain = jnp.sum(grad_out * normed, axis=0)
    grad_in = factor * (
        grad_normed - normed * jnp.mean(grad_normed * normed, axis=-1, keepdims=True)
    )
    return (grad_in, grad_gain)


def block_scores(query_block, key_rows, row_start):
    head_size = query_block.shape[-1]
    raw = jnp.einsum("qjgd,kjd->jgqk", query_block, key_rows, preferred_element_type=jnp.float32)
    scores = raw * head_size ** (-0.5)
    rows = row_start + jnp.arange(query_block.shape[0])
    columns = jnp.arange(key_rows.shape[0])
    return jnp.where(columns[None, :] <= rows[:, None], scores, -1e30)


def on_device(
    tokens,
    norm1_gain,
    query_weight,
    key_weight,
    value_weight,
    output_weight,
    norm2_gain,
    router_weight,
    expert_gate,
    expert_up,
    expert_down,
    routes,
    cotangent,
):
    tok_count = tokens.shape[1]
    model_width = tokens.shape[2]
    seq_size = lax.axis_size("seq")
    fsdp_size = lax.axis_size("fsdp")
    experts_all = router_weight.shape[1]
    local_experts = expert_gate.shape[0]
    kv_local = KV_HEADS // seq_size
    group_size = HEADS // KV_HEADS
    length = tok_count * seq_size
    row_block = min(512, length)
    block_count = length // row_block
    score_scale = HEAD ** (-0.5)
    dense = (
        lax.all_gather(norm1_gain, ("seq", "fsdp"), axis=0, tiled=True),
        lax.all_gather(query_weight, ("seq", "fsdp"), axis=0, tiled=True),
        lax.all_gather(key_weight, ("seq", "fsdp"), axis=0, tiled=True),
        lax.all_gather(value_weight, ("seq", "fsdp"), axis=0, tiled=True),
        lax.all_gather(output_weight, ("seq", "fsdp"), axis=0, tiled=True),
        lax.all_gather(norm2_gain, ("seq", "fsdp"), axis=0, tiled=True),
        lax.all_gather(router_weight, ("seq", "fsdp"), axis=0, tiled=True),
    )
    experts = (
        lax.all_gather(expert_gate, "seq", axis=1, tiled=True),
        lax.all_gather(expert_up, "seq", axis=1, tiled=True),
        lax.all_gather(expert_down, "seq", axis=1, tiled=True),
    )
    gain_one, query_w, key_w, value_w, output_w, gain_two, router_w = dense
    gate_w, up_w, down_w = experts
    inputs = tokens.reshape(tok_count, model_width).astype(jnp.float32)
    normed_one, factor_one, pre_one = norm_forward(inputs, gain_one)
    hidden_one = pre_one.astype(jnp.bfloat16)
    positions = lax.axis_index("seq") * tok_count + jnp.arange(tok_count)
    local_cos, local_sin = rope_angles(positions, HEAD)
    query_pre = jnp.dot(hidden_one, query_w, preferred_element_type=jnp.float32).reshape(
        tok_count, HEADS, HEAD
    )
    query_tok = (
        rotate(query_pre, local_cos, local_sin)
        .astype(jnp.bfloat16)
        .reshape(tok_count, seq_size, -1)
    )
    key_pre = jnp.dot(hidden_one, key_w, preferred_element_type=jnp.float32).reshape(
        tok_count, KV_HEADS, HEAD
    )
    key_tok = (
        rotate(key_pre, local_cos, local_sin).astype(jnp.bfloat16).reshape(tok_count, seq_size, -1)
    )
    value_tok = (
        jnp.dot(hidden_one, value_w, preferred_element_type=jnp.float32)
        .astype(jnp.bfloat16)
        .reshape(tok_count, seq_size, -1)
    )
    query_heads, key_heads, value_heads = (
        lax.all_to_all(query_tok, "seq", split_axis=1, concat_axis=0, tiled=True),
        lax.all_to_all(key_tok, "seq", split_axis=1, concat_axis=0, tiled=True),
        lax.all_to_all(value_tok, "seq", split_axis=1, concat_axis=0, tiled=True),
    )
    query_blocks = query_heads.reshape(block_count, row_block, kv_local, group_size, HEAD)
    key_rows = key_heads.reshape(length, kv_local, HEAD)
    value_rows = value_heads.reshape(length, kv_local, HEAD)
    starts = jnp.arange(block_count) * row_block

    def forward_block(pieces):
        query_block, row_start = pieces
        scores = block_scores(query_block, key_rows, row_start)
        row_peak = jnp.max(scores, axis=-1, keepdims=True)
        exp_scores = jnp.exp(scores - row_peak)
        row_total = jnp.sum(exp_scores, axis=-1, keepdims=True)
        attn_probs = (exp_scores / row_total).astype(jnp.bfloat16)
        mixed = jnp.einsum(
            "jgqk,kjd->qjgd", attn_probs, value_rows, preferred_element_type=jnp.float32
        )
        return (mixed.astype(jnp.bfloat16), (row_peak + jnp.log(row_total))[..., 0])

    mixed_blocks, log_totals = lax.map(forward_block, (query_blocks, starts))
    mixed_heads = mixed_blocks.reshape(length, 1, -1)
    mixed_tok = lax.all_to_all(mixed_heads, "seq", split_axis=0, concat_axis=1, tiled=True).reshape(
        tok_count, -1
    )
    residual = inputs + jnp.dot(mixed_tok, output_w, preferred_element_type=jnp.float32)
    normed_two, factor_two, pre_two = norm_forward(residual, gain_two)
    hidden_two = pre_two.astype(jnp.bfloat16)
    logits = jnp.dot(hidden_two, router_w, preferred_element_type=jnp.float32)
    choice_rows = routes.reshape(tok_count, TOPK)
    expert_ids = jnp.arange(experts_all)
    picker = (choice_rows[:, :, None] == expert_ids[None, None, :]).astype(jnp.float32)
    chosen = jnp.sum(logits[:, None, :] * picker, axis=-1)
    chosen_exp = jnp.exp(chosen - jnp.max(chosen, axis=-1, keepdims=True))
    gates = chosen_exp / jnp.sum(chosen_exp, axis=-1, keepdims=True)
    flat_expert = choice_rows.reshape(-1)
    onehot = (flat_expert[:, None] == expert_ids[None, :]).astype(jnp.int32)
    slot_rank = jnp.sum((jnp.cumsum(onehot, axis=0) - onehot) * onehot, axis=1)
    slot_index = slot_rank * experts_all + flat_expert
    owners = jnp.arange(tok_count * TOPK) // TOPK
    slot_owner = jnp.zeros((CAP * experts_all,), jnp.int32).at[slot_index].set(owners)
    slot_used = jnp.zeros((CAP * experts_all, 1), jnp.bfloat16).at[slot_index].set(1.0)
    sent_rows = (hidden_two[slot_owner] * slot_used).reshape(CAP, experts_all, model_width)
    arrived = lax.all_to_all(sent_rows, "fsdp", split_axis=1, concat_axis=1, tiled=True)
    slot_count = arrived.shape[0]
    grouped = arrived.reshape(slot_count, fsdp_size, local_experts, model_width)
    gate_pre = jnp.einsum("cnld,ldf->cnlf", grouped, gate_w, preferred_element_type=jnp.float32)
    up_pre = jnp.einsum("cnld,ldf->cnlf", grouped, up_w, preferred_element_type=jnp.float32)
    activated = (jax.nn.silu(gate_pre) * up_pre).astype(jnp.bfloat16)
    produced = jnp.einsum("cnlf,lfd->cnld", activated, down_w, preferred_element_type=jnp.float32)
    produced = produced.astype(jnp.bfloat16).reshape(slot_count, experts_all, model_width)
    returned = lax.all_to_all(produced, "fsdp", split_axis=1, concat_axis=1, tiled=True)
    returned, arrived, gate_pre, up_pre, activated = (
        returned,
        arrived,
        gate_pre,
        up_pre,
        activated,
    )
    assigned = returned.reshape(CAP * experts_all, model_width)[slot_index]
    assigned = assigned.reshape(tok_count, TOPK, model_width).astype(jnp.float32)
    moe_out = jnp.sum(gates[:, :, None] * assigned, axis=1)
    layer_out = (residual + moe_out).astype(jnp.bfloat16).reshape(1, tok_count, model_width)
    dense_back = (
        lax.all_gather(norm1_gain, ("seq", "fsdp"), axis=0, tiled=True),
        lax.all_gather(query_weight, ("seq", "fsdp"), axis=0, tiled=True),
        lax.all_gather(key_weight, ("seq", "fsdp"), axis=0, tiled=True),
        lax.all_gather(value_weight, ("seq", "fsdp"), axis=0, tiled=True),
        lax.all_gather(output_weight, ("seq", "fsdp"), axis=0, tiled=True),
        lax.all_gather(norm2_gain, ("seq", "fsdp"), axis=0, tiled=True),
        lax.all_gather(router_weight, ("seq", "fsdp"), axis=0, tiled=True),
    )
    experts_back = (
        lax.all_gather(expert_gate, "seq", axis=1, tiled=True),
        lax.all_gather(expert_up, "seq", axis=1, tiled=True),
        lax.all_gather(expert_down, "seq", axis=1, tiled=True),
    )
    gain_one, query_w, key_w, value_w, output_w, gain_two, router_w = dense_back
    gate_w, up_w, down_w = experts_back
    grad_out = cotangent.reshape(tok_count, model_width).astype(jnp.float32)
    grad_gates = jnp.sum(grad_out[:, None, :] * assigned, axis=-1)
    grad_rows = (
        (gates[:, :, None] * grad_out[:, None, :])
        .astype(jnp.bfloat16)
        .reshape(tok_count * TOPK, model_width)
    )
    grad_sent = (
        jnp.zeros((CAP * experts_all, model_width), jnp.bfloat16).at[slot_index].set(grad_rows)
    )
    grad_sent = grad_sent.reshape(CAP, experts_all, model_width)
    grad_arrived = lax.all_to_all(grad_sent, "fsdp", split_axis=1, concat_axis=1, tiled=True)
    grad_arrived = grad_arrived.reshape(CAP, fsdp_size, local_experts, model_width)
    grad_act = jnp.einsum(
        "cnld,lfd->cnlf", grad_arrived, down_w, preferred_element_type=jnp.float32
    )
    sigmoid_gate = jax.nn.sigmoid(gate_pre)
    grad_gate = (grad_act * up_pre * sigmoid_gate * (1.0 + gate_pre * (1.0 - sigmoid_gate))).astype(
        jnp.bfloat16
    )
    grad_up = (grad_act * gate_pre * sigmoid_gate).astype(jnp.bfloat16)
    rows_arrived = arrived.reshape(CAP, fsdp_size, local_experts, model_width)
    grad_down_w = jnp.einsum(
        "cnlf,cnld->lfd", activated, grad_arrived, preferred_element_type=jnp.float32
    )
    grad_gate_w = jnp.einsum(
        "cnld,cnlf->ldf", rows_arrived, grad_gate, preferred_element_type=jnp.float32
    )
    grad_up_w = jnp.einsum(
        "cnld,cnlf->ldf", rows_arrived, grad_up, preferred_element_type=jnp.float32
    )
    grad_back = jnp.einsum("cnlf,ldf->cnld", grad_gate, gate_w, preferred_element_type=jnp.float32)
    grad_back = grad_back + jnp.einsum(
        "cnlf,ldf->cnld", grad_up, up_w, preferred_element_type=jnp.float32
    )
    grad_back = grad_back.astype(jnp.bfloat16).reshape(CAP, experts_all, model_width)
    grad_returned = lax.all_to_all(grad_back, "fsdp", split_axis=1, concat_axis=1, tiled=True)
    grad_expert_gate, grad_expert_up, grad_expert_down = (
        lax.psum_scatter(
            grad_gate_w.astype(jnp.bfloat16), "seq", scatter_dimension=1, tiled=True
        ).astype(jnp.float32),
        lax.psum_scatter(
            grad_up_w.astype(jnp.bfloat16), "seq", scatter_dimension=1, tiled=True
        ).astype(jnp.float32),
        lax.psum_scatter(
            grad_down_w.astype(jnp.bfloat16), "seq", scatter_dimension=1, tiled=True
        ).astype(jnp.float32),
    )
    grad_hidden = grad_returned.reshape(CAP * experts_all, model_width)[slot_index]
    grad_hidden = jnp.sum(
        grad_hidden.reshape(tok_count, TOPK, model_width).astype(jnp.float32), axis=1
    )
    grad_chosen = gates * (grad_gates - jnp.sum(gates * grad_gates, axis=-1, keepdims=True))
    grad_logits = jnp.sum(grad_chosen[:, :, None] * picker, axis=1).astype(jnp.bfloat16)
    grad_router = jnp.einsum(
        "td,te->de", hidden_two, grad_logits, preferred_element_type=jnp.float32
    )
    grad_hidden = grad_hidden + jnp.einsum(
        "te,de->td", grad_logits, router_w, preferred_element_type=jnp.float32
    )
    grad_two_in, grad_gain_two = norm_backward(grad_hidden, normed_two, factor_two, gain_two)
    grad_residual = grad_out + grad_two_in
    grad_branch = grad_residual.astype(jnp.bfloat16)
    grad_output_w = jnp.einsum(
        "tq,td->qd", mixed_tok, grad_branch, preferred_element_type=jnp.float32
    )
    grad_mixed = jnp.einsum("td,qd->tq", grad_branch, output_w, preferred_element_type=jnp.float32)
    grad_mixed = grad_mixed.astype(jnp.bfloat16).reshape(tok_count, seq_size, -1)
    grad_heads = lax.all_to_all(grad_mixed, "seq", split_axis=1, concat_axis=0, tiled=True)
    grad_heads = grad_heads.reshape(block_count, row_block, kv_local, group_size, HEAD)

    def backward_block(carry, pieces):
        key_grad, value_grad = carry
        query_block, grad_block, log_block, row_start = pieces
        scores = block_scores(query_block, key_rows, row_start)
        attn_probs = jnp.exp(scores - log_block[..., None])
        grad_probs = jnp.einsum(
            "qjgd,kjd->jgqk", grad_block, value_rows, preferred_element_type=jnp.float32
        )
        row_dot = jnp.sum(attn_probs * grad_probs, axis=-1, keepdims=True)
        grad_scores = (attn_probs * (grad_probs - row_dot)).astype(jnp.bfloat16)
        query_grad = (
            jnp.einsum("jgqk,kjd->qjgd", grad_scores, key_rows, preferred_element_type=jnp.float32)
            * score_scale
        )
        key_grad = (
            key_grad
            + jnp.einsum(
                "jgqk,qjgd->kjd", grad_scores, query_block, preferred_element_type=jnp.float32
            )
            * score_scale
        )
        value_grad = value_grad + jnp.einsum(
            "jgqk,qjgd->kjd",
            attn_probs.astype(jnp.bfloat16),
            grad_block,
            preferred_element_type=jnp.float32,
        )
        return ((key_grad, value_grad), query_grad)

    zero_rows = jnp.zeros((length, kv_local, HEAD), jnp.float32)
    (key_grad, value_grad), query_grads = lax.scan(
        backward_block, (zero_rows, zero_rows), (query_blocks, grad_heads, log_totals, starts)
    )
    full_cos, full_sin = rope_angles(jnp.arange(length), HEAD)
    query_grad_pre = unrotate(
        query_grads.reshape(length, kv_local * group_size, HEAD), full_cos, full_sin
    )
    query_grad_pre = query_grad_pre.astype(jnp.bfloat16).reshape(length, 1, -1)
    key_grad_pre = (
        unrotate(key_grad, full_cos, full_sin).astype(jnp.bfloat16).reshape(length, 1, -1)
    )
    value_grad_low = value_grad.astype(jnp.bfloat16).reshape(length, 1, -1)
    grad_query_tok, grad_key_tok, grad_value_tok = (
        lax.all_to_all(query_grad_pre, "seq", split_axis=0, concat_axis=1, tiled=True),
        lax.all_to_all(key_grad_pre, "seq", split_axis=0, concat_axis=1, tiled=True),
        lax.all_to_all(value_grad_low, "seq", split_axis=0, concat_axis=1, tiled=True),
    )
    grad_query_tok = grad_query_tok.reshape(tok_count, -1)
    grad_key_tok = grad_key_tok.reshape(tok_count, -1)
    grad_value_tok = grad_value_tok.reshape(tok_count, -1)
    grad_query_w = jnp.einsum(
        "td,tq->dq", hidden_one, grad_query_tok, preferred_element_type=jnp.float32
    )
    grad_key_w = jnp.einsum(
        "td,tq->dq", hidden_one, grad_key_tok, preferred_element_type=jnp.float32
    )
    grad_value_w = jnp.einsum(
        "td,tq->dq", hidden_one, grad_value_tok, preferred_element_type=jnp.float32
    )
    grad_hidden_one = jnp.einsum(
        "tq,dq->td", grad_query_tok, query_w, preferred_element_type=jnp.float32
    )
    grad_hidden_one = grad_hidden_one + jnp.einsum(
        "tq,dq->td", grad_key_tok, key_w, preferred_element_type=jnp.float32
    )
    grad_hidden_one = grad_hidden_one + jnp.einsum(
        "tq,dq->td", grad_value_tok, value_w, preferred_element_type=jnp.float32
    )
    grad_one_in, grad_gain_one = norm_backward(grad_hidden_one, normed_one, factor_one, gain_one)
    grad_inputs = (grad_residual + grad_one_in).reshape(1, tok_count, model_width)
    dense_grads = (
        lax.psum_scatter(grad_gain_one, ("seq", "fsdp"), scatter_dimension=0, tiled=True),
        lax.psum_scatter(grad_query_w, ("seq", "fsdp"), scatter_dimension=0, tiled=True),
        lax.psum_scatter(grad_key_w, ("seq", "fsdp"), scatter_dimension=0, tiled=True),
        lax.psum_scatter(grad_value_w, ("seq", "fsdp"), scatter_dimension=0, tiled=True),
        lax.psum_scatter(grad_output_w, ("seq", "fsdp"), scatter_dimension=0, tiled=True),
        lax.psum_scatter(grad_gain_two, ("seq", "fsdp"), scatter_dimension=0, tiled=True),
        lax.psum_scatter(grad_router, ("seq", "fsdp"), scatter_dimension=0, tiled=True),
    )
    return (
        layer_out,
        grad_inputs,
        dense_grads[0],
        dense_grads[1],
        dense_grads[2],
        dense_grads[3],
        dense_grads[4],
        dense_grads[5],
        dense_grads[6],
        grad_expert_gate,
        grad_expert_up,
        grad_expert_down,
    )


def solution(mesh):
    in_specs = (
        P("fsdp", "seq", None),
        P(("seq", "fsdp")),
        P(("seq", "fsdp"), None),
        P(("seq", "fsdp"), None),
        P(("seq", "fsdp"), None),
        P(("seq", "fsdp"), None),
        P(("seq", "fsdp")),
        P(("seq", "fsdp"), None),
        P("fsdp", "seq", None),
        P("fsdp", "seq", None),
        P("fsdp", "seq", None),
        P("fsdp", "seq", None),
        P("fsdp", "seq", None),
    )
    out_specs = (
        P("fsdp", "seq", None),
        P("fsdp", "seq", None),
        P(("seq", "fsdp")),
        P(("seq", "fsdp"), None),
        P(("seq", "fsdp"), None),
        P(("seq", "fsdp"), None),
        P(("seq", "fsdp"), None),
        P(("seq", "fsdp")),
        P(("seq", "fsdp"), None),
        P("fsdp", "seq", None),
        P("fsdp", "seq", None),
        P("fsdp", "seq", None),
    )
    return jax.shard_map(
        on_device, mesh=mesh, in_specs=in_specs, out_specs=out_specs, check_vma=False
    )
```

profile of v0, /device:TPU:1, one launch (start us, length us, event | category | flops | bytes accessed | tf_op | source)
XLA Modules:
  0.0 4910.7 jit_solution(14749295802598208069)
XLA Ops:
  15.0 68.7 %all-reduce.6 = (bf16[1024]{0:T(1024)(128)(2,1)S(1)}, bf16[1024]{0:T(1024)(128)(2,1)S(1)}) all-reduce(bf16[1024]{0:T(1024)(128)(2,1)S(1)} %dynamic-update-slice, bf16[1024]{0:T(1024)(128)(2,1)S(1)} %dynamic-update-slice.1), channel_id=1, replica_groups=mesh['seq'=4,'fsdp'=32] {'seq','fsdp'}, use_global_device_ids=true, to_apply=%add | all-reduce | flops 2048 | bytes 8192
  93.9 214.3 %all-gather.12.cloned.1.call-done = bf16[1024,512]{1,0:T(8,128)(2,1)} async-done(((bf16[8,512]{1,0:T(8,128)(2,1)}), bf16[1024,512]{1,0:T(8,128)(2,1)}) %all-gather.12.cloned.1.call-update) | async-done | bytes 1048592 | tf_op jit(solution)/shard_map/all_gather | solution.py:109
  314.3 287.7 %all-gather.10.cloned.1.call-done = bf16[1024,512]{1,0:T(8,128)(2,1)} async-done(((bf16[8,512]{1,0:T(8,128)(2,1)}), bf16[1024,512]{1,0:T(8,128)(2,1)}) %all-gather.10.cloned.1.call-update) | async-done | bytes 1048592 | tf_op jit(solution)/shard_map/all_gather | solution.py:108
  604.9 300.9 %all-gather.8.cloned.1.call-done = bf16[1024,1024]{1,0:T(8,128)(2,1)} async-done(((bf16[8,1024]{1,0:T(8,128)(2,1)}), bf16[1024,1024]{1,0:T(8,128)(2,1)}) %all-gather.8.cloned.1.call-update) | async-done | bytes 2097168 | tf_op jit(solution)/shard_map/all_gather | solution.py:107
  933.0 17.3 while.27
  974.5 14.6 scatter_custom_fusion.1
  990.2 213.9 %all-gather.14.cloned.1.call-done = bf16[1024,1024]{1,0:T(8,128)(2,1)} async-done(((bf16[8,1024]{1,0:T(8,128)(2,1)}), bf16[1024,1024]{1,0:T(8,128)(2,1)}) %all-gather.14.cloned.1.call-update) | async-done | bytes 2097168 | tf_op jit(solution)/shard_map/all_gather | solution.py:110
  1215.6 10.7 copy_multiply_fusion
  1226.3 10.6 all-to-all-start.4
  1236.9 387.2 %all_gather.46 = bf16[1024,32]{1,0:T(8,128)(2,1)S(1)} all-gather(bf16[8,32]{1,0:T(8,128)(2,1)S(1)} %copy-done.36), channel_id=1, replica_groups=mesh['seq'=4,'fsdp'=32] {'seq','fsdp'}, dimensions={0}, use_global_device_ids=true | all-gather | bytes 66048 | tf_op jit(solution)/shard_map/all_gather | solution.py:112
  1626.0 13.7 scatter_custom_fusion.2
  1654.1 71.5 %all-gather.18.cloned.1.call-done = bf16[1,1024,512]{2,1,0:T(8,128)(2,1)} async-done(((bf16[1,256,512]{2,1,0:T(8,128)(2,1)}), bf16[1,1024,512]{2,1,0:T(8,128)(2,1)}) %all-gather.18.cloned.1.call-update) | async-done | bytes 1048592 | tf_op jit(solution)/shard_map/all_gather | solution.py:116
  1725.6 9.5 fusion.68
  1735.2 18.2 all-gather.20.cloned.1.call-done
  1753.4 9.8 fusion.66
  1763.2 13.2 all-gather.16.cloned.1.call-done
  1776.3 12.4 fusion.83
  1820.4 64.6 %all-to-all-done.5 = bf16[80,32,1024]{2,0,1:T(8,128)(2,1)} async-done(((bf16[80,32,1024]{2,0,1:T(8,128)(2,1)}), bf16[80,32,1024]{2,0,1:T(8,128)(2,1)}, u32[]{:S(2)}, u32[]{:S(2)}) %all-to-all-start.5) | async-done | bytes 5242912 | tf_op jit(solution)/shard_map/all_to_all | solution.py:198
  1885.0 12.0 all-to-all-start.7
  1922.5 14.7 gather_fusion.1
  1946.4 21.1 all-to-all-done.7
  1975.2 14.3 gather_fusion.2
  2018.4 51.3 %while.28 = (s32[]{:T(128)}, f32[1024,2,64]{0,2,1:T(8,128)S(1)}, f32[1024,2,64]{0,2,1:T(8,128)}, f32[2,512,2,2,64]{1,0,4,3,2:T(2,128)}, bf16[2,512,2,2,64]{1,4,3...) while((s32[]{:T(128)}, f32[1024,2,64]{0,2,1:T(8,128)S(1)}, ...), condition=%wide.region_23.24_spmd.clone, body=%wide.region_21.23_spmd.clone.sunk | while | flops 1374943744 | bytes 71626920 | solution.py:327
  2033.2 10.4 dynamic_update_slice.20
  2059.3 10.4 dynamic_update_slice.20
  2103.1 11.9 all_to_all.141
  2126.1 104.7 %all-reduce.9.cloned.1.call-done = f32[1024,32]{1,0:T(8,128)} async-done(((f32[1024,32]{1,0:T(8,128)}), f32[1024,32]{1,0:T(8,128)}) %all-reduce.9.cloned.1.call-update) | async-done | bytes 131088
  2236.7 65.5 %all-reduce.5 = (f32[1024]{0:T(1024)S(1)}, f32[1024]{0:T(1024)S(1)}) all-reduce(f32[1024]{0:T(1024)S(1)} %get-tuple-element.265, f32[1024]{0:T(1024)S(1)} %get-tuple-element.263), channel_id=2, replica_groups=mesh['seq'=4,'fsdp'=32] {'seq','fsdp'}, use_global_device_ids=true, to_apply=%region_26.27.clone | all-reduce | flops 2048 | bytes 16384
  2304.6 454.9 %reduce-scatter.12.cloned.1.call-done = f32[8,512]{1,0:T(8,128)} async-done(((f32[1024,512]{1,0:T(8,128)}), f32[8,512]{1,0:T(8,128)}) %reduce-scatter.12.cloned.1.call-update) | async-done | bytes 16400 | tf_op jit(solution)/shard_map/reduce_scatter | solution.py:371
  2759.5 711.7 %reduce-scatter.10.cloned.1.call-done = f32[8,512]{1,0:T(8,128)} async-done(((f32[1024,512]{1,0:T(8,128)}), f32[8,512]{1,0:T(8,128)}) %reduce-scatter.10.cloned.1.call-update) | async-done | bytes 16400 | tf_op jit(solution)/shard_map/reduce_scatter | solution.py:370
  3471.2 716.8 %reduce-scatter.14.cloned.1.call-done = f32[8,1024]{1,0:T(8,128)} async-done(((f32[1024,1024]{1,0:T(8,128)}), f32[8,1024]{1,0:T(8,128)}) %reduce-scatter.14.cloned.1.call-update) | async-done | bytes 32784 | tf_op jit(solution)/shard_map/reduce_scatter | solution.py:372
  4188.0 715.2 %reduce-scatter.8.cloned.1.call-done = f32[8,1024]{1,0:T(8,128)} async-done(((f32[1024,1024]{1,0:T(8,128)}), f32[8,1024]{1,0:T(8,128)}) %reduce-scatter.8.cloned.1.call-update) | async-done | bytes 32784 | tf_op jit(solution)/shard_map/reduce_scatter | solution.py:369
  (318 shorter events, 308.1 us)
Async XLA Ops:
  8.0 595.5 %copy-start.4 = (bf16[1,256,1024]{2,1,0:T(8,128)(2,1)S(1)}, bf16[1,256,1024]{2,1,0:T(8,128)(2,1)}, u32[]{:S(2)}) copy-start(bf16[1,256,1024]{2,1,0:T(8,128)(2,1)} %param.17) | copy-start | bytes 1572868
  8.0 300.2 %all-gather.12.cloned.1.call-start = ((), (), s32[]{:S(2)}) async-start(), calls=%async_computation.21 | async-start | bytes 1056768 | tf_op jit(solution)/shard_map/all_gather | solution.py:109
  8.8 593.2 %all-gather.10.cloned.1.call-start = ((), (), s32[]{:S(2)}) async-start(), calls=%async_computation.20 | async-start | bytes 1056768 | tf_op jit(solution)/shard_map/all_gather | solution.py:108
  9.5 896.3 %all-gather.8.cloned.1.call-start = ((), (), s32[]{:S(2)}) async-start(), calls=%async_computation.19 | async-start | bytes 2113536 | tf_op jit(solution)/shard_map/all_gather | solution.py:107
  10.2 1193.9 %all-gather.14.cloned.1.call-start = ((), (), s32[]{:S(2)}) async-start(), calls=%async_computation.22 | async-start | bytes 2113536 | tf_op jit(solution)/shard_map/all_gather | solution.py:110
  10.8 591.2 %copy-start.37 = (f32[32]{0:T(128)}, f32[32]{0:T(128)S(1)}, u32[]{:S(2)}) copy-start(f32[32]{0:T(128)S(1)} %multiply_power_fusion) | copy-start | bytes 388
  13.3 895.3 %copy-start.29 = (f32[256]{0:T(256)}, f32[256]{0:T(256)S(1)}, u32[]{:S(2)}) copy-start(f32[256]{0:T(256)S(1)} %add_rsqrt_fusion.1) | copy-start | bytes 3076
  83.8 824.9 %copy-start.22 = (f32[1024]{0:T(1024)}, f32[1024]{0:T(1024)S(1)}, u32[]{:S(2)}) copy-start(f32[1024]{0:T(1024)S(1)} %convert_element_type.242) | copy-start | bytes 12292
  310.9 599.6 %all-to-all-start.2 = ((bf16[256,4,128]{2,0,1:T(8,128)(2,1)}), bf16[256,4,128]{2,0,1:T(8,128)(2,1)S(1)}, u32[]{:S(2)}, u32[]{:S(2)}) async-start(bf16[256,4,128]{2,0,1:T(8,128)(2,1)} %bitcast.405), calls=%async_computation.2 | async-start | bytes 524288 | tf_op jit(solution)/shard_map/all_to_all | solution.py:148
  910.5 9.3 all-to-all-start.1
  919.8 12.5 all-to-all-start
  924.3 701.7 %copy-start.31 = (s32[2048,1]{0,1:T(1,128)}, s32[2048,1]{0,1:T(1,128)S(1)}, u32[]{:S(2)}) copy-start(s32[2048,1]{0,1:T(1,128)S(1)} %compare_select_fusion) | copy-start | bytes 24580
  961.9 27.4 all-to-all-start.3
  1206.7 417.5 %copy-start = (bf16[256,1024]{1,0:T(8,128)(2,1)}, bf16[256,1024]{1,0:T(8,128)(2,1)S(1)}, u32[]{:S(2)}) copy-start(bf16[256,1024]{1,0:T(8,128)(2,1)S(1)} %multiply_convert_fusion) | copy-start | bytes 1572868
  1226.3 398.3 %copy-start.26 = (s32[1,256,8]{1,2,0:T(8,128)S(1)}, s32[1,256,8]{1,2,0:T(8,128)}, u32[]{:S(2)}) copy-start(s32[1,256,8]{1,2,0:T(8,128)} %param.28) | copy-start | bytes 24580
  1226.3 421.2 %all-to-all-start.4 = ((bf16[80,32,1024]{2,0,1:T(8,128)(2,1)}), bf16[80,32,1024]{2,0,1:T(8,128)(2,1)}, u32[]{:S(2)}, u32[]{:S(2)}) async-start(bf16[80,32,1024]{2,0,1:T(8,128)(2,1)} %copy_multiply_fusion), calls=%async_computation.4 | async-start | bytes 10485760 | tf_op jit(solution)/shard_map/all_to_all | solution.py:190
  1647.5 105.9 %all-to-all-start.6 = ((bf16[80,32,1024]{2,0,1:T(8,128)(2,1)}), bf16[80,32,1024]{2,0,1:T(8,128)(2,1)}, u32[]{:S(2)}, u32[]{:S(2)}) async-start(bf16[80,32,1024]{2,0,1:T(8,128)(2,1)} %copy.261), calls=%async_computation.6 | async-start | bytes 10485760 | tf_op jit(solution)/shard_map/all_to_all | solution.py:237
  1652.4 73.3 %all-gather.18.cloned.1.call-start = ((), (), s32[]{:S(2)}) async-start(), calls=%async_computation.24 | async-start | bytes 1310720 | tf_op jit(solution)/shard_map/all_gather | solution.py:116
  1653.0 100.4 %all-gather.20.cloned.1.call-start = ((), (), s32[]{:S(2)}) async-start(), calls=%async_computation.25 | async-start | bytes 1310720 | tf_op jit(solution)/shard_map/all_gather | solution.py:117
  1653.5 122.8 %all-gather.16.cloned.1.call-start = ((), (), s32[]{:S(2)}) async-start(), calls=%async_computation.23 | async-start | bytes 1310720 | tf_op jit(solution)/shard_map/all_gather | solution.py:115
  1797.2 87.9 %all-to-all-start.5 = ((bf16[80,32,1024]{2,0,1:T(8,128)(2,1)}), bf16[80,32,1024]{2,0,1:T(8,128)(2,1)}, u32[]{:S(2)}, u32[]{:S(2)}) async-start(bf16[80,32,1024]{2,0,1:T(8,128)(2,1)} %copy.258), calls=%async_computation.5 | async-start | bytes 10485760 | tf_op jit(solution)/shard_map/all_to_all | solution.py:198
  1885.0 82.4 %all-to-all-start.7 = ((bf16[80,32,1024]{2,0,1:T(8,128)(2,1)}), bf16[80,32,1024]{2,0,1:T(8,128)(2,1)}, u32[]{:S(2)}, u32[]{:S(2)}) async-start(bf16[80,32,1024]{2,0,1:T(8,128)(2,1)} %copy.263), calls=%async_computation.7 | async-start | bytes 10485760 | tf_op jit(solution)/shard_map/all_to_all | solution.py:262
  1897.1 223.5 %reduce-scatter.20.cloned.1.call-start = ((), (), s32[]{:S(2)}) async-start(), calls=%async_computation.32 | async-start | bytes 1310720 | tf_op jit(solution)/shard_map/reduce_scatter | solution.py:270
  1904.9 217.5 %reduce-scatter.18.cloned.1.call-start = ((), (), s32[]{:S(2)}) async-start(), calls=%async_computation.31 | async-start | bytes 1310720 | tf_op jit(solution)/shard_map/reduce_scatter | solution.py:267
  1999.7 17.8 all-to-all-start.8
  2008.8 115.5 %reduce-scatter.16.cloned.1.call-start = ((), (), s32[]{:S(2)}) async-start(), calls=%async_computation.30 | async-start | bytes 1310720 | tf_op jit(solution)/shard_map/reduce_scatter | solution.py:264
  2072.6 8.6 all-to-all-start.11
  2076.1 154.7 %all-reduce.9.cloned.1.call-start = ((), (), s32[]{:S(2)}) async-start(), calls=%async_computation.33 | async-start | bytes 1048576
  2077.2 682.3 %reduce-scatter.12.cloned.1.call-start = ((), (), s32[]{:S(2)}) async-start(), calls=%async_computation.28 | async-start | bytes 2113536 | tf_op jit(solution)/shard_map/reduce_scatter | solution.py:371
  2083.7 1387.5 %reduce-scatter.10.cloned.1.call-start = ((), (), s32[]{:S(2)}) async-start(), calls=%async_computation.27 | async-start | bytes 2113536 | tf_op jit(solution)/shard_map/reduce_scatter | solution.py:370
  2096.6 2091.4 %reduce-scatter.14.cloned.1.call-start = ((), (), s32[]{:S(2)}) async-start(), calls=%async_computation.29 | async-start | bytes 4227072 | tf_op jit(solution)/shard_map/reduce_scatter | solution.py:372
  2099.4 2803.8 %reduce-scatter.8.cloned.1.call-start = ((), (), s32[]{:S(2)}) async-start(), calls=%async_computation.26 | async-start | bytes 4227072 | tf_op jit(solution)/shard_map/reduce_scatter | solution.py:369
  (38 other events, 1457.4 us)
Sparse Core Ops, SparseCore 0:
  10.5 297.6 all-gather.11
  309.9 292.0 all-gather.9
  603.7 302.0 all-gather.7
  907.3 296.7 all-gather.13
  2082.1 148.6 all-reduce.8
Sparse Core Ops, SparseCore 1:
  1654.5 71.1 all-gather.17
  1727.2 26.2 all-gather.19
  1754.9 21.4 all-gather.15
  1905.0 61.4 reduce-scatter.19
  1969.0 26.3 reduce-scatter.17
  2017.5 23.3 reduce-scatter.15
  2083.7 675.7 reduce-scatter.11
  2762.3 708.8 reduce-scatter.9
  3474.1 713.8 reduce-scatter.13
  4190.9 712.2 reduce-scatter.7
where the time goes:
time: 4960 us; the launch traced here: 4910 us
  waiting for transfers between devices  3930 us (79%)
  blocking collectives  542 us (11%)
  local copies, waits for them, and re-layouts  152 us (3%)
  matrix products  122 us (2%)
  other arithmetic  83.3 us (2%)
  starting transfers between devices  66.8 us (1%)
    reduce_scatter x1, waiting for transfers between devices, on_device(): lax.psum_scatter(grad_output_w, ('seq', 'fsdp'), scatter_dimension=0, til...  717 us
    reduce_scatter x1, waiting for transfers between devices, on_device(): lax.psum_scatter(grad_query_w, ('seq', 'fsdp'), scatter_dimension=0, tile...  715 us
    reduce_scatter x1, waiting for transfers between devices, on_device(): lax.psum_scatter(grad_key_w, ('seq', 'fsdp'), scatter_dimension=0, tiled=...  712 us
    reduce_scatter x1, waiting for transfers between devices, on_device(): lax.psum_scatter(grad_value_w, ('seq', 'fsdp'), scatter_dimension=0, tile...  455 us
    all_gather x1, blocking collectives, on_device(): lax.all_gather(router_weight, ('seq', 'fsdp'), axis=0, tiled=True)  387 us
    all_gather x1, waiting for transfers between devices, on_device(): lax.all_gather(query_weight, ('seq', 'fsdp'), axis=0, tiled=True)  301 us
    all_gather x1, waiting for transfers between devices, on_device(): lax.all_gather(key_weight, ('seq', 'fsdp'), axis=0, tiled=True)  288 us
    all_gather x1, waiting for transfers between devices, on_device(): lax.all_gather(value_weight, ('seq', 'fsdp'), axis=0, tiled=True)  214 us
  transfers between devices with their start and end apart: 25, of which 17 were waited for; matrix products, arithmetic and copies ran while one was open for 6% of the time, Pallas kernels for 0%

commit v1 on v0

v1 whole, which is shorter than its diff:
```python
import functools

import jax
import jax.numpy as jnp
from jax import lax
from jax.experimental import pallas as pl
from jax.experimental.pallas import tpu as pltpu
from jax.sharding import Mesh
from jax.sharding import PartitionSpec as P

HEADS = 16
KV_HEADS = 8
HEAD = 64
TOPK = 8
CAP = 80
TOK = 256
D = 1024
FF = 512
EXPERTS = 32
SHARE = 8
SLOTS = SHARE * CAP
BLOCKS = 8
HALF = FF // 2
GROUP = 4
LENGTH = 1024

epsilon = 1e-06
rope_base = 10000.0

AXES = ("ylo", "core", "yhi", "x", "z")
SEQ = ("ylo", "core")
FSDP = ("yhi", "x", "z")
PLANE = ("x", "yhi", "ylo")

f32 = jnp.float32
bf16 = jnp.bfloat16

NT = (((1,), (1,)), ((), ()))
TN = (((0,), (0,)), ((), ()))
VMEM_LIMIT = 56 * 1024 * 1024


def dot(a, b, dims=(((1,), (0,)), ((), ()))):
    return lax.dot_general(a, b, dims, preferred_element_type=f32)


def iota(shape, axis):
    return lax.broadcasted_iota(jnp.int32, shape, axis)


def as_bf16(cond):
    return jnp.where(cond, 1.0, 0.0).astype(bf16)


def head_lanes_rope(head):
    lane = iota((1, 256), 1) % 128
    return (lane >= 32 * head) & (lane < 32 * head + 32)


def head_lanes(head):
    lane = iota((1, 256), 1)
    return (lane >= 64 * head) & (lane < 64 * head + 64)


def spread_keys():
    row, col = iota((128, 256), 0), iota((128, 256), 1)
    source = (col // 128) * 64 + ((col % 128) // 64) * 32 + col % 32
    return row == source, (col % 64) < 32


def spread_values():
    row, col = iota((128, 256), 0), iota((128, 256), 1)
    return row == (col // 128) * 64 + col % 64, (col % 128) < 64


def front_kernel(x_ref, w_ref, gain_ref, cos_ref, sin_ref, q_ref, k_ref, v_ref, o_ref, lse_ref, h_ref):
    wq = w_ref[:, :256]
    wk = dot(w_ref[:, 256:384], as_bf16(spread_keys()[0])).astype(bf16)
    wv = dot(w_ref[:, 384:512], as_bf16(spread_values()[0])).astype(bf16)
    for i in range(4):
        rows = slice(256 * i, 256 * i + 256)
        x = x_ref[rows].astype(f32)
        r = lax.rsqrt(jnp.mean(x * x, axis=-1, keepdims=True) + epsilon)
        h = (x * r * gain_ref[...]).astype(bf16)
        h_ref[rows] = h
        c, s = cos_ref[rows], sin_ref[rows]
        for w, out in ((wq, q_ref), (wk, k_ref)):
            pre = dot(h, w)
            a, b = pre[:, :128], pre[:, 128:]
            out[rows] = jnp.concatenate([a * c - b * s, b * c + a * s], axis=1).astype(bf16)
        v_ref[rows] = dot(h, wv).astype(bf16)
    for i in range(4):
        rows = slice(256 * i, 256 * i + 256)
        n = 256 * (i + 1)
        seen = iota((256, n), 1) <= iota((256, n), 0) + 256 * i
        mixed = jnp.zeros((256, 256), f32)
        logs = jnp.zeros((256, 128), f32)
        for head in range(GROUP):
            q = q_ref[rows] * as_bf16(head_lanes_rope(head))
            scores = jnp.where(seen, dot(q, k_ref[:n], NT) * HEAD**-0.5, -1e30)
            peak = jnp.max(scores, axis=-1, keepdims=True)
            e = jnp.exp(scores - peak)
            total = jnp.sum(e, axis=-1, keepdims=True)
            probs = (e * (1.0 / total)).astype(bf16)
            mixed = mixed + dot(probs, v_ref[:n] * as_bf16(head_lanes(head)))
            logs = jnp.where(iota((256, 128), 1) == head, peak + jnp.log(total), logs)
        o_ref[rows] = mixed.astype(bf16)
        lse_ref[rows] = logs


def front(x_all, w, gain, cos, sin):
    shape = jax.ShapeDtypeStruct
    return pl.pallas_call(
        front_kernel,
        out_shape=(
            shape((LENGTH, 256), bf16),
            shape((LENGTH, 256), bf16),
            shape((LENGTH, 256), bf16),
            shape((LENGTH, 256), bf16),
            shape((LENGTH, 128), f32),
            shape((LENGTH, D), bf16),
        ),
        compiler_params=pltpu.CompilerParams(vmem_limit_bytes=VMEM_LIMIT),
        cost_estimate=pl.CostEstimate(flops=8_000_000_000, bytes_accessed=10_000_000, transcendentals=4_000_000),
        name="front",
    )(x_all, w, gain, cos, sin)


def back_kernel(q_ref, k_ref, v_ref, do_ref, lse_ref, cos_ref, sin_ref, out_ref, dk_ref, dv_ref):
    dk_ref[...] = jnp.zeros_like(dk_ref)
    dv_ref[...] = jnp.zeros_like(dv_ref)
    scale = HEAD**-0.5
    for i in range(4):
        rows = slice(256 * i, 256 * i + 256)
        n = 256 * (i + 1)
        seen = iota((256, n), 1) <= iota((256, n), 0) + 256 * i
        dq = jnp.zeros((256, 256), f32)
        for head in range(GROUP):
            lanes = head_lanes_rope(head)
            q = q_ref[rows] * as_bf16(lanes)
            do = do_ref[rows] * as_bf16(head_lanes(head))
            scores = dot(q, k_ref[:n], NT) * scale - lse_ref[rows, head : head + 1]
            probs = jnp.where(seen, jnp.exp(jnp.where(seen, scores, 0.0)), 0.0)
            dprobs = dot(do, v_ref[:n], NT)
            row_dot = jnp.sum(probs * dprobs, axis=-1, keepdims=True)
            ds = (probs * (dprobs - row_dot)).astype(bf16)
            dq = dq + jnp.where(lanes, dot(ds, k_ref[:n]), 0.0)
            dk_ref[:n] += dot(ds, q, TN)
            dv_ref[:n] += dot(probs.astype(bf16), do, TN)
        c, s = cos_ref[rows], sin_ref[rows]
        a, b = dq[:, :128] * scale, dq[:, 128:] * scale
        out_ref[rows, :256] = jnp.concatenate([a * c + b * s, b * c - a * s], axis=1).astype(bf16)
    keep_keys, first_key = spread_keys()
    keep_values, first_value = spread_values()
    pick_keys = as_bf16(keep_keys & first_key)
    pick_values = as_bf16(keep_values & first_value)
    for i in range(4):
        rows = slice(256 * i, 256 * i + 256)
        c, s = cos_ref[rows], sin_ref[rows]
        a, b = dk_ref[rows, :128] * scale, dk_ref[rows, 128:] * scale
        a, b = a * c + b * s, b * c - a * s
        a, b = a + pltpu.roll(a, 96, 1), b + pltpu.roll(b, 96, 1)
        out_ref[rows, 256:384] = dot(jnp.concatenate([a, b], axis=1).astype(bf16), pick_keys, NT).astype(bf16)
        a, b = dv_ref[rows, :128], dv_ref[rows, 128:]
        a, b = a + pltpu.roll(a, 64, 1), b + pltpu.roll(b, 64, 1)
        out_ref[rows, 384:512] = dot(jnp.concatenate([a, b], axis=1).astype(bf16), pick_values, NT).astype(bf16)


def back(q, k, v, do, lse, cos, sin):
    return pl.pallas_call(
        back_kernel,
        out_shape=jax.ShapeDtypeStruct((LENGTH, 512), bf16),
        scratch_shapes=[pltpu.VMEM((LENGTH, 256), f32), pltpu.VMEM((LENGTH, 256), f32)],
        compiler_params=pltpu.CompilerParams(vmem_limit_bytes=VMEM_LIMIT),
        cost_estimate=pl.CostEstimate(flops=14_000_000_000, bytes_accessed=6_000_000, transcendentals=4_000_000),
        name="back",
    )(q, k, v, do, lse, cos, sin)


def slot_rows(codes, z):
    row = iota((SLOTS, EXPERTS), 0)
    start = (iota((SLOTS, EXPERTS), 1) - SHARE * z) * CAP
    own = (row >= start) & (row < start + CAP)
    place = jnp.sum(jnp.where(own, row - start, 0), axis=1, keepdims=True).astype(f32)
    spread = dot(as_bf16(own), codes, NT)
    return as_bf16(spread == place), own


def slot_columns(codes, z):
    column = iota((EXPERTS, SLOTS), 1)
    start = (iota((EXPERTS, SLOTS), 0) - SHARE * z) * CAP
    own = (column >= start) & (column < start + CAP)
    place = jnp.sum(jnp.where(own, column - start, 0), axis=0, keepdims=True).astype(f32)
    return as_bf16(dot(codes, as_bf16(own)) == place)


def gate_table(logits, codes):
    routed = codes >= 0
    logits = jnp.where(routed, logits, -1e30)
    e = jnp.where(routed, jnp.exp(logits - jnp.max(logits, axis=-1, keepdims=True)), 0.0)
    return e / jnp.sum(e, axis=-1, keepdims=True)


def split(values):
    high = values.astype(bf16)
    return high, (values - high.astype(f32)).astype(bf16)


SCALAR = pl.BlockSpec(memory_space=pltpu.SMEM)
ANYWHERE = pl.BlockSpec(memory_space=pl.ANY)
PAIR = 2 * CAP


def whole(*shape):
    return pl.BlockSpec(shape, lambda e: (0,) * len(shape))


def per_expert(*shape):
    return pl.BlockSpec((1,) + shape, lambda e: (e,) + (0,) * len(shape))


def call(kernel, name, flops, moved, **kwargs):
    return pl.pallas_call(
        kernel,
        compiler_params=pltpu.CompilerParams(vmem_limit_bytes=VMEM_LIMIT),
        cost_estimate=pl.CostEstimate(flops=flops, bytes_accessed=moved, transcendentals=0),
        name=name,
        **kwargs,
    )


def rows_kernel(with_gates, z_ref, *refs):
    z = z_ref[0]
    if with_gates:
        values_refs, codes_refs, router_ref = refs[:2], refs[2:4], refs[4]
        rows_ref, gates_ref = refs[-2:]
    else:
        values_refs, codes_refs, rows_ref = refs[:2], refs[:2], refs[-1]
    for b in range(2):
        codes = codes_refs[b][:, -128:][:, :EXPERTS]
        values = values_refs[b][:, :D]
        place, own = slot_rows(codes, z)
        rows = dot(place, values).astype(bf16)
        for j in range(SHARE):
            rows_ref[j, 0, b * CAP : (b + 1) * CAP] = rows[j * CAP : (j + 1) * CAP]
        if with_gates:
            high, low = split(gate_table(dot(values, router_ref[...]), codes.astype(f32)))
            both = dot(place, high) + dot(place, low)
            gate = jnp.sum(jnp.where(own, both, 0.0), axis=1, keepdims=True)
            for j in range(SHARE):
                gates_ref[j, 0, b * CAP : (b + 1) * CAP] = gate[j * CAP : (j + 1) * CAP]


def rows_of(z, index, pair, codes, router, kept):
    with_gates = router is not None
    full = pl.BlockSpec((TOK, pair[0].shape[1]), lambda e: (0, 0))
    last = pl.BlockSpec((TOK, 128), lambda e: (0, D // 128))
    args, specs = [z, *pair], [SCALAR, full, full]
    if with_gates:
        args += [*codes, router]
        specs += [last, last, pl.BlockSpec((D, EXPERTS), lambda e: (0, 0))]
    widths = [(D, bf16)] + ([(1, f32)] if with_gates else [])
    out_specs = [pl.BlockSpec((SHARE, 1, PAIR, w), lambda e: (0, index, 0, 0)) for w, _ in widths]
    out_shape = [jax.ShapeDtypeStruct((SHARE, 4, PAIR, w), t) for w, t in widths]
    aliases = {}
    if kept is not None:
        aliases = {len(args) + i: i for i in range(len(kept))}
        args += kept
        specs += [ANYWHERE] * len(kept)
    return call(
        functools.partial(rows_kernel, with_gates), "rows", 1_500_000_000, 4_000_000,
        grid=(1,), in_specs=specs, out_specs=out_specs, out_shape=out_shape, input_output_aliases=aliases,
    )(*args)


def down_of(parts):
    return jnp.concatenate(
        [
            jnp.concatenate([parts[0, 128 * j : 128 * j + 128], parts[1, 128 * j : 128 * j + 128]], axis=0)
            for j in range(4)
        ],
        axis=1,
    )


def main_kernel(z_ref, x_ref, gy_ref, gate_ref, w_ref, *refs):
    codes_refs = refs[:8]
    act_ref, dg_ref, du_ref, own_ref, other_ref, kept, dgates, codes_kept = refs[8:]
    e = pl.program_id(0)
    z = z_ref[0]
    x = x_ref[0].reshape(SLOTS, D)
    gate_w = w_ref[:, :512].reshape(D, HALF)
    up_w = w_ref[:, 512:1024].reshape(D, HALF)
    da = dot(gy_ref[0].reshape(SLOTS, D), down_of(w_ref[:, 1024:]), NT)
    g = dot(x, gate_w)
    u = dot(x, up_w)
    gate = gate_ref[0].reshape(SLOTS, 1)
    s = jax.nn.sigmoid(g)
    silu = g * s
    act = silu * u
    dgates[e] = jnp.sum(act * da, axis=1, keepdims=True).reshape(BLOCKS, CAP, 1)
    act_ref[0] = (act * gate).astype(bf16)
    da = da * gate
    dg = (da * u * (s + silu * (1.0 - s))).astype(bf16)
    du = (da * silu).astype(bf16)
    dg_ref[0] = dg
    du_ref[0] = du
    back = dot(dg, gate_w, NT) + dot(du, up_w, NT)
    kept[e] = back.astype(bf16).reshape(BLOCKS, CAP, D)

    @pl.when(e == 0)
    def _():
        for b in range(BLOCKS):
            codes_kept[b] = codes_refs[b][...]

    @pl.when(e == SHARE - 1)
    def _():
        def pair(j, carry):
            for c, out in ((0, own_ref), (1, other_ref)):
                b = 2 * j + c
                codes = codes_kept[b][:, :EXPERTS]
                place = slot_columns(codes, z)
                rows = jnp.concatenate([kept[i, b] for i in range(SHARE)], axis=0)
                out[j, :, :D] = dot(place, rows).astype(bf16)
                _, own = slot_rows(codes, z)
                dgate = jnp.concatenate([dgates[i, b] for i in range(SHARE)], axis=0)
                high, low = split(jnp.where(own, dgate, 0.0))
                scattered = dot(place, high) + dot(place, low)
                out[j, :, D:] = jnp.concatenate([scattered, jnp.zeros((TOK, 128 - EXPERTS), f32)], axis=1).astype(bf16)
            return carry

        lax.fori_loop(0, 4, pair, 0)


def codes_specs():
    return [pl.BlockSpec((TOK, 128), lambda e: (0, D // 128))] * BLOCKS


def main(z, x, gy, gates, weights, codes):
    shape = jax.ShapeDtypeStruct
    hidden = shape((SHARE, SLOTS, HALF), bf16)
    back = shape((4, TOK, D + 128), bf16)
    return call(
        main_kernel, "experts", 17_000_000_000, 45_000_000,
        grid=(SHARE,),
        in_specs=[
            SCALAR, per_expert(4, PAIR, D), per_expert(4, PAIR, D), per_expert(4, PAIR, 1),
            pl.BlockSpec((2, 1536, 256), lambda e: (e, 0, 0)), *codes_specs(),
        ],
        out_specs=[per_expert(SLOTS, HALF)] * 3 + [whole(4, TOK, D + 128)] * 2,
        out_shape=[hidden, hidden, hidden, back, back],
        scratch_shapes=[
            pltpu.VMEM((SHARE, BLOCKS, CAP, D), bf16),
            pltpu.VMEM((SHARE, BLOCKS, CAP, 1), f32),
            pltpu.VMEM((BLOCKS, TOK, 128), bf16),
        ],
    )(z, x, gy, gates, weights, *codes)


def grads_kernel(x_ref, gy_ref, act_ref, dg_ref, du_ref, out_ref):
    x = x_ref[0].reshape(SLOTS, D)
    for i, grad in enumerate((dg_ref, du_ref)):
        made = dot(grad[0], x, TN).astype(bf16)
        out_ref[0, 0, i * HALF : (i + 1) * HALF] = made[:, :512]
        out_ref[0, 1, i * HALF : (i + 1) * HALF] = made[:, 512:]
    made = dot(act_ref[0], gy_ref[0].reshape(SLOTS, D), TN).astype(bf16)
    for i in range(2):
        out_ref[0, i, 512:640] = made[128 * i : 128 * i + 128, :512]
        out_ref[0, i, 640:768] = made[128 * i : 128 * i + 128, 512:]


def grads(x, gy, act, dg, du):
    return call(
        grads_kernel, "expert_grads", 8_000_000_000, 42_000_000,
        grid=(SHARE,),
        in_specs=[per_expert(4, PAIR, D)] * 2 + [per_expert(SLOTS, HALF)] * 3,
        out_specs=per_expert(2, 768, 512),
        out_shape=jax.ShapeDtypeStruct((SHARE, 2, 768, 512), bf16),
    )(x, gy, act, dg, du)


def outs_kernel(z_ref, act_ref, w_ref, *refs):
    codes_refs = refs[:8]
    own_ref, other_ref, kept, codes_kept = refs[8:]
    e = pl.program_id(0)
    z = z_ref[0]
    kept[e] = dot(act_ref[0], down_of(w_ref[...])).astype(bf16).reshape(BLOCKS, CAP, D)

    @pl.when(e == 0)
    def _():
        for b in range(BLOCKS):
            codes_kept[b] = codes_refs[b][...]

    @pl.when(e == SHARE - 1)
    def _():
        def pair(j, carry):
            for c, out in ((0, own_ref), (1, other_ref)):
                b = 2 * j + c
                place = slot_columns(codes_kept[b][:, :EXPERTS], z)
                rows = jnp.concatenate([kept[i, b] for i in range(SHARE)], axis=0)
                out[j] = dot(place, rows).astype(bf16)
            return carry

        lax.fori_loop(0, 4, pair, 0)


def outs(z, act, weights, codes):
    back = jax.ShapeDtypeStruct((4, TOK, D), bf16)
    return call(
        outs_kernel, "expert_outs", 6_000_000_000, 12_000_000,
        grid=(SHARE,),
        in_specs=[
            SCALAR, per_expert(SLOTS, HALF), pl.BlockSpec((2, 512, 256), lambda e: (e, 2, 0)), *codes_specs(),
        ],
        out_specs=[whole(4, TOK, D)] * 2,
        out_shape=[back, back],
        scratch_shapes=[pltpu.VMEM((SHARE, BLOCKS, CAP, D), bf16), pltpu.VMEM((BLOCKS, TOK, 128), bf16)],
    )(z, act, weights, *codes)


def shift(values, axis, by):
    n = 4 if axis in ("x", "z") else 2
    return lax.ppermute(values, axis, [(i, (i + by) % n) for i in range(n)])


def swap(values, axis):
    return shift(values, axis, 1)


def in_order(axis, own, other):
    first = lax.axis_index(axis) == 0
    return jnp.where(first, own, other), jnp.where(first, other, own)


def of_index(axis, zero, one):
    first = lax.axis_index(axis) == 0
    return jnp.where(first, zero, one), jnp.where(first, one, zero)


def gather_seq(values):
    pair = jnp.stack(in_order("ylo", values, swap(values, "ylo")))
    zero, one = in_order("core", pair, swap(pair, "core"))
    return jnp.stack([zero[0], one[0], zero[1], one[1]])


def scatter_seq(values):
    parts = values.astype(bf16).reshape((2, 2) + values.shape[1:])
    keep, send = of_index("core", parts[:, 0], parts[:, 1])
    pair = (keep.astype(f32) + swap(send, "core").astype(f32)).astype(bf16)
    keep, send = of_index("ylo", pair[0], pair[1])
    return keep.astype(f32) + swap(send, "ylo").astype(f32)


def gather_near(values):
    blocks = [values, shift(values, "z", 1), shift(values, "z", -1), shift(values, "z", 2)]
    return [(block, swap(block, "core")) for block in blocks]


def scatter_near(own, other):
    got = swap(other, "core")
    sums = [(own[j].astype(f32) + got[j].astype(f32)).astype(bf16) for j in range(4)]
    parts = [sums[0], shift(sums[1], "z", -1), shift(sums[2], "z", 1), shift(sums[3], "z", 2)]
    return sum(part.astype(f32) for part in parts)


def after(values, *others):
    return lax.optimization_barrier((values, *others))[0]


def on_device(
    tokens, norm1_gain, query_weight, key_weight, value_weight, output_weight, norm2_gain, router_weight,
    expert_gate, expert_up, expert_down, routes, cotangent,
):
    z = lax.axis_index("z").astype(jnp.int32).reshape(1)
    own_tokens = tokens.reshape(TOK, D)
    x_all = gather_seq(own_tokens).reshape(LENGTH, D)

    def halve(weight):
        parts = weight.reshape(TOK, 2, 2, 128)
        mine, theirs = of_index("core", parts[:, :, 0], parts[:, :, 1])
        return mine.reshape(TOK, HALF), theirs.reshape(TOK, HALF)

    gate_mine, gate_theirs = halve(expert_gate)
    up_mine, up_theirs = halve(expert_up)
    got = swap(jnp.stack([gate_theirs, up_theirs]), "core")
    down_part = expert_down.reshape(128, 4, 256).transpose(1, 0, 2).reshape(512, 256)
    expert_w = jnp.concatenate(
        [*in_order("core", gate_mine, got[0]), *in_order("core", up_mine, got[1]), down_part], axis=0
    )
    expert_w = lax.all_gather(expert_w, PLANE, axis=0).reshape(16, 1536, 256)

    query_part = query_weight.reshape(8, 4, GROUP, 2, 32).transpose(1, 0, 3, 2, 4).reshape(4, 8, 256)
    key_part = key_weight.reshape(8, 4, 2, 2, 32).transpose(1, 0, 3, 2, 4).reshape(4, 8, 128)
    value_part = value_weight.reshape(8, 4, 128).transpose(1, 0, 2)
    router_part = router_weight.reshape(8, 2, 4, 4).transpose(0, 3, 2, 1).reshape(8, EXPERTS)
    small = jnp.concatenate(
        [router_part, norm1_gain[:, None], norm2_gain[:, None], jnp.zeros((8, 94), bf16)], axis=1
    )
    packed = jnp.concatenate(
        [query_part, key_part, value_part, jnp.broadcast_to(small[None], (4, 8, 128))], axis=2
    )
    packed = jnp.broadcast_to(packed[:, None], (4, 32, 8, 640)).reshape(128, 8, 640)
    arrived = lax.all_to_all(packed, AXES, split_axis=0, concat_axis=0, tiled=True).reshape(D, 640)
    group_w = arrived[:, :512]
    router_w = arrived[:, 512:544]
    gain_one = arrived[:, 544].astype(f32).reshape(1, D)
    gain_two = arrived[:, 545].astype(f32).reshape(1, D)

    choices = routes.reshape(TOK, TOPK)
    column = jnp.arange(EXPERTS)
    expert_of = (column % 2) * 16 + (column % 8) // 2 * 4 + column // 8
    chosen = jnp.any(choices[:, :, None] == expert_of[None, None, :], axis=1)
    earlier = (jnp.arange(TOK)[None, :] < jnp.arange(TOK)[:, None]).astype(bf16)
    rank = dot(earlier, chosen.astype(bf16))
    own_codes = jnp.where(chosen, rank, -1.0).astype(bf16)
    grad_out = cotangent.reshape(TOK, D)
    gy_pairs = gather_near(jnp.concatenate([grad_out, own_codes, jnp.zeros((TOK, 96), bf16)], axis=1))
    codes = [block for pair in gy_pairs for block in pair]

    lane = jnp.arange(128) % 32
    angles = jnp.arange(LENGTH).astype(f32)[:, None] * (rope_base ** (-2.0 * lane.astype(f32) / HEAD))[None, :]
    cos, sin = jnp.cos(angles), jnp.sin(angles)
    q, k, v, mixed, lse, hidden_all = front(x_all, group_w, gain_one, cos, sin)

    output_part = after(output_weight, arrived)
    output_part = lax.all_to_all(
        jnp.broadcast_to(output_part[None], (32, 8, D)), FSDP, split_axis=0, concat_axis=0, tiled=True
    ).reshape(256, D)
    output_w = gather_seq(output_part).reshape(D, D)

    mixed = lax.all_to_all(mixed.reshape(4, TOK, 256), SEQ, split_axis=0, concat_axis=0, tiled=True)
    mixed = mixed.transpose(1, 0, 2).reshape(TOK, D)

    inputs = own_tokens.astype(f32)
    residual = inputs + dot(mixed, output_w)
    factor_two = lax.rsqrt(jnp.mean(residual * residual, axis=-1, keepdims=True) + epsilon)
    normed_two = residual * factor_two
    hidden_two = (normed_two * gain_two).astype(bf16)
    h_pairs = gather_near(hidden_two)

    gy_rows, rows = None, None
    for j in range(4):
        gy_rows = rows_of(z, j, gy_pairs[j], None, None, gy_rows)
    for j in range(4):
        rows = rows_of(z, j, h_pairs[j], gy_pairs[j], router_w, rows)
    (gy_rows,), (rows, gate_rows) = gy_rows, rows

    act, dg, du, back_own, back_other = main(z, rows, gy_rows, gate_rows, expert_w, codes)
    grad_hidden = scatter_near(back_own, back_other)
    expert_grads = grads(rows, gy_rows, act, dg, du)
    moe_own, moe_other = outs(z, act, expert_w, codes)
    layer_out = (residual + scatter_near(moe_own, moe_other)).astype(bf16).reshape(1, TOK, D)

    gates = gate_table(dot(hidden_two, router_w), own_codes.astype(f32))
    dgates = grad_hidden[:, D : D + EXPERTS]
    dlogits = (gates * (dgates - jnp.sum(gates * dgates, axis=-1, keepdims=True))).astype(bf16)
    grad_router = dot(hidden_two, dlogits, TN)
    grad_hidden = grad_hidden[:, :D] + dot(dlogits, router_w, NT)
    grad_gain_two = jnp.sum(grad_hidden * normed_two, axis=0)
    scaled = grad_hidden * gain_two
    grad_residual = grad_out.astype(f32) + factor_two * (
        scaled - normed_two * jnp.mean(scaled * normed_two, axis=-1, keepdims=True)
    )
    dz = grad_residual.astype(bf16)
    do = dot(dz, output_w, NT).astype(bf16).reshape(TOK, 4, 256).transpose(1, 0, 2)
    do = lax.all_to_all(do, SEQ, split_axis=0, concat_axis=0, tiled=True).reshape(LENGTH, 256)

    expert_grads = lax.psum_scatter(expert_grads.reshape(16 * 768, 512), PLANE, scatter_dimension=0, tiled=True)
    keep, send = of_index("core", expert_grads[:512, :256], expert_grads[:512, 256:])
    both = jnp.stack(in_order("core", keep, swap(send, "core"))).reshape(2, 2, 2, 128, TOK)
    both = both.transpose(1, 4, 2, 0, 3).reshape(2, 1, TOK, FF).astype(f32)
    grad_down = expert_grads[512:].reshape(2, 128, 512).transpose(1, 0, 2).reshape(1, 128, D).astype(f32)

    grad_output = dot(mixed, dz, TN).astype(bf16).reshape(128, 8, D)
    grad_output = lax.all_to_all(grad_output, AXES, split_axis=0, concat_axis=0, tiled=True)
    grad_output = jnp.sum(grad_output.astype(f32), axis=0)

    dqkv = back(q, k, v, do, lse, cos, sin)
    grad_group = dot(hidden_all, dqkv, TN).astype(bf16)
    partial = dot(dqkv, group_w, NT)
    x_float = x_all.astype(f32)
    normed_all = x_float * lax.rsqrt(jnp.mean(x_float * x_float, axis=-1, keepdims=True) + epsilon)
    grad_gain_one = jnp.sum(partial * normed_all, axis=0)
    grad_hidden_one = scatter_seq(partial.reshape(4, TOK, D))
    small = jnp.concatenate([grad_router, grad_gain_two[:, None], grad_gain_one[:, None]], axis=1)
    first = jnp.concatenate([grad_group, small.astype(bf16), jnp.zeros((D, 94), bf16)], axis=1)
    first = lax.all_to_all(first.reshape(128, 8, 640), AXES, split_axis=0, concat_axis=0, tiled=True)
    first = jnp.sum(first.astype(f32).reshape(4, 32, 8, 640), axis=1)
    grad_query = first[:, :, :256].reshape(4, 8, 2, GROUP, 32).transpose(1, 0, 3, 2, 4).reshape(8, D)
    grad_key = first[:, :, 256:384].reshape(4, 8, 2, 2, 32).transpose(1, 0, 3, 2, 4).reshape(8, 512)
    grad_value = first[:, :, 384:512].transpose(1, 0, 2).reshape(8, 512)
    small = jnp.sum(first[:, :, 512:], axis=0)
    grad_router = small[:, :EXPERTS].reshape(8, 4, 4, 2).transpose(0, 3, 2, 1).reshape(8, EXPERTS)

    factor_one = lax.rsqrt(jnp.mean(inputs * inputs, axis=-1, keepdims=True) + epsilon)
    normed_one = inputs * factor_one
    scaled = grad_hidden_one * gain_one
    grad_inputs = grad_residual + factor_one * (
        scaled - normed_one * jnp.mean(scaled * normed_one, axis=-1, keepdims=True)
    )
    return (
        layer_out, grad_inputs.reshape(1, TOK, D), small[:, 33], grad_query, grad_key, grad_value, grad_output,
        small[:, 32], grad_router, both[0], both[1], grad_down,
    )


def solution(mesh):
    fine = Mesh(mesh.devices.reshape(2, 2, 2, 4, 4), AXES)
    tok = P(FSDP, SEQ, None)
    row = P(AXES, None)
    vec = P(AXES)
    in_specs = (tok, vec, row, row, row, row, vec, row, tok, tok, tok, tok, tok)
    out_specs = (tok, tok, vec, row, row, row, row, vec, row, tok, tok, tok)
    return jax.shard_map(on_device, mesh=fine, in_specs=in_specs, out_specs=out_specs, check_vma=False)
```

time: 4960 us -> 522 us (0.11)
  waiting for transfers between devices: 3930 us -> 180 us
  blocking collectives: 542 us -> 42.1 us
  Pallas kernels: 0 us -> 131 us
  local copies, waits for them, and re-layouts: 152 us -> 33.3 us
  matrix products: 122 us -> 12.8 us
  other arithmetic: 83.3 us -> 32.7 us
    reduce_scatter x7 -> x1, waiting for transfers between devices: 2600 us -> 0.02 us  [on_device(): lax.psum_scatter(expert_grads.reshape(16 * 768, 512), PLANE, scatter_dime...]
    all_gather x7 -> x1, waiting for transfers between devices: 1120 us -> 0.01 us  [on_device(): expert_w = lax.all_gather(expert_w, PLANE, axis=0).reshape(16, 1536, 256)]
    all_gather x1 -> x0, blocking collectives: 387 us -> none  [on_device(): lax.all_gather(router_weight, ('seq', 'fsdp'), axis=0, tiled=True)]
    ppermute x0 -> x30, waiting for transfers between devices: none -> 135 us  [shift(): return lax.ppermute(values, axis, [(i, (i + by) % n) for i in range(n)])]
    unnamed x2 -> x0, blocking collectives: 134 us -> none
    pallas_call x0 -> x13, Pallas kernels: none -> 131 us  [the longest x8 38.2 us: rows_of(): call(functools.partial(rows_kernel, with_gates), 'rows', 1500000000, 4000...]
    dot_general x38 -> x9, matrix products: 122 us -> 12.8 us  [dot(): return lax.dot_general(a, b, dims, preferred_element_type=f32)]
    unnamed x16 -> x2, waiting for transfers between devices: 109 us -> 0.03 us
  transfers between devices with their start and end apart: 25 -> 37, of which waited for: 17 -> 15; matrix products, arithmetic and copies ran while one was open for 6% -> 12% of each run, Pallas kernels for 0% -> 15%
where the time goes in v1:
time: 522 us; the launch traced here: 515 us
  waiting for transfers between devices  180 us (34%)
  Pallas kernels  131 us (25%)
  starting transfers between devices  67.3 us (13%)
  blocking collectives  42.1 us (8%)
  local copies, waits for them, and re-layouts  33.3 us (6%)
  other arithmetic  32.7 us (6%)
  between operations  15 us (3%)
  matrix products  12.8 us (2%)
    ppermute x30, waiting for transfers between devices, shift(): return lax.ppermute(values, axis, [(i, (i + by) % n) for i in range(n)])  135 us
    all_to_all x1, blocking collectives, on_device(): lax.all_to_all(packed, AXES, split_axis=0, concat_axis=0, tiled=True)  42.1 us
    ppermute x30, starting transfers between devices, shift(): return lax.ppermute(values, axis, [(i, (i + by) % n) for i in range(n)])  39.2 us
    pallas_call x8, Pallas kernels, rows_of(): call(functools.partial(rows_kernel, with_gates), 'rows', 1500000000, 4000...  38.2 us
    pallas_call x1, Pallas kernels, main(): call(main_kernel, 'experts', 17000000000, 45000000, grid=(SHARE,), in_spe...  33.1 us
    pallas_call x1, Pallas kernels, grads(): call(grads_kernel, 'expert_grads', 8000000000, 42000000, grid=(SHARE,), i...  19.5 us
    pallas_call x1, Pallas kernels, outs(): call(outs_kernel, 'expert_outs', 6000000000, 12000000, grid=(SHARE,), in_...  14.7 us
    pallas_call x1, Pallas kernels, back(): pl.pallas_call(back_kernel, out_shape=jax.ShapeDtypeStruct((LENGTH, 512),...  14.6 us
  transfers between devices with their start and end apart: 37, of which 15 were waited for; matrix products, arithmetic and copies ran while one was open for 12% of the time, Pallas kernels for 15%

profile of v1, /device:TPU:1, one launch (start us, length us, event | category | flops | bytes accessed | tf_op | source)
XLA Modules:
  0.0 514.5 jit_solution(12337031106358950084)
XLA Ops:
  14.9 42.1 %all_to_all.30 = bf16[128,8,640]{2,1,0:T(8,128)(2,1)S(1)} all-to-all(bf16[128,8,640]{2,1,0:T(8,128)(2,1)S(1)} %bitcast.195), channel_id=1, replica_groups=mesh['ylo'=2,'core'=2,'yhi'=2,'x'=4,'z'=4] {'ylo','core','yhi','x','z'}, dimensions={0} | all-to-all | bytes 2621440 | tf_op jit(solution)/shard_map/all_to_all | solution.py:503
  57.9 5.7 %all-to-all-start.2 = ((bf16[32,8,1024]{2,1,0:T(8,128)(2,1)}), bf16[32,8,1024]{2,1,0:T(8,128)(2,1)S(1)}, u32[]{:S(2)}, u32[]{:S(2)}) async-start(bf16[32,8,1024]{2,1,0:T(8,128)(2,1)} %broadcast_in_dim.67), calls=%async_computation.2 | async-start | bytes 1048576 | tf_op jit(solution)/shard_map/all_to_all | solution.py:526
  65.3 14.2 %all-to-all-done.2 = bf16[32,8,1024]{2,1,0:T(8,128)(2,1)S(1)} async-done(((bf16[32,8,1024]{2,1,0:T(8,128)(2,1)}), bf16[32,8,1024]{2,1,0:T(8,128)(2,1)S(1)}, u32[]{:S(2)}, u32[]{:S(2)}) %all-to-all-start.2) | async-done | bytes 524320 | tf_op jit(solution)/shard_map/all_to_all | solution.py:526
  82.2 13.4 %collective-permute-done = bf16[256,1024]{1,0:T(8,128)(2,1)S(1)} collective-permute-done((bf16[256,1024]{1,0:T(8,128)(2,1)S(1)}, bf16[256,1024]{1,0:T(8,128)(2,1)S(1)}, u32[]{:S(2)}, u32[]{:S(2)}) %collective-permute-start) | collective-permute-done | bytes 524320 | tf_op jit(solution)/shard_map/ppermute | solution.py:423
  96.4 21.7 %collective-permute-done.2 = bf16[256,1024]{1,0:T(8,128)(2,1)} collective-permute-done((bf16[256,1024]{1,0:T(8,128)(2,1)S(1)}, bf16[256,1024]{1,0:T(8,128)(2,1)}, u32[]{:S(2)}, u32[]{:S(2)}) %collective-permute-start.2) | collective-permute-done | bytes 524320 | tf_op jit(solution)/shard_map/ppermute | solution.py:423
  133.3 19.8 %collective-permute-done.10.refs_2_.refs_0_.refs_4_ = bf16[256,1152]{1,0:T(8,128)(2,1)} collective-permute-done((bf16[256,1152]{1,0:T(8,128)(2,1)}, bf16[256,1152]{1,0:T(8,128)(2,1)}, u32[]{:S(2)}, u32[]{:S(2)}) %collective-permute-start.10) | collective-permute-done | bytes 589856 | tf_op jit(solution)/shard_map/ppermute | solution.py:423
  164.1 10.8 %front.1 = (bf16[1024,256]{1,0:T(8,128)(2,1)}, bf16[1024,256]{1,0:T(8,128)(2,1)}, bf16[1024,256]{1,0:T(8,128)(2,1)}, bf16[1024,256]{1,0:T(8,128)(2,1)}, f32[1024,128]{1,0:T(8,128)}, /*index=5*/bf16[1024,1024]{1,0:T(8,128)(2,1)}) custom-call(bf16[1024,1024]{1,0:T(8,128)(2,1)} %bitcast.197, bf16[1024,512]{1,0:T(8,128)(2,1)} %slice.214.w_ref, ...), custom_call_target="tpu_custom_call" | custom-call | flops 8000000000 | bytes 10000000 | tf_op jit(solution)/shard_map/front/pallas_call | solution.py:113
  174.9 3.9 all-to-all-start.1
  182.2 4.5 all-to-all-done.1
  194.3 3.9 rows.12.refs_2_
  198.2 6.6 %collective-permute-done.12.refs_0_ = bf16[256,1024]{1,0:T(8,128)(2,1)} collective-permute-done((bf16[256,1024]{1,0:T(8,128)(2,1)S(1)}, bf16[256,1024]{1,0:T(8,128)(2,1)}, u32[]{:S(2)}, u32[]{:S(2)}) %collective-permute-start.12) | collective-permute-done | bytes 524320 | tf_op jit(solution)/shard_map/ppermute | solution.py:423
  204.8 11.6 %collective-permute-start.13 = (bf16[256,1024]{1,0:T(8,128)(2,1)}, bf16[256,1024]{1,0:T(8,128)(2,1)S(1)}, u32[]{:S(2)}, u32[]{:S(2)}) collective-permute-start(bf16[256,1024]{1,0:T(8,128)(2,1)} %collective-permute-done.12.refs_0_), channel_id=1, source_target_pairs={{0,32},{32,0},{1,33},{33,1},{2,34},{34,2},{3,35},{35,3},{4,36},{36... | collective-permute-start | bytes 1572872 | tf_op jit(solution)/shard_map/ppermute | solution.py:423
  220.3 3.9 rows.14.refs_2_
  231.0 5.7 %rows.8 = (bf16[8,4,160,1024]{3,2,1,0:T(8,128)(2,1)}, f32[8,4,160,1]{3,2,1,0:T(8,128)}) custom-call(s32[1]{0:T(128)} %bitcast.21.z_ref, bf16[256,1024]{1,0:T(8,128)(2,1)} %copy-done.6, bf16[256,1024]{1,0:T(8,128)(2,1)} %copy-done.35, bf16[256,1152]{1,0:T(8,128)(2,1)} %concatenate.21.refs_2_.refs_0_, ...), custom_call_target="tpu_custom_call" | custom-call | flops 1500000000 | bytes 4000000 | tf_op jit(solution)/shard_map/rows/pallas_call | solution.py:270
  237.5 5.6 %rows.9 = (bf16[8,4,160,1024]{3,2,1,0:T(8,128)(2,1)}, f32[8,4,160,1]{3,2,1,0:T(8,128)}) custom-call(s32[1]{0:T(128)} %bitcast.21.z_ref, bf16[256,1024]{1,0:T(8,128)(2,1)} %collective-permute-done.12.refs_0_, bf16[256,1024]{1,0:T(8,128)(2,1)} %copy-done.22, ...), custom_call_target="tpu_custom_call", output_to_operand_aliasing={{0}: (6, {}), {1}: (7, {})} | custom-call | flops 1500000000 | bytes 4000000 | tf_op jit(solution)/shard_map/rows/pallas_call | solution.py:270
  243.9 5.6 %rows.10 = (bf16[8,4,160,1024]{3,2,1,0:T(8,128)(2,1)}, f32[8,4,160,1]{3,2,1,0:T(8,128)}) custom-call(s32[1]{0:T(128)} %bitcast.21.z_ref, bf16[256,1024]{1,0:T(8,128)(2,1)} %collective-permute-done.8.refs_0_, bf16[256,1024]{1,0:T(8,128)(2,1)} %copy-done.21, ...), custom_call_target="tpu_custom_call", output_to_operand_aliasing={{0}: (6, {}), {1}: (7, {})} | custom-call | flops 1500000000 | bytes 4000000 | tf_op jit(solution)/shard_map/rows/pallas_call | solution.py:270
  250.3 5.7 %rows.11 = (bf16[8,4,160,1024]{3,2,1,0:T(8,128)(2,1)}, f32[8,4,160,1]{3,2,1,0:T(8,128)}) custom-call(s32[1]{0:T(128)} %bitcast.21.z_ref, bf16[256,1024]{1,0:T(8,128)(2,1)} %collective-permute-done.4.refs_0_, bf16[256,1024]{1,0:T(8,128)(2,1)} %copy-done.20, ...), custom_call_target="tpu_custom_call", output_to_operand_aliasing={{0}: (6, {}), {1}: (7, {})} | custom-call | flops 1500000000 | bytes 4000000 | tf_op jit(solution)/shard_map/rows/pallas_call | solution.py:270
  256.0 33.1 %experts.1 = (bf16[8,640,256]{2,1,0:T(8,128)(2,1)}, bf16[8,640,256]{2,1,0:T(8,128)(2,1)}, bf16[8,640,256]{2,1,0:T(8,128)(2,1)}, bf16[4,256,1152]{2,1,0:T(8,128)(2,1)}, bf16[4,256,1152]{2,1,0:T(8,128)(2,1)}) custom-call(s32[1]{0:T(128)} %bitcast.21.z_ref, bf16[8,4,160,1024]{3,2,1,0:T(8,128)(2,1)} %get-tuple-element.42.x_ref, ...), custom_call_target="tpu_custom_call" | custom-call | flops 16999999488 | bytes 45000000 | tf_op jit(solution)/shard_map/experts/pallas_call | solution.py:343
  289.1 19.5 %expert_grads.1 = bf16[8,2,768,512]{3,2,1,0:T(8,128)(2,1)} custom-call(bf16[8,4,160,1024]{3,2,1,0:T(8,128)(2,1)} %get-tuple-element.42.x_ref, bf16[8,4,160,1024]{3,2,1,0:T(8,128)(2,1)} %rows.15.gy_ref, bf16[8,640,256]{2,1,0:T(8,128)(2,1)} %get-tuple-element.44.act_ref, bf16[8,640,256]{2,1,0:T(8,128)(2,1)} %get-tuple-element.54.dg_ref, ...), custom_call_target="tpu_custom_call" | custom-call | flops 8000000000 | bytes 42000000 | tf_op jit(solution)/shard_map/expert_grads/pallas_call | solution.py:373
  308.7 14.7 %expert_outs.1 = (bf16[4,256,1024]{2,1,0:T(8,128)(2,1)}, bf16[4,256,1024]{2,1,0:T(8,128)(2,1)}) custom-call(s32[1]{0:T(128)} %bitcast.21.z_ref, bf16[8,640,256]{2,1,0:T(8,128)(2,1)} %get-tuple-element.44.act_ref, bf16[16,1536,256]{2,1,0:T(8,128)(2,1)} %bitcast.231, bf16[256,1152]{1,0:T(8,128)(2,1)} %concatenate.21.refs_2_.refs_0_, ...), custom_call_target="tpu_custom_call" | custom-call | flops 6000000000 | bytes 12000000 | tf_op jit(solution)/shard_map/expert_outs/pallas_call | solution.py:409
  331.9 10.4 %collective-permute-done.26 = bf16[256,1152]{1,0:T(8,128)(2,1)S(1)} collective-permute-done((bf16[256,1152]{1,0:T(8,128)(2,1)S(1)}, bf16[256,1152]{1,0:T(8,128)(2,1)S(1)}, u32[]{:S(2)}, u32[]{:S(2)}) %collective-permute-start.26) | collective-permute-done | bytes 589856 | tf_op jit(solution)/shard_map/ppermute | solution.py:423
  342.2 13.0 %collective-permute-done.25 = bf16[256,1152]{1,0:T(8,128)(2,1)S(1)} collective-permute-done((bf16[256,1152]{1,0:T(8,128)(2,1)S(1)}, bf16[256,1152]{1,0:T(8,128)(2,1)S(1)}, u32[]{:S(2)}, u32[]{:S(2)}) %collective-permute-start.25) | collective-permute-done | bytes 589856 | tf_op jit(solution)/shard_map/ppermute | solution.py:423
  356.5 9.6 %collective-permute-done.22 = bf16[256,1024]{1,0:T(8,128)(2,1)S(1)} collective-permute-done((bf16[256,1024]{1,0:T(8,128)(2,1)S(1)}, bf16[256,1024]{1,0:T(8,128)(2,1)S(1)}, u32[]{:S(2)}, u32[]{:S(2)}) %collective-permute-start.22) | collective-permute-done | bytes 524320 | tf_op jit(solution)/shard_map/ppermute | solution.py:423
  366.1 11.4 %collective-permute-done.21 = bf16[256,1024]{1,0:T(8,128)(2,1)S(1)} collective-permute-done((bf16[256,1024]{1,0:T(8,128)(2,1)S(1)}, bf16[256,1024]{1,0:T(8,128)(2,1)S(1)}, u32[]{:S(2)}, u32[]{:S(2)}) %collective-permute-start.21) | collective-permute-done | bytes 524320 | tf_op jit(solution)/shard_map/ppermute | solution.py:423
  380.6 4.5 all-to-all-start.3
  385.4 13.2 %all-to-all-done.3 = bf16[4,256,256]{2,1,0:T(8,128)(2,1)S(1)} async-done(((bf16[4,256,256]{2,1,0:T(8,128)(2,1)}), bf16[4,256,256]{2,1,0:T(8,128)(2,1)S(1)}, u32[]{:S(2)}, u32[]{:S(2)}) %all-to-all-start.3) | async-done | bytes 524320 | tf_op jit(solution)/shard_map/all_to_all | solution.py:566
  399.4 14.6 %back.1 = bf16[1024,512]{1,0:T(8,128)(2,1)} custom-call(bf16[1024,256]{1,0:T(8,128)(2,1)} %get-tuple-element.49.q_ref, bf16[1024,256]{1,0:T(8,128)(2,1)} %get-tuple-element.50.k_ref, bf16[1024,256]{1,0:T(8,128)(2,1)} %get-tuple-element.51.v_ref, bf16[1024,256]{1,0:T(8,128)(2,1)} %bitcast.213, f32[1024,128]{1,0:T(8,128)} %get-tuple-element.52.lse_ref, ...), custom_call_target="tpu_custom_call" | custom-call | flops 14000000000 | bytes 6000000 | tf_op jit(solution)/shard_map/back/pallas_call | solution.py:170
  414.0 4.0 multiply_reduce_fusion
  423.1 8.0 %all-to-all-start.4 = ((bf16[128,8,640]{2,1,0:T(8,128)(2,1)}), bf16[128,8,640]{2,1,0:T(8,128)(2,1)S(1)}, u32[]{:S(2)}, u32[]{:S(2)}) async-start(bf16[128,8,640]{2,1,0:T(8,128)(2,1)} %bitcast.194), calls=%async_computation.4 | async-start | bytes 2621440 | tf_op jit(solution)/shard_map/all_to_all | solution.py:587
  438.4 13.5 %all-to-all-done.4 = bf16[128,8,640]{2,1,0:T(8,128)(2,1)S(1)} async-done(((bf16[128,8,640]{2,1,0:T(8,128)(2,1)}), bf16[128,8,640]{2,1,0:T(8,128)(2,1)S(1)}, u32[]{:S(2)}, u32[]{:S(2)}) %all-to-all-start.4) | async-done | bytes 1310752 | tf_op jit(solution)/shard_map/all_to_all | solution.py:587
  453.0 5.8 %all-to-all-start.5 = ((bf16[128,8,1024]{2,1,0:T(8,128)(2,1)}), bf16[128,8,1024]{2,1,0:T(8,128)(2,1)}, u32[]{:S(2)}, u32[]{:S(2)}) async-start(bf16[128,8,1024]{2,1,0:T(8,128)(2,1)} %convert_bitcast_fusion), calls=%async_computation.5 | async-start | bytes 4194304 | tf_op jit(solution)/shard_map/all_to_all | solution.py:575
  467.9 25.8 %collective-permute-done.28 = bf16[256,1024]{1,0:T(8,128)(2,1)S(1)} collective-permute-done((bf16[256,1024]{1,0:T(8,128)(2,1)}, bf16[256,1024]{1,0:T(8,128)(2,1)S(1)}, u32[]{:S(2)}, u32[]{:S(2)}) %collective-permute-start.28) | collective-permute-done | bytes 524320 | tf_op jit(solution)/shard_map/ppermute | solution.py:423
  (252 shorter events, 113.5 us)
Async XLA Ops:
  7.2 248.8 %all-gather.3.cloned.1.call-start = ((), (), s32[]{:S(2)}) async-start(), calls=%async_computation.8 | async-start | bytes 13369344 | tf_op jit(solution)/shard_map/all_gather | solution.py:490
  57.9 21.5 %all-to-all-start.2 = ((bf16[32,8,1024]{2,1,0:T(8,128)(2,1)}), bf16[32,8,1024]{2,1,0:T(8,128)(2,1)S(1)}, u32[]{:S(2)}, u32[]{:S(2)}) async-start(bf16[32,8,1024]{2,1,0:T(8,128)(2,1)} %broadcast_in_dim.67), calls=%async_computation.2 | async-start | bytes 1048576 | tf_op jit(solution)/shard_map/all_to_all | solution.py:526
  63.7 31.9 %collective-permute-start = (bf16[256,1024]{1,0:T(8,128)(2,1)S(1)}, bf16[256,1024]{1,0:T(8,128)(2,1)S(1)}, u32[]{:S(2)}, u32[]{:S(2)}) collective-permute-start(bf16[256,1024]{1,0:T(8,128)(2,1)S(1)} %bitcast.191), channel_id=1, source_target_pairs={{0,64},{64,0},{1,65},{65,1},{2,66},{66,2},{3,67},{67,3},{4,68},{68... | collective-permute-start | bytes 1572872 | tf_op jit(solution)/shard_map/ppermute | solution.py:423
  79.5 38.6 %collective-permute-start.2 = (bf16[256,1024]{1,0:T(8,128)(2,1)S(1)}, bf16[256,1024]{1,0:T(8,128)(2,1)}, u32[]{:S(2)}, u32[]{:S(2)}) collective-permute-start(bf16[256,1024]{1,0:T(8,128)(2,1)S(1)} %bitcast.198), channel_id=1, source_target_pairs={{0,64},{64,0},{1,65},{65,1},{2,66},{66,2},{3,67},{67,3},{4,68},{68... | collective-permute-start | bytes 1572872 | tf_op jit(solution)/shard_map/ppermute | solution.py:423
  121.4 39.2 %collective-permute-start.1 = (bf16[2,256,1024]{2,1,0:T(8,128)(2,1)}, bf16[2,256,1024]{2,1,0:T(8,128)(2,1)}, u32[]{:S(2)}, u32[]{:S(2)}) collective-permute-start(bf16[2,256,1024]{2,1,0:T(8,128)(2,1)} %pad_maximum_fusion.2), channel_id=1, source_target_pairs={{0,32},{32,0},{1,33},{33,1},{2,34},{34,2},{3,35},{35,3},{4,36},{36... | collective-permute-start | bytes 3145736 | tf_op jit(solution)/shard_map/ppermute | solution.py:423
  124.8 28.3 %collective-permute-start.10 = (bf16[256,1152]{1,0:T(8,128)(2,1)}, bf16[256,1152]{1,0:T(8,128)(2,1)}, u32[]{:S(2)}, u32[]{:S(2)}) collective-permute-start(bf16[256,1152]{1,0:T(8,128)(2,1)} %concatenate.21.refs_2_.refs_0_), channel_id=1, source_target_pairs={{0,3},{1,0},{2,1},{3,2},{4,7},{5,4},{6,5},{7,6},{8,11},{9,8},{10,9... | collective-permute-start | bytes 1769480 | tf_op jit(solution)/shard_map/ppermute | solution.py:423
  127.6 28.8 %collective-permute-start.14 = (bf16[256,1152]{1,0:T(8,128)(2,1)}, bf16[256,1152]{1,0:T(8,128)(2,1)}, u32[]{:S(2)}, u32[]{:S(2)}) collective-permute-start(bf16[256,1152]{1,0:T(8,128)(2,1)} %concatenate.21.refs_2_.refs_0_), channel_id=1, source_target_pairs={{0,1},{1,2},{2,3},{3,0},{4,5},{5,6},{6,7},{7,4},{8,9},{9,10},{10,1... | collective-permute-start | bytes 1769480 | tf_op jit(solution)/shard_map/ppermute | solution.py:423
  127.6 62.0 %collective-permute-start.6 = (bf16[256,1152]{1,0:T(8,128)(2,1)}, bf16[256,1152]{1,0:T(8,128)(2,1)}, u32[]{:S(2)}, u32[]{:S(2)}) collective-permute-start(bf16[256,1152]{1,0:T(8,128)(2,1)} %concatenate.21.refs_2_.refs_0_), channel_id=1, source_target_pairs={{0,2},{1,3},{2,0},{3,1},{4,6},{5,7},{6,4},{7,5},{8,10},{9,11},{10,... | collective-permute-start | bytes 1769480 | tf_op jit(solution)/shard_map/ppermute | solution.py:423
  129.4 62.8 %collective-permute-start.17 = (bf16[256,1152]{1,0:T(8,128)(2,1)}, bf16[256,1152]{1,0:T(8,128)(2,1)}, u32[]{:S(2)}, u32[]{:S(2)}) collective-permute-start(bf16[256,1152]{1,0:T(8,128)(2,1)} %concatenate.21.refs_2_.refs_0_), channel_id=1, source_target_pairs={{0,32},{32,0},{1,33},{33,1},{2,34},{34,2},{3,35},{35,3},{4,36},{36... | collective-permute-start | bytes 1769480 | tf_op jit(solution)/shard_map/ppermute | solution.py:423
  153.2 40.5 %collective-permute-start.11 = (bf16[256,1152]{1,0:T(8,128)(2,1)}, bf16[256,1152]{1,0:T(8,128)(2,1)}, u32[]{:S(2)}, u32[]{:S(2)}) collective-permute-start(bf16[256,1152]{1,0:T(8,128)(2,1)} %collective-permute-done.10.refs_2_.refs_0_.refs_4_), channel_id=1, source_target_pairs={{0,32},{32,0},{1,33},{33,1},{2,34},{34,2},{3,35},{35,3},{4,36},{36... | collective-permute-start | bytes 1769480 | tf_op jit(solution)/shard_map/ppermute | solution.py:423
  156.4 37.3 %collective-permute-start.15 = (bf16[256,1152]{1,0:T(8,128)(2,1)}, bf16[256,1152]{1,0:T(8,128)(2,1)}, u32[]{:S(2)}, u32[]{:S(2)}) collective-permute-start(bf16[256,1152]{1,0:T(8,128)(2,1)} %collective-permute-done.14.refs_2_.refs_0_), channel_id=1, source_target_pairs={{0,32},{32,0},{1,33},{33,1},{2,34},{34,2},{3,35},{35,3},{4,36},{36... | collective-permute-start | bytes 1769480 | tf_op jit(solution)/shard_map/ppermute | solution.py:423
  160.6 18.2 %collective-permute-start.3 = (bf16[2,256,1024]{2,1,0:T(8,128)(2,1)}, bf16[2,256,1024]{2,1,0:T(8,128)(2,1)}, u32[]{:S(2)}, u32[]{:S(2)}) collective-permute-start(bf16[2,256,1024]{2,1,0:T(8,128)(2,1)} %pad_maximum_fusion.3), channel_id=1, source_target_pairs={{0,32},{32,0},{1,33},{33,1},{2,34},{34,2},{3,35},{35,3},{4,36},{36... | collective-permute-start | bytes 3145736 | tf_op jit(solution)/shard_map/ppermute | solution.py:423
  178.8 315.3 %reduce-scatter.2.cloned.1.call-start = ((), (), s32[]{:S(2)}) async-start(), calls=%async_computation.7 | async-start | bytes 13369344 | tf_op jit(solution)/shard_map/reduce_scatter | solution.py:568
  189.6 30.7 %collective-permute-start.8 = (bf16[256,1024]{1,0:T(8,128)(2,1)S(1)}, bf16[256,1024]{1,0:T(8,128)(2,1)}, u32[]{:S(2)}, u32[]{:S(2)}) collective-permute-start(bf16[256,1024]{1,0:T(8,128)(2,1)S(1)} %multiply_convert_fusion.refs_0_), channel_id=1, source_target_pairs={{0,3},{1,0},{2,1},{3,2},{4,7},{5,4},{6,5},{7,6},{8,11},{9,8},{10,9... | collective-permute-start | bytes 1572872 | tf_op jit(solution)/shard_map/ppermute | solution.py:423
  192.2 32.5 %collective-permute-start.7 = (bf16[256,1152]{1,0:T(8,128)(2,1)}, bf16[256,1152]{1,0:T(8,128)(2,1)S(1)}, u32[]{:S(2)}, u32[]{:S(2)}) collective-permute-start(bf16[256,1152]{1,0:T(8,128)(2,1)} %collective-permute-done.6.refs_2_.refs_0_.refs_6_), channel_id=1, source_target_pairs={{0,32},{32,0},{1,33},{33,1},{2,34},{34,2},{3,35},{35,3},{4,36},{36... | collective-permute-start | bytes 1769480 | tf_op jit(solution)/shard_map/ppermute | solution.py:423
  193.7 30.6 %collective-permute-start.4 = (bf16[256,1024]{1,0:T(8,128)(2,1)S(1)}, bf16[256,1024]{1,0:T(8,128)(2,1)}, u32[]{:S(2)}, u32[]{:S(2)}) collective-permute-start(bf16[256,1024]{1,0:T(8,128)(2,1)S(1)} %multiply_convert_fusion.refs_0_), channel_id=1, source_target_pairs={{0,2},{1,3},{2,0},{3,1},{4,6},{5,7},{6,4},{7,5},{8,10},{9,11},{10,... | collective-permute-start | bytes 1572872 | tf_op jit(solution)/shard_map/ppermute | solution.py:423
  193.7 36.5 %collective-permute-start.16 = (bf16[256,1024]{1,0:T(8,128)(2,1)S(1)}, bf16[256,1024]{1,0:T(8,128)(2,1)S(1)}, u32[]{:S(2)}, u32[]{:S(2)}) collective-permute-start(bf16[256,1024]{1,0:T(8,128)(2,1)S(1)} %multiply_convert_fusion.refs_0_), channel_id=1, source_target_pairs={{0,32},{32,0},{1,33},{33,1},{2,34},{34,2},{3,35},{35,3},{4,36},{36... | collective-permute-start | bytes 1572872 | tf_op jit(solution)/shard_map/ppermute | solution.py:423
  204.8 31.9 %collective-permute-start.13 = (bf16[256,1024]{1,0:T(8,128)(2,1)}, bf16[256,1024]{1,0:T(8,128)(2,1)S(1)}, u32[]{:S(2)}, u32[]{:S(2)}) collective-permute-start(bf16[256,1024]{1,0:T(8,128)(2,1)} %collective-permute-done.12.refs_0_), channel_id=1, source_target_pairs={{0,32},{32,0},{1,33},{33,1},{2,34},{34,2},{3,35},{35,3},{4,36},{36... | collective-permute-start | bytes 1572872 | tf_op jit(solution)/shard_map/ppermute | solution.py:423
  220.3 22.8 %collective-permute-start.9 = (bf16[256,1024]{1,0:T(8,128)(2,1)}, bf16[256,1024]{1,0:T(8,128)(2,1)S(1)}, u32[]{:S(2)}, u32[]{:S(2)}) collective-permute-start(bf16[256,1024]{1,0:T(8,128)(2,1)} %collective-permute-done.8.refs_0_), channel_id=1, source_target_pairs={{0,32},{32,0},{1,33},{33,1},{2,34},{34,2},{3,35},{35,3},{4,36},{36... | collective-permute-start | bytes 1572872 | tf_op jit(solution)/shard_map/ppermute | solution.py:423
  224.2 25.3 %collective-permute-start.5 = (bf16[256,1024]{1,0:T(8,128)(2,1)}, bf16[256,1024]{1,0:T(8,128)(2,1)S(1)}, u32[]{:S(2)}, u32[]{:S(2)}) collective-permute-start(bf16[256,1024]{1,0:T(8,128)(2,1)} %collective-permute-done.4.refs_0_), channel_id=1, source_target_pairs={{0,32},{32,0},{1,33},{33,1},{2,34},{34,2},{3,35},{35,3},{4,36},{36... | collective-permute-start | bytes 1572872 | tf_op jit(solution)/shard_map/ppermute | solution.py:423
  308.6 16.9 %collective-permute-start.23 = (bf16[4,256,1152]{2,1,0:T(8,128)(2,1)}, bf16[4,256,1152]{2,1,0:T(8,128)(2,1)S(1)}, u32[]{:S(2)}, u32[]{:S(2)}) collective-permute-start(bf16[4,256,1152]{2,1,0:T(8,128)(2,1)} %get-tuple-element.48), channel_id=1, source_target_pairs={{0,32},{32,0},{1,33},{33,1},{2,34},{34,2},{3,35},{35,3},{4,36},{36... | collective-permute-start | bytes 7077896 | tf_op jit(solution)/shard_map/ppermute | solution.py:423
  326.0 16.2 %collective-permute-start.26 = (bf16[256,1152]{1,0:T(8,128)(2,1)S(1)}, bf16[256,1152]{1,0:T(8,128)(2,1)S(1)}, u32[]{:S(2)}, u32[]{:S(2)}) collective-permute-start(bf16[256,1152]{1,0:T(8,128)(2,1)S(1)} %get-tuple-element.125), channel_id=1, source_target_pairs={{0,2},{1,3},{2,0},{3,1},{4,6},{5,7},{6,4},{7,5},{8,10},{9,11},{10,... | collective-permute-start | bytes 1769480 | tf_op jit(solution)/shard_map/ppermute | solution.py:423
  326.1 29.1 %collective-permute-start.25 = (bf16[256,1152]{1,0:T(8,128)(2,1)S(1)}, bf16[256,1152]{1,0:T(8,128)(2,1)S(1)}, u32[]{:S(2)}, u32[]{:S(2)}) collective-permute-start(bf16[256,1152]{1,0:T(8,128)(2,1)S(1)} %get-tuple-element.126), channel_id=1, source_target_pairs={{0,1},{1,2},{2,3},{3,0},{4,5},{5,6},{6,7},{7,4},{8,9},{9,10},{10,1... | collective-permute-start | bytes 1769480 | tf_op jit(solution)/shard_map/ppermute | solution.py:423
  326.2 29.0 %collective-permute-start.24 = (bf16[256,1152]{1,0:T(8,128)(2,1)S(1)}, bf16[256,1152]{1,0:T(8,128)(2,1)S(1)}, u32[]{:S(2)}, u32[]{:S(2)}) collective-permute-start(bf16[256,1152]{1,0:T(8,128)(2,1)S(1)} %get-tuple-element.124), channel_id=1, source_target_pairs={{0,3},{1,0},{2,1},{3,2},{4,7},{5,4},{6,5},{7,6},{8,11},{9,8},{10,9... | collective-permute-start | bytes 1769480 | tf_op jit(solution)/shard_map/ppermute | solution.py:423
  330.1 36.0 %collective-permute-start.22 = (bf16[256,1024]{1,0:T(8,128)(2,1)S(1)}, bf16[256,1024]{1,0:T(8,128)(2,1)S(1)}, u32[]{:S(2)}, u32[]{:S(2)}) collective-permute-start(bf16[256,1024]{1,0:T(8,128)(2,1)S(1)} %get-tuple-element.130), channel_id=1, source_target_pairs={{0,2},{1,3},{2,0},{3,1},{4,6},{5,7},{6,4},{7,5},{8,10},{9,11},{10,... | collective-permute-start | bytes 1572872 | tf_op jit(solution)/shard_map/ppermute | solution.py:423
  331.9 45.6 %collective-permute-start.21 = (bf16[256,1024]{1,0:T(8,128)(2,1)S(1)}, bf16[256,1024]{1,0:T(8,128)(2,1)S(1)}, u32[]{:S(2)}, u32[]{:S(2)}) collective-permute-start(bf16[256,1024]{1,0:T(8,128)(2,1)S(1)} %get-tuple-element.131), channel_id=1, source_target_pairs={{0,1},{1,2},{2,3},{3,0},{4,5},{5,6},{6,7},{7,4},{8,9},{9,10},{10,1... | collective-permute-start | bytes 1572872 | tf_op jit(solution)/shard_map/ppermute | solution.py:423
  342.2 35.3 %collective-permute-start.20 = (bf16[256,1024]{1,0:T(8,128)(2,1)S(1)}, bf16[256,1024]{1,0:T(8,128)(2,1)S(1)}, u32[]{:S(2)}, u32[]{:S(2)}) collective-permute-start(bf16[256,1024]{1,0:T(8,128)(2,1)S(1)} %get-tuple-element.129), channel_id=1, source_target_pairs={{0,3},{1,0},{2,1},{3,2},{4,7},{5,4},{6,5},{7,6},{8,11},{9,8},{10,9... | collective-permute-start | bytes 1572872 | tf_op jit(solution)/shard_map/ppermute | solution.py:423
  380.6 18.0 %all-to-all-start.3 = ((bf16[4,256,256]{2,1,0:T(8,128)(2,1)}), bf16[4,256,256]{2,1,0:T(8,128)(2,1)S(1)}, u32[]{:S(2)}, u32[]{:S(2)}) async-start(bf16[4,256,256]{2,1,0:T(8,128)(2,1)} %bitcast.202), calls=%async_computation.3 | async-start | bytes 1048576 | tf_op jit(solution)/shard_map/all_to_all | solution.py:566
  423.1 28.8 %all-to-all-start.4 = ((bf16[128,8,640]{2,1,0:T(8,128)(2,1)}), bf16[128,8,640]{2,1,0:T(8,128)(2,1)S(1)}, u32[]{:S(2)}, u32[]{:S(2)}) async-start(bf16[128,8,640]{2,1,0:T(8,128)(2,1)} %bitcast.194), calls=%async_computation.4 | async-start | bytes 2621440 | tf_op jit(solution)/shard_map/all_to_all | solution.py:587
  433.8 25.0 %collective-permute-start.27 = (bf16[2,256,1024]{2,1,0:T(8,128)(2,1)}, bf16[2,256,1024]{2,1,0:T(8,128)(2,1)}, u32[]{:S(2)}, u32[]{:S(2)}) collective-permute-start(bf16[2,256,1024]{2,1,0:T(8,128)(2,1)} %select_bitcast_fusion), channel_id=1, source_target_pairs={{0,32},{32,0},{1,33},{33,1},{2,34},{34,2},{3,35},{35,3},{4,36},{36... | collective-permute-start | bytes 3145736 | tf_op jit(solution)/shard_map/ppermute | solution.py:423
  453.0 44.5 %all-to-all-start.5 = ((bf16[128,8,1024]{2,1,0:T(8,128)(2,1)}), bf16[128,8,1024]{2,1,0:T(8,128)(2,1)}, u32[]{:S(2)}, u32[]{:S(2)}) async-start(bf16[128,8,1024]{2,1,0:T(8,128)(2,1)} %convert_bitcast_fusion), calls=%async_computation.5 | async-start | bytes 4194304 | tf_op jit(solution)/shard_map/all_to_all | solution.py:575
  462.3 31.3 %collective-permute-start.28 = (bf16[256,1024]{1,0:T(8,128)(2,1)}, bf16[256,1024]{1,0:T(8,128)(2,1)S(1)}, u32[]{:S(2)}, u32[]{:S(2)}) collective-permute-start(bf16[256,1024]{1,0:T(8,128)(2,1)} %select_bitcast_fusion.1), channel_id=1, source_target_pairs={{0,64},{64,0},{1,65},{65,1},{2,66},{66,2},{3,67},{67,3},{4,68},{68... | collective-permute-start | bytes 1572872 | tf_op jit(solution)/shard_map/ppermute | solution.py:423
  (44 other events, 417.5 us)
Sparse Core Ops, SparseCore 0:
  13.9 130.5 all-gather.2
  308.7 96.9 reduce-scatter.1

commit v2 on v1

v2 whole, which is shorter than its diff:
```python
import functools

import jax
import jax.numpy as jnp
from jax import lax
from jax.experimental import pallas as pl
from jax.experimental.pallas import tpu as pltpu
from jax.sharding import Mesh
from jax.sharding import PartitionSpec as P

HEADS = 16
KV_HEADS = 8
HEAD = 64
TOPK = 8
CAP = 80
TOK = 256
D = 1024
FF = 512
EXPERTS = 32
SHARE = 8
SLOTS = SHARE * CAP
BLOCKS = 8
HALF = FF // 2
GROUP = 4
LENGTH = 1024

epsilon = 1e-06
rope_base = 10000.0

AXES = ("ylo", "core", "yhi", "x", "z")
SEQ = ("ylo", "core")
FSDP = ("yhi", "x", "z")
PLANE = ("x", "yhi", "ylo")

f32 = jnp.float32
bf16 = jnp.bfloat16

NT = (((1,), (1,)), ((), ()))
TN = (((0,), (0,)), ((), ()))
VMEM_LIMIT = 56 * 1024 * 1024


def dot(a, b, dims=(((1,), (0,)), ((), ()))):
    return lax.dot_general(a, b, dims, preferred_element_type=f32)


def iota(shape, axis):
    return lax.broadcasted_iota(jnp.int32, shape, axis)


def as_bf16(cond):
    return jnp.where(cond, 1.0, 0.0).astype(bf16)


def call(kernel, name, flops, moved, **kwargs):
    return pl.pallas_call(
        kernel,
        compiler_params=pltpu.CompilerParams(vmem_limit_bytes=VMEM_LIMIT),
        cost_estimate=pl.CostEstimate(flops=flops, bytes_accessed=moved, transcendentals=0),
        name=name,
        **kwargs,
    )


def shape(*dims, dtype=bf16):
    return jax.ShapeDtypeStruct(dims, dtype)


SCALAR = pl.BlockSpec(memory_space=pltpu.SMEM)
ANYWHERE = pl.BlockSpec(memory_space=pl.ANY)
VECTOR = pl.BlockSpec(memory_space=pltpu.VMEM)


def column_of(row):
    n = row.shape[1]
    step = min(n, 128)
    same = iota((step, step), 0) == iota((step, step), 1)
    parts = [jnp.sum(jnp.where(same, row[:, i : i + step], 0.0), axis=1, keepdims=True) for i in range(0, n, step)]
    return jnp.concatenate(parts, axis=0) if len(parts) > 1 else parts[0]


def row_of(column):
    n = column.shape[0]
    same = iota((128, 128), 0) == iota((128, 128), 1)
    parts = [jnp.sum(jnp.where(same, column[i : i + 128], 0.0), axis=0, keepdims=True) for i in range(0, n, 128)]
    return jnp.concatenate(parts, axis=1)


def codes_kernel(routes_ref, gy_ref, gy_out_ref):
    routes = routes_ref[...]
    expert = iota((TOK, EXPERTS), 1)
    chosen = jnp.zeros((TOK, EXPERTS), jnp.bool_)
    for i in range(TOPK):
        chosen = chosen | (routes[:, i : i + 1] == expert)
    earlier = as_bf16(iota((TOK, TOK), 1) < iota((TOK, TOK), 0))
    codes = jnp.where(chosen, dot(earlier, as_bf16(chosen)), -1.0)
    gy_out_ref[:, :D] = gy_ref[...]
    gy_out_ref[:, D:] = jnp.concatenate([codes, jnp.zeros((TOK, 128 - EXPERTS), f32)], axis=1).astype(bf16)


def with_codes(routes, gy):
    return call(
        codes_kernel, "codes", 50_000_000, 1_500_000, in_specs=[VECTOR] * 2, out_shape=shape(TOK, D + 128)
    )(routes, gy)


def pack_kernel(
    place_ref, query_ref, key_ref, value_ref, router_ref, one_ref, two_ref, gate_ref, up_ref,
    packed_ref, keep_ref, send_ref,
):
    core = place_ref[1]
    lane = iota((8, 128), 1)
    small = jnp.concatenate([router_ref[...].astype(f32), jnp.zeros((8, 96), f32)], axis=1)
    small = jnp.where(lane == 32, column_of(one_ref[...].astype(f32)), small)
    small = jnp.where(lane == 33, column_of(two_ref[...].astype(f32)), small).astype(bf16)
    for s in range(4):
        part = jnp.concatenate(
            [
                query_ref[:, 256 * s : 256 * s + 256],
                key_ref[:, 128 * s : 128 * s + 128],
                value_ref[:, 128 * s : 128 * s + 128],
                small,
            ],
            axis=1,
        )
        for f in range(32):
            packed_ref[32 * s + f] = part
    for i, ref in enumerate((gate_ref, up_ref)):
        for j in range(2):
            keep_ref[i, :, 128 * j : 128 * j + 128] = ref[:, pl.ds(256 * j + 128 * core, 128)]
            send_ref[i, :, 128 * j : 128 * j + 128] = ref[:, pl.ds(256 * j + 128 * (1 - core), 128)]


def pack(place, *args):
    return call(
        pack_kernel, "pack", 100_000_000, 4_000_000,
        in_specs=[SCALAR] + [VECTOR] * len(args),
        out_shape=(shape(128, 8, 640), shape(2, TOK, HALF), shape(2, TOK, HALF)),
    )(place, *args)


def assemble_kernel(place_ref, keep_ref, got_ref, down_ref, out_ref):
    core = place_ref[1]
    for i in range(2):
        out_ref[pl.ds(512 * i + 256 * core, 256)] = keep_ref[i]
        out_ref[pl.ds(512 * i + 256 * (1 - core), 256)] = got_ref[i]
    for j in range(4):
        out_ref[1024 + 128 * j : 1152 + 128 * j] = down_ref[:, 256 * j : 256 * j + 256]


def assemble(place, keep, got, down):
    return call(
        assemble_kernel, "assemble", 1_000_000, 2_000_000,
        in_specs=[SCALAR] + [VECTOR] * 3, out_shape=shape(1536, 256),
    )(place, keep, got, down)


def head_lanes_rope(head):
    lane = iota((1, 256), 1) % 128
    return (lane >= 32 * head) & (lane < 32 * head + 32)


def head_lanes(head):
    lane = iota((1, 256), 1)
    return (lane >= 64 * head) & (lane < 64 * head + 64)


def spread_queries():
    row, col = iota((256, 256), 0), iota((256, 256), 1)
    return row == ((col % 128) // 32) * 64 + (col // 128) * 32 + col % 32


def spread_keys():
    row, col = iota((128, 256), 0), iota((128, 256), 1)
    return row == ((col % 128) // 64) * 64 + (col // 128) * 32 + col % 32, (col % 64) < 32


def spread_values():
    row, col = iota((128, 256), 0), iota((128, 256), 1)
    return row == (col // 128) * 64 + col % 64, (col % 128) < 64


def positions(place_ref):
    ylo, core = place_ref[0], place_ref[1]
    return [(y, c, 2 * y + c) for c in (core, 1 - core) for y in (ylo, 1 - ylo)]


def normed(x):
    return x * lax.rsqrt(jnp.mean(x * x, axis=-1, keepdims=True) + epsilon)


def front_kernel(
    place_ref, x0_ref, x1_ref, x2_ref, x3_ref, w_ref, cos_ref, sin_ref,
    q_ref, k_ref, v_ref, o0_ref, o1_ref, o2_ref, o3_ref, lse_ref, h_ref, gains_ref, o_ref,
):
    gain = row_of(w_ref[:, 512:640].astype(f32)[:, 32:33])
    gains_ref[0:1] = gain
    gains_ref[1:2] = row_of(w_ref[:, 512:640].astype(f32)[:, 33:34])
    wq = dot(w_ref[:, :256], as_bf16(spread_queries())).astype(bf16)
    wk = dot(w_ref[:, 256:384], as_bf16(spread_keys()[0])).astype(bf16)
    wv = dot(w_ref[:, 384:512], as_bf16(spread_values()[0])).astype(bf16)
    for (_, _, at), x_ref in zip(positions(place_ref), (x0_ref, x1_ref, x2_ref, x3_ref)):
        rows = pl.ds(pl.multiple_of(256 * at, 256), 256)
        h = (normed(x_ref[...].astype(f32)) * gain).astype(bf16)
        h_ref[rows] = h
        c, s = cos_ref[rows], sin_ref[rows]
        for w, out in ((wq, q_ref), (wk, k_ref)):
            pre = dot(h, w)
            a, b = pre[:, :128], pre[:, 128:]
            out[rows] = jnp.concatenate([a * c - b * s, b * c + a * s], axis=1).astype(bf16)
        v_ref[rows] = dot(h, wv).astype(bf16)
    for i in range(4):
        rows = slice(256 * i, 256 * i + 256)
        n = 256 * (i + 1)
        seen = iota((256, n), 1) <= iota((256, n), 0) + 256 * i
        mixed = jnp.zeros((256, 256), f32)
        logs = jnp.zeros((256, 128), f32)
        for head in range(GROUP):
            q = q_ref[rows] * as_bf16(head_lanes_rope(head))
            scores = jnp.where(seen, dot(q, k_ref[:n], NT) * HEAD**-0.5, -1e30)
            peak = jnp.max(scores, axis=-1, keepdims=True)
            e = jnp.exp(scores - peak)
            total = jnp.sum(e, axis=-1, keepdims=True)
            probs = (e * (1.0 / total)).astype(bf16)
            mixed = mixed + dot(probs, v_ref[:n] * as_bf16(head_lanes(head)))
            logs = jnp.where(iota((256, 128), 1) == head, peak + jnp.log(total), logs)
        o_ref[i] = mixed.astype(bf16)
        lse_ref[rows] = logs
    for (_, _, at), out in zip(positions(place_ref), (o0_ref, o1_ref, o2_ref, o3_ref)):
        out[...] = o_ref[at]


def front(place, blocks, w, cos, sin):
    return call(
        front_kernel, "front", 8_000_000_000, 10_000_000,
        in_specs=[SCALAR] + [VECTOR] * 7,
        out_shape=(
            shape(LENGTH, 256), shape(LENGTH, 256), shape(LENGTH, 256), *[shape(TOK, 256)] * 4,
            shape(LENGTH, 128, dtype=f32), shape(LENGTH, D), shape(8, D, dtype=f32),
        ),
        scratch_shapes=[pltpu.VMEM((4, TOK, 256), bf16)],
    )(place, *blocks, w, cos, sin)


def output_blocks(own_ref, other_ref):
    return [ref[:, D * i : D * i + D] for ref in (own_ref, other_ref) for i in range(2)]


def mid_kernel(x_ref, m0_ref, m1_ref, m2_ref, m3_ref, own_ref, other_ref, gains_ref, residual_ref, h_ref):
    total = x_ref[...].astype(f32)
    for mixed_ref, w in zip((m0_ref, m1_ref, m2_ref, m3_ref), output_blocks(own_ref, other_ref)):
        total = total + dot(mixed_ref[...], w)
    residual_ref[...] = total
    h_ref[...] = (normed(total) * gains_ref[1:2]).astype(bf16)


def mid(x, mixed, own, other, gains):
    return call(
        mid_kernel, "mid", 1_000_000_000, 5_000_000,
        in_specs=[VECTOR] * 8,
        out_shape=(shape(TOK, D, dtype=f32), shape(TOK, D)),
    )(x, *mixed, own, other, gains)


def turn_kernel(
    place_ref, part0_ref, part1_ref, part2_ref, part3_ref, gy_ref, residual_ref, small_ref, gains_ref,
    m0_ref, m1_ref, m2_ref, m3_ref, own_ref, other_ref,
    do0_ref, do1_ref, do2_ref, do3_ref, grad_ref, keep_ref, send_ref, sums_ref,
):
    parts = (part0_ref, part1_ref, part2_ref, part3_ref)
    summed = sum(part[...].astype(f32) for part in parts)
    residual = residual_ref[...]
    factor = lax.rsqrt(jnp.mean(residual * residual, axis=-1, keepdims=True) + epsilon)
    normal = residual * factor
    gain = gains_ref[1:2]
    h = (normal * gain).astype(bf16)
    router = small_ref[:, 512 : 512 + EXPERTS]
    table = gate_table(dot(h, router), gy_ref[:, D:].astype(f32)[:, :EXPERTS])
    dgates = summed[:, D : D + EXPERTS]
    dlogits = (table * (dgates - jnp.sum(table * dgates, axis=-1, keepdims=True))).astype(bf16)
    dh = summed[:, :D] + dot(dlogits, router, NT)
    grad_gain = column_of(jnp.sum(dh * normal, axis=0, keepdims=True))
    grad_router = dot(h, dlogits, TN)
    sums = jnp.concatenate([grad_router, jnp.zeros((D, 128 - EXPERTS), f32)], axis=1)
    sums_ref[...] = jnp.where(iota((D, 128), 1) == 33, grad_gain, sums)
    scaled = dh * gain
    grad = gy_ref[:, :D].astype(f32) + factor * (scaled - normal * jnp.mean(scaled * normal, axis=-1, keepdims=True))
    grad_ref[...] = grad
    dz = grad.astype(bf16)
    mixed_refs, do_refs = (m0_ref, m1_ref, m2_ref, m3_ref), (do0_ref, do1_ref, do2_ref, do3_ref)
    for i, ((y, _, _), w) in enumerate(zip(positions(place_ref), output_blocks(own_ref, other_ref))):
        do_refs[i][...] = dot(dz, w, NT).astype(bf16)
        out = keep_ref if i < 2 else send_ref
        out[y] = dot(mixed_refs[i][...], dz, TN).astype(bf16)


def turn_back(place, parts, gy, residual, small, gains, mixed, own, other):
    pair = shape(2, TOK, D)
    return call(
        turn_kernel, "turn", 2_000_000_000, 10_000_000,
        in_specs=[SCALAR] + [VECTOR] * 14,
        out_shape=(*[shape(TOK, 256)] * 4, shape(TOK, D, dtype=f32), pair, pair, shape(D, 128, dtype=f32)),
    )(place, *parts, gy, residual, small, gains, *mixed, own, other)


def back_kernel(
    place_ref, q_ref, k_ref, v_ref, do0_ref, do1_ref, do2_ref, do3_ref, lse_ref, cos_ref, sin_ref, w_ref,
    x0_ref, x1_ref, x2_ref, x3_ref, out_ref, keep_ref, send_ref, gain_ref, do_ref, dk_ref, dv_ref,
):
    for (_, _, at), ref in zip(positions(place_ref), (do0_ref, do1_ref, do2_ref, do3_ref)):
        do_ref[at] = ref[...]
    dk_ref[...] = jnp.zeros_like(dk_ref)
    dv_ref[...] = jnp.zeros_like(dv_ref)
    scale = HEAD**-0.5
    place_queries = as_bf16(spread_queries())
    for i in range(4):
        rows = slice(256 * i, 256 * i + 256)
        n = 256 * (i + 1)
        seen = iota((256, n), 1) <= iota((256, n), 0) + 256 * i
        dq = jnp.zeros((256, 256), f32)
        for head in range(GROUP):
            lanes = head_lanes_rope(head)
            q = q_ref[rows] * as_bf16(lanes)
            do = do_ref[i] * as_bf16(head_lanes(head))
            scores = dot(q, k_ref[:n], NT) * scale - lse_ref[rows, head : head + 1]
            probs = jnp.where(seen, jnp.exp(jnp.where(seen, scores, 0.0)), 0.0)
            dprobs = dot(do, v_ref[:n], NT)
            row_dot = jnp.sum(probs * dprobs, axis=-1, keepdims=True)
            ds = (probs * (dprobs - row_dot)).astype(bf16)
            dq = dq + jnp.where(lanes, dot(ds, k_ref[:n]), 0.0)
            dk_ref[:n] += dot(ds, q, TN)
            dv_ref[:n] += dot(probs.astype(bf16), do, TN)
        c, s = cos_ref[rows], sin_ref[rows]
        a, b = dq[:, :128] * scale, dq[:, 128:] * scale
        dq = jnp.concatenate([a * c + b * s, b * c - a * s], axis=1).astype(bf16)
        out_ref[rows, :256] = dot(dq, place_queries, NT).astype(bf16)
    keep_keys, first_key = spread_keys()
    keep_values, first_value = spread_values()
    pick_keys = as_bf16(keep_keys & first_key)
    pick_values = as_bf16(keep_values & first_value)
    for i in range(4):
        rows = slice(256 * i, 256 * i + 256)
        c, s = cos_ref[rows], sin_ref[rows]
        a, b = dk_ref[rows, :128] * scale, dk_ref[rows, 128:] * scale
        a, b = a * c + b * s, b * c - a * s
        a, b = a + pltpu.roll(a, 96, 1), b + pltpu.roll(b, 96, 1)
        out_ref[rows, 256:384] = dot(jnp.concatenate([a, b], axis=1).astype(bf16), pick_keys, NT).astype(bf16)
        a, b = dv_ref[rows, :128], dv_ref[rows, 128:]
        a, b = a + pltpu.roll(a, 64, 1), b + pltpu.roll(b, 64, 1)
        out_ref[rows, 384:512] = dot(jnp.concatenate([a, b], axis=1).astype(bf16), pick_values, NT).astype(bf16)
    w = w_ref[:, :512]
    grad_gain = jnp.zeros((1, D), f32)
    for i, ((y, _, at), x_ref) in enumerate(zip(positions(place_ref), (x0_ref, x1_ref, x2_ref, x3_ref))):
        partial = dot(out_ref[pl.ds(pl.multiple_of(256 * at, 256), 256)], w, NT)
        grad_gain = grad_gain + jnp.sum(partial * normed(x_ref[...].astype(f32)), axis=0, keepdims=True)
        out = keep_ref if i < 2 else send_ref
        out[y] = partial.astype(bf16)
    gain_ref[...] = jnp.broadcast_to(grad_gain, (8, D))


def back(place, q, k, v, do, lse, cos, sin, w, blocks):
    pair = shape(2, TOK, D)
    return call(
        back_kernel, "back", 20_000_000_000, 16_000_000,
        in_specs=[SCALAR] + [VECTOR] * 15,
        out_shape=(shape(LENGTH, 512), pair, pair, shape(8, D, dtype=f32)),
        scratch_shapes=[
            pltpu.VMEM((4, TOK, 256), bf16), pltpu.VMEM((LENGTH, 256), f32), pltpu.VMEM((LENGTH, 256), f32),
        ],
    )(place, q, k, v, *do, lse, cos, sin, w, *blocks)


def projections_kernel(h_ref, dqkv_ref, sums_ref, gain_ref, first_ref):
    first_ref[:, :512] = dot(h_ref[...], dqkv_ref[...], TN).astype(bf16)
    small = jnp.where(iota((D, 128), 1) == 32, column_of(gain_ref[0:1]), sums_ref[...])
    first_ref[:, 512:] = small.astype(bf16)


def projections(h, dqkv, sums, gain):
    return call(
        projections_kernel, "projections", 1_500_000_000, 5_000_000, in_specs=[VECTOR] * 4, out_shape=shape(D, 640)
    )(h, dqkv, sums, gain)


def own_slots(expert, slot, z):
    start = ((expert % 16) // 4 * 2 + expert // 16) * CAP
    own = (expert % 4 == z) & (slot >= start) & (slot < start + CAP)
    return own, jnp.where(own, slot - start, 0)


def slot_tables(z, spread, start):
    own, place = own_slots(iota((EXPERTS, SLOTS), 0), iota((EXPERTS, SLOTS), 1), z)
    spread[...] = as_bf16(own)
    start[...] = jnp.sum(place, axis=0, keepdims=True).astype(f32)


SLOT_TABLES = [pltpu.VMEM((EXPERTS, SLOTS), bf16), pltpu.VMEM((1, SLOTS), f32)]


def gate_table(logits, codes):
    routed = codes >= 0
    logits = jnp.where(routed, logits, -1e30)
    e = jnp.where(routed, jnp.exp(logits - jnp.max(logits, axis=-1, keepdims=True)), 0.0)
    return e / jnp.sum(e, axis=-1, keepdims=True)


def split(values):
    high = values.astype(bf16)
    return high, (values - high.astype(f32)).astype(bf16)


def whole(*shape):
    return pl.BlockSpec(shape, lambda e: (0,) * len(shape))


def per_expert(*shape):
    return pl.BlockSpec((1,) + shape, lambda e: (e,) + (0,) * len(shape))


def rows_kernel(n, with_gates, z_ref, *refs):
    i = pl.program_id(0)
    z = z_ref[0]
    values_refs, refs = refs[:n], refs[n:]
    if with_gates:
        codes_refs, router_ref, refs = refs[:n], refs[n], refs[n + 1 :]
        rows_ref, gates_ref, turn_ref, values, codes, own, start = refs[-7:]
    else:
        rows_ref, turn_ref, values, codes, own, start = refs[-6:]
    for b in range(n):

        @pl.when(i == b)
        def _():
            values[...] = values_refs[b][:, :D]
            codes[...] = codes_refs[b][...] if with_gates else values_refs[b][:, D:]

    @pl.when(i == 0)
    def _():
        turn_ref[...] = jnp.zeros_like(turn_ref)
        mine, offset = own_slots(iota((SLOTS, EXPERTS), 1), iota((SLOTS, EXPERTS), 0), z)
        own[...] = as_bf16(mine)
        start[...] = jnp.sum(offset, axis=1, keepdims=True).astype(f32)

    slots = codes[:, :EXPERTS]
    place = as_bf16(dot(own[...], slots, NT) == start[...])
    rows_ref[:, 0] = dot(place, values[...]).astype(bf16).reshape(SHARE, CAP, D)
    if with_gates:
        table = gate_table(dot(values[...], router_ref[:, :EXPERTS]), slots.astype(f32))
        high, low = split(table)
        both = dot(place, high) + dot(place, low)
        gate = jnp.sum(both * own[...].astype(f32), axis=1, keepdims=True)
        gates_ref[:, 0] = gate.reshape(SHARE, CAP, 1)


def rows_of(z, first, blocks, codes, router, kept, turn):
    n, with_gates = len(blocks), router is not None
    args, specs = [z, *blocks], [SCALAR] + [whole(TOK, blocks[0].shape[1])] * n
    if with_gates:
        args += [*codes, router]
        specs += [pl.BlockSpec((TOK, 128), lambda e: (0, D // 128))] * n + [pl.BlockSpec((D, 128), lambda e: (0, 4))]
    args.append(turn)
    specs.append(ANYWHERE)
    widths = [(D, bf16)] + ([(1, f32)] if with_gates else [])
    out_specs = [pl.BlockSpec((SHARE, 1, CAP, w), lambda e: (0, first + e, 0, 0)) for w, _ in widths]
    out_shape = [shape(SHARE, BLOCKS, CAP, w, dtype=t) for w, t in widths]
    out_specs.append(whole(8, 128))
    out_shape.append(shape(8, 128, dtype=f32))
    aliases = {}
    if kept is not None:
        aliases = {len(args) + i: i for i in range(len(kept))}
        args += kept
        specs += [ANYWHERE] * len(kept)
    *kept, turn = call(
        functools.partial(rows_kernel, n, with_gates), "rows", n * 750_000_000, n * 2_000_000,
        grid=(n,), in_specs=specs, out_specs=out_specs, out_shape=out_shape, input_output_aliases=aliases,
        scratch_shapes=[
            pltpu.VMEM((TOK, D), bf16), pltpu.VMEM((TOK, 128), bf16), pltpu.VMEM((SLOTS, EXPERTS), bf16),
            pltpu.VMEM((SLOTS, 1), f32),
        ],
    )(*args)
    return kept, turn


def down_of(parts):
    return jnp.concatenate(
        [
            jnp.concatenate([parts[0, 128 * j : 128 * j + 128], parts[1, 128 * j : 128 * j + 128]], axis=0)
            for j in range(4)
        ],
        axis=1,
    )


def codes_specs():
    return [pl.BlockSpec((TOK, 128), lambda e: (0, D // 128))] * BLOCKS


PARTS = 2


def main_kernel(z_ref, x_ref, gy_ref, gate_ref, w_ref, *refs):
    codes_refs = refs[:8]
    act_ref, out_ref, own_ref, other_ref, kept, dgates, hidden, codes_kept, spread, start, mine = refs[8:]
    e = pl.program_id(0)

    @pl.when(e == 0)
    def _():
        for b in range(BLOCKS):
            codes_kept[b] = codes_refs[b][...]
        slot_tables(z_ref[0], spread, start)
        own, _ = own_slots(iota((SLOTS, EXPERTS), 1), iota((SLOTS, EXPERTS), 0), z_ref[0])
        mine[...] = own.astype(f32)

    down_w = down_of(w_ref[:, 1024:])
    gate_w = w_ref[:, :512].reshape(D, HALF)
    up_w = w_ref[:, 512:1024].reshape(D, HALF)
    both_w = jnp.concatenate([gate_w, up_w], axis=1)
    step = BLOCKS // PARTS
    for i in range(PARTS):
        blocks, rows = slice(step * i, step * i + step), slice(step * i * CAP, step * (i + 1) * CAP)
        x = x_ref[0, blocks].reshape(step * CAP, D)
        gate = gate_ref[0, blocks].reshape(step * CAP, 1)
        da = dot(gy_ref[0, blocks].reshape(step * CAP, D), down_w, NT)
        g = dot(x, gate_w)
        u = dot(x, up_w)
        s = jax.nn.sigmoid(g)
        silu = g * s
        act = silu * u
        dgates[blocks, e] = jnp.sum(act * da, axis=1, keepdims=True).reshape(step, CAP, 1)
        act_ref[0, rows] = (act * gate).astype(bf16)
        da = da * gate
        hidden[rows, :HALF] = (da * u * (s + silu * (1.0 - s))).astype(bf16)
        hidden[rows, HALF:] = (da * silu).astype(bf16)
        kept[blocks, e] = dot(hidden[rows], both_w, NT).astype(bf16).reshape(step, CAP, D)
    made = dot(hidden[...], x_ref[0].reshape(SLOTS, D), TN).astype(bf16)
    for i in range(2):
        out_ref[0, i, :512] = made[:, 512 * i : 512 * i + 512]
    made = dot(act_ref[0], gy_ref[0].reshape(SLOTS, D), TN).astype(bf16)
    for i in range(2):
        out_ref[0, i, 512:640] = made[128 * i : 128 * i + 128, :512]
        out_ref[0, i, 640:768] = made[128 * i : 128 * i + 128, 512:]

    @pl.when(e == SHARE - 1)
    def _():
        def pair(j, carry):
            for c, out in ((0, own_ref), (1, other_ref)):
                b = 2 * j + c
                place = as_bf16(dot(codes_kept[b][:, :EXPERTS], spread[...]) == start[...])
                out[j, :, :D] = dot(place, kept[b].reshape(SLOTS, D)).astype(bf16)
                high, low = split(mine[...] * dgates[b].reshape(SLOTS, 1))
                scattered = dot(place, high) + dot(place, low)
                out[j, :, D:] = jnp.concatenate([scattered, jnp.zeros((TOK, 128 - EXPERTS), f32)], axis=1).astype(bf16)
            return carry

        lax.fori_loop(0, 4, pair, 0)


def main(z, x, gy, gates, weights, codes):
    back = shape(4, TOK, D + 128)
    return call(
        main_kernel, "experts", 25_000_000_000, 60_000_000,
        grid=(SHARE,),
        in_specs=[
            SCALAR, per_expert(BLOCKS, CAP, D), per_expert(BLOCKS, CAP, D), per_expert(BLOCKS, CAP, 1),
            pl.BlockSpec((2, 1536, 256), lambda e: (e, 0, 0)), *codes_specs(),
        ],
        out_specs=[
            per_expert(SLOTS, HALF), per_expert(2, 768, 512), whole(4, TOK, D + 128), whole(4, TOK, D + 128),
        ],
        out_shape=[shape(SHARE, SLOTS, HALF), shape(SHARE, 2, 768, 512), back, back],
        scratch_shapes=[
            pltpu.VMEM((BLOCKS, SHARE, CAP, D), bf16),
            pltpu.VMEM((BLOCKS, SHARE, CAP, 1), f32),
            pltpu.VMEM((SLOTS, 2 * HALF), bf16),
            pltpu.VMEM((BLOCKS, TOK, 128), bf16),
            *SLOT_TABLES,
            pltpu.VMEM((SLOTS, EXPERTS), f32),
        ],
    )(z, x, gy, gates, weights, *codes)


def outs_kernel(z_ref, act_ref, w_ref, *refs):
    codes_refs = refs[:8]
    own_ref, other_ref, kept, codes_kept, spread, start = refs[8:]
    e = pl.program_id(0)
    kept[:, e] = dot(act_ref[0], down_of(w_ref[...])).astype(bf16).reshape(BLOCKS, CAP, D)

    @pl.when(e == 0)
    def _():
        for b in range(BLOCKS):
            codes_kept[b] = codes_refs[b][...]
        slot_tables(z_ref[0], spread, start)

    @pl.when(e == SHARE - 1)
    def _():
        def pair(j, carry):
            for c, out in ((0, own_ref), (1, other_ref)):
                b = 2 * j + c
                place = as_bf16(dot(codes_kept[b][:, :EXPERTS], spread[...]) == start[...])
                out[j] = dot(place, kept[b].reshape(SLOTS, D)).astype(bf16)
            return carry

        lax.fori_loop(0, 4, pair, 0)


def outs(z, act, weights, codes):
    back = jax.ShapeDtypeStruct((4, TOK, D), bf16)
    return call(
        outs_kernel, "expert_outs", 6_000_000_000, 12_000_000,
        grid=(SHARE,),
        in_specs=[
            SCALAR, per_expert(SLOTS, HALF), pl.BlockSpec((2, 512, 256), lambda e: (e, 2, 0)), *codes_specs(),
        ],
        out_specs=[whole(4, TOK, D)] * 2,
        out_shape=[back, back],
        scratch_shapes=[
            pltpu.VMEM((BLOCKS, SHARE, CAP, D), bf16), pltpu.VMEM((BLOCKS, TOK, 128), bf16), *SLOT_TABLES,
        ],
    )(z, act, weights, *codes)


def finish_kernel(place_ref, mine_ref, got_ref, gate_ref, up_ref, down_ref):
    core = place_ref[1]
    for i, out in enumerate((gate_ref, up_ref)):
        for j in range(2):
            rows = slice(256 * i + 128 * j, 256 * i + 128 * j + 128)
            keep = mine_ref[rows, pl.ds(pl.multiple_of(256 * core, 256), 256)].astype(f32)
            out[:, pl.ds(pl.multiple_of(256 * j + 128 * core, 128), 128)] = keep.T
            got = got_ref[rows].astype(f32)
            out[:, pl.ds(pl.multiple_of(256 * j + 128 * (1 - core), 128), 128)] = got.T
    for j in range(2):
        down_ref[:, 512 * j : 512 * j + 512] = mine_ref[512 + 128 * j : 640 + 128 * j].astype(f32)


def finish(place, mine, got):
    return call(
        finish_kernel, "finish", 1_000_000, 4_000_000,
        in_specs=[SCALAR, VECTOR, VECTOR],
        out_shape=(shape(TOK, FF, dtype=f32), shape(TOK, FF, dtype=f32), shape(128, D, dtype=f32)),
    )(place, mine, got)


def shift(values, axis, by):
    n = 4 if axis in ("x", "z") else 2
    return lax.ppermute(values, axis, [(i, (i + by) % n) for i in range(n)])


def swap(values, axis):
    return shift(values, axis, 1)


def gather_z(values):
    return [values, shift(values, "z", 1), shift(values, "z", -1), shift(values, "z", 2)]


def with_core(blocks):
    return [(block, swap(block, "core")) for block in blocks]


def exchange_seq(own, across, beside, both):
    return [own, swap(across, "ylo"), swap(beside, "core"), swap(swap(both, "ylo"), "core")]


def core_sums(own, other):
    got = swap(other, "core")
    return [(own[j].astype(f32) + got[j].astype(f32)).astype(bf16) for j in range(4)]


def scatter_z(sums):
    return [sums[0], shift(sums[1], "z", -1), shift(sums[2], "z", 1), shift(sums[3], "z", 2)]


def fence(*values):
    return lax.optimization_barrier(values)


def on_device(
    tokens, norm1_gain, query_weight, key_weight, value_weight, output_weight, norm2_gain, router_weight,
    expert_gate, expert_up, expert_down, routes, cotangent,
):
    ylo, core = lax.axis_index("ylo"), lax.axis_index("core")
    z = lax.axis_index("z").astype(jnp.int32).reshape(1)
    place = jnp.stack([ylo, core]).astype(jnp.int32)

    own = tokens.reshape(TOK, D)
    across = swap(own, "ylo")
    gy_own = with_codes(routes.reshape(TOK, TOPK), cotangent.reshape(TOK, D))
    gy_blocks = gather_z(gy_own)

    packed, keep, send = pack(
        place, query_weight, key_weight, value_weight, router_weight, norm1_gain.reshape(1, 8), norm2_gain.reshape(1, 8),
        expert_gate.reshape(TOK, FF), expert_up.reshape(TOK, FF),
    )

    arrived = lax.all_to_all(packed, AXES, split_axis=0, concat_axis=0, tiled=True).reshape(D, 640)
    beside = swap(own, "core")

    expert_w = assemble(place, keep, swap(send, "core"), expert_down.reshape(128, D))
    expert_w, arrived, across, beside = fence(expert_w, arrived, across, beside)
    expert_w = lax.all_gather(expert_w, PLANE, axis=0).reshape(16, 1536, 256)

    lane = jnp.arange(128) % 32
    angles = jnp.arange(LENGTH).astype(f32)[:, None] * (rope_base ** (-2.0 * lane.astype(f32) / HEAD))[None, :]
    cos, sin = fence(jnp.cos(angles), jnp.sin(angles))
    blocks = [own, across, beside, swap(across, "core")]
    q, k, v, *mixed, lse, hidden_all, gains = front(place, blocks, arrived, cos, sin)

    output_rows = jnp.concatenate([output_weight, swap(output_weight, "ylo")], axis=1)
    output_rows, _ = fence(output_rows, arrived)
    output_own = lax.all_to_all(
        jnp.broadcast_to(output_rows[None], (32, 8, 2 * D)), FSDP, split_axis=0, concat_axis=0, tiled=True
    ).reshape(TOK, 2 * D)

    mixed = exchange_seq(*mixed)
    output_own, *rest = fence(output_own, *mixed, *gy_blocks)
    mixed, gy_blocks = rest[:4], rest[4:]
    output_other = swap(output_own, "core")
    gy_blocks = [block for pair in with_core(gy_blocks) for block in pair]
    residual, hidden_two = mid(own, mixed, output_own, output_other, gains)

    h_blocks = gather_z(hidden_two)
    turn, _ = fence(jnp.zeros((8, 128), f32), hidden_two)
    gy_rows, turn = rows_of(z, 0, gy_blocks, None, None, None, turn)
    rows, turn = rows_of(z, 0, (hidden_two, swap(hidden_two, "core")), gy_blocks[:2], arrived, None, turn)
    *h_blocks, turn = fence(*h_blocks, turn)
    h_blocks = [block for pair in with_core(h_blocks[1:]) for block in pair]
    rows, turn = rows_of(z, 2, h_blocks, gy_blocks[2:], arrived, rows, turn)
    (gy_rows,), (rows, gate_rows) = gy_rows, rows

    act, expert_grads, back_own, back_other = main(z, rows, gy_rows, gate_rows, expert_w, gy_blocks)
    sums = core_sums(back_own, back_other)
    parts = scatter_z(sums)
    moe_act, *_ = fence(act, *sums)
    moe_own, moe_other = outs(z, moe_act, expert_w, gy_blocks)
    expert_grads = lax.psum_scatter(expert_grads.reshape(16 * 768, 512), PLANE, scatter_dimension=0, tiled=True)

    moe_sums = core_sums(moe_own, moe_other)
    *do, grad_residual, keep, send, small = turn_back(
        place, parts, gy_own, residual, arrived, gains, mixed, output_own, output_other
    )

    do = exchange_seq(*do)
    grad_output_sum = (keep.astype(f32) + swap(send, "core").astype(f32)).astype(bf16).reshape(64, 8, D)
    grad_output_sum, *rest = fence(grad_output_sum, *moe_sums, *do)
    moe_sums, do = rest[:4], rest[4:]
    moe_near = [shift(moe_sums[1], "z", -1), shift(moe_sums[2], "z", 1)]
    grad_output = lax.all_to_all(grad_output_sum, ("ylo",) + FSDP, split_axis=0, concat_axis=0, tiled=True)
    dqkv, keep, send, gain = back(place, q, k, v, do, lse, cos, sin, arrived, blocks)
    dqkv, keep, send, own, grad_output, *moe_near = fence(dqkv, keep, send, own, grad_output, *moe_near)
    first = projections(hidden_all, dqkv, small, gain)

    away = jnp.where(core == 0, expert_grads[:512, 256:], expert_grads[:512, :256])
    finished = finish(place, expert_grads, swap(away, "core"))

    pair = (keep.astype(f32) + swap(send, "core").astype(f32)).astype(bf16)
    kept = jnp.where(ylo == 0, pair[0], pair[1])
    got = swap(jnp.where(ylo == 0, pair[1], pair[0]), "ylo")
    got, moe_far, grad_gate, grad_up, grad_down = fence(got, shift(moe_sums[3], "z", 2), *finished)
    grad_hidden_one = kept.astype(f32) + got.astype(f32)
    first = lax.all_to_all(first.reshape(128, 8, 640), AXES, split_axis=0, concat_axis=0, tiled=True)
    grad_output = jnp.sum(grad_output.astype(f32), axis=0)
    layer_out = sum(part.astype(f32) for part in (moe_sums[0], *moe_near, moe_far))
    layer_out = (residual + layer_out).astype(bf16).reshape(1, TOK, D)
    first = jnp.sum(first.astype(f32).reshape(4, 32, 8, 640), axis=1)
    grad_query = first[:, :, :256].transpose(1, 0, 2).reshape(8, D)
    grad_key = first[:, :, 256:384].transpose(1, 0, 2).reshape(8, 512)
    grad_value = first[:, :, 384:512].transpose(1, 0, 2).reshape(8, 512)
    small = jnp.sum(first[:, :, 512:], axis=0)

    inputs = own.astype(f32)
    factor_one = lax.rsqrt(jnp.mean(inputs * inputs, axis=-1, keepdims=True) + epsilon)
    normed_one = inputs * factor_one
    scaled = grad_hidden_one * gains[0:1]
    grad_inputs = grad_residual + factor_one * (
        scaled - normed_one * jnp.mean(scaled * normed_one, axis=-1, keepdims=True)
    )

    return (
        layer_out, grad_inputs.reshape(1, TOK, D), small[:, 32], grad_query, grad_key, grad_value, grad_output,
        small[:, 33], small[:, :EXPERTS], grad_gate.reshape(1, TOK, FF), grad_up.reshape(1, TOK, FF),
        grad_down.reshape(1, 128, D),
    )


def solution(mesh):
    fine = Mesh(mesh.devices.reshape(2, 2, 2, 4, 4), AXES)
    tok = P(FSDP, SEQ, None)
    row = P(AXES, None)
    vec = P(AXES)
    in_specs = (tok, vec, row, row, row, row, vec, row, tok, tok, tok, tok, tok)
    out_specs = (tok, tok, vec, row, row, row, row, vec, row, tok, tok, tok)
    return jax.shard_map(on_device, mesh=fine, in_specs=in_specs, out_specs=out_specs, check_vma=False)
```

time: 522 us -> 346 us (0.66)
  the two profiles are of different devices: /device:TPU:1 before, /device:TPU:79 now
where the time goes in v2:
time: 346 us; the launch traced here: 341 us
  Pallas kernels  142 us (41%)
  starting transfers between devices  85.7 us (25%)
  waiting for transfers between devices  68.8 us (20%)
  other arithmetic  20 us (6%)
  between operations  14.6 us (4%)
  local copies, waits for them, and re-layouts  9.82 us (3%)
    ppermute x40, waiting for transfers between devices, shift(): return lax.ppermute(values, axis, [(i, (i + by) % n) for i in range(n)])  52.3 us
    ppermute x40, starting transfers between devices, shift(): return lax.ppermute(values, axis, [(i, (i + by) % n) for i in range(n)])  45.5 us
    pallas_call x1, Pallas kernels, main(): call(main_kernel, 'experts', 25000000000, 60000000, grid=(SHARE,), in_spe...  41.7 us
    pallas_call x3, Pallas kernels, rows_of(): call(functools.partial(rows_kernel, n, with_gates), 'rows', n * 750000000...  30.3 us
    pallas_call x1, Pallas kernels, back(): call(back_kernel, 'back', 20000000000, 16000000, in_specs=[SCALAR] + [VEC...  16.6 us
    pallas_call x1, Pallas kernels, outs(): call(outs_kernel, 'expert_outs', 6000000000, 12000000, grid=(SHARE,), in_...  14.7 us
    all_to_all x1, waiting for transfers between devices, on_device(): lax.all_to_all(first.reshape(128, 8, 640), AXES, split_axis=0, concat_axi...  12.2 us
    pallas_call x1, Pallas kernels, front(): call(front_kernel, 'front', 8000000000, 10000000, in_specs=[SCALAR] + [VE...  12 us
  transfers between devices with their start and end apart: 46, of which 16 were waited for; matrix products, arithmetic and copies ran while one was open for 6% of the time, Pallas kernels for 29%

profile of v2, /device:TPU:79, one launch (start us, length us, event | category | flops | bytes accessed | tf_op | source)
XLA Modules:
  0.0 340.9 jit_solution(13489360283868084953)
XLA Ops:
  10.2 10.3 %all-to-all-start = ((bf16[128,8,640]{2,1,0:T(8,128)(2,1)}), bf16[128,8,640]{2,1,0:T(8,128)(2,1)S(1)}, u32[]{:S(2)}, u32[]{:S(2)}) async-start(bf16[128,8,640]{2,1,0:T(8,128)(2,1)} %get-tuple-element.100), calls=%async_computation | async-start | bytes 2621440 | tf_op jit(solution)/shard_map/all_to_all | solution.py:694
  26.2 20.1 %collective-permute-done.2.x1_ref = bf16[256,1024]{1,0:T(8,128)(2,1)S(1)} collective-permute-done((bf16[256,1024]{1,0:T(8,128)(2,1)S(1)}, bf16[256,1024]{1,0:T(8,128)(2,1)S(1)}, u32[]{:S(2)}, u32[]{:S(2)}) %collective-permute-start.2) | collective-permute-done | bytes 524320 | tf_op jit(solution)/shard_map/ppermute | solution.py:644
  47.3 2.5 codes.1.refs_0_.refs_2_.gy_ref
  49.8 3.0 collective-permute-start.11
  56.9 8.6 %all-to-all-start.1 = ((bf16[32,8,2048]{2,1,0:T(8,128)(2,1)}), bf16[32,8,2048]{2,1,0:T(8,128)(2,1)S(1)}, u32[]{:S(2)}, u32[]{:S(2)}) async-start(bf16[32,8,2048]{2,1,0:T(8,128)(2,1)} %broadcast_in_dim.4), calls=%async_computation.1 | async-start | bytes 2097152 | tf_op jit(solution)/shard_map/all_to_all | solution.py:709
  66.0 3.1 multiply_sine_fusion
  69.1 12.0 %front.1 = (bf16[1024,256]{1,0:T(8,128)(2,1)}, bf16[1024,256]{1,0:T(8,128)(2,1)}, bf16[1024,256]{1,0:T(8,128)(2,1)}, bf16[256,256]{1,0:T(8,128)(2,1)}, bf16[256,...) custom-call(s32[2]{0:T(128)} %pad_add_fusion.place_ref, ...), custom_call_target="tpu_custom_call" | custom-call | flops 8000000000 | bytes 10000000 | tf_op jit(solution)/shard_map/front/pallas_call | solution.py:234
  82.9 3.0 collective-permute-start.6
  87.9 2.6 collective-permute-start.8
  95.6 4.8 %mid.1 = (f32[256,1024]{1,0:T(8,128)}, bf16[256,1024]{1,0:T(8,128)(2,1)}) custom-call(bf16[256,1024]{1,0:T(8,128)(2,1)} %bitcast.69, bf16[256,256]{1,0:T(8,128)(2,1)} %get-tuple-element.111.m0_ref, bf16[256,256]{1,0:T(8,128)(2,1)} %copy-done.29, bf16[256,256]{1,0:T(8,128)(2,1)} %copy-done.30, bf16[256,256]{1,0:T(8,128)(2,1)} %copy-done.31, ...), custom_call_target="tpu_custom_call" | custom-call | flops 1000000000 | bytes 5000000 | tf_op jit(solution)/shard_map/mid/pallas_call | solution.py:258
  102.4 2.5 collective-permute-start.15
  105.5 10.5 %rows.3 = (bf16[8,8,80,1024]{3,2,1,0:T(8,128)(2,1)}, f32[8,128]{1,0:T(8,128)}) custom-call(s32[1]{0:T(128)} %bitcast.12.z_ref, bf16[256,1152]{1,0:T(8,128)(2,1)} %codes.1.refs_0_.refs_2_.gy_ref, bf16[256,1152]{1,0:T(8,128)(2,1)} %collective-permute-done.17.refs_1_.refs_3_, bf16[256,1152]{1,0:T(8,128)(2,1)} %collective-permute-done.9.refs_2_.refs_6_, ...), custom_call_target="tpu_custom_call" | custom-call | flops 6000000000 | bytes 16000000 | tf_op jit(solution)/shard_map/rows/pallas_call | solution.py:472
  116.8 6.0 %rows.4 = (bf16[8,8,80,1024]{3,2,1,0:T(8,128)(2,1)}, f32[8,8,80,1]{3,2,1,0:T(8,128)}, f32[8,128]{1,0:T(8,128)}) custom-call(s32[1]{0:T(128)} %bitcast.12.z_ref, bf16[256,1024]{1,0:T(8,128)(2,1)} %get-tuple-element.118.refs_0_, bf16[256,1024]{1,0:T(8,128)(2,1)} %copy-done.37, bf16[256,1152]{1,0:T(8,128)(2,1)} %codes.1.refs_0_.refs_2_.gy_ref, ...), custom_call_target="tpu_custom_call" | custom-call | flops 1500000000 | bytes 4000000 | tf_op jit(solution)/shard_map/rows/pallas_call | solution.py:472
  122.9 2.9 collective-permute-done.15.refs_4_
  130.7 13.7 %rows.5 = (bf16[8,8,80,1024]{3,2,1,0:T(8,128)(2,1)}, f32[8,8,80,1]{3,2,1,0:T(8,128)}, f32[8,128]{1,0:T(8,128)}) custom-call(s32[1]{0:T(128)} %bitcast.12.z_ref, bf16[256,1024]{1,0:T(8,128)(2,1)} %copy-done.21, bf16[256,1024]{1,0:T(8,128)(2,1)} %copy-done.24, bf16[256,1024]{1,0:T(8,128)(2,1)} %copy-done.22, ...), custom_call_target="tpu_custom_call", output_to_operand_aliasing={{0}: (15, {}), {1}: (16, {})} | custom-call | flops 4499999744 | bytes 12000000 | tf_op jit(solution)/shard_map/rows/pallas_call | solution.py:472
  144.4 4.3 %all-gather.3.cloned.1.call-done = bf16[24576,256]{1,0:T(8,128)(2,1)} async-done(((bf16[1536,256]{1,0:T(8,128)(2,1)}), bf16[24576,256]{1,0:T(8,128)(2,1)}) %all-gather.3.cloned.1.call-update) | async-done | bytes 12582928 | tf_op jit(solution)/shard_map/all_gather | solution.py:699
  148.7 41.7 %experts.1 = (bf16[8,640,256]{2,1,0:T(8,128)(2,1)}, bf16[8,2,768,512]{3,2,1,0:T(8,128)(2,1)}, bf16[4,256,1152]{2,1,0:T(8,128)(2,1)}, bf16[4,256,1152]{2,1,0:T(8,128)(2,1)}) custom-call(s32[1]{0:T(128)} %bitcast.12.z_ref, bf16[8,8,80,1024]{3,2,1,0:T(8,128)(2,1)} %get-tuple-element.132.x_ref, bf16[8,8,80,1024]{3,2,1,0:T(8,128)(2,1)} %get-tuple-element.133.gy_ref, ...), custom_call_target="tpu_custom_call" | custom-call | flops 24999999488 | bytes 60000000 | tf_op jit(solution)/shard_map/experts/pallas_call | solution.py:559
  191.4 4.4 %collective-permute-done.24 = bf16[4,256,1152]{2,1,0:T(8,128)(2,1)S(1)} collective-permute-done((bf16[4,256,1152]{2,1,0:T(8,128)(2,1)}, bf16[4,256,1152]{2,1,0:T(8,128)(2,1)S(1)}, u32[]{:S(2)}, u32[]{:S(2)}) %collective-permute-start.24) | collective-permute-done | bytes 2359328 | tf_op jit(solution)/shard_map/ppermute | solution.py:644
  200.0 14.7 %expert_outs.1 = (bf16[4,256,1024]{2,1,0:T(8,128)(2,1)}, bf16[4,256,1024]{2,1,0:T(8,128)(2,1)}) custom-call(s32[1]{0:T(128)} %bitcast.12.z_ref, bf16[8,640,256]{2,1,0:T(8,128)(2,1)} %get-tuple-element.141.act_ref, bf16[16,1536,256]{2,1,0:T(8,128)(2,1)} %bitcast.92, bf16[256,1152]{1,0:T(8,128)(2,1)} %codes.1.refs_0_.refs_2_.gy_ref, ...), custom_call_target="tpu_custom_call" | custom-call | flops 6000000000 | bytes 12000000 | tf_op jit(solution)/shard_map/expert_outs/pallas_call | solution.py:607
  216.0 9.8 %collective-permute-done.27.part3_ref = bf16[256,1152]{1,0:T(8,128)(2,1)S(1)} collective-permute-done((bf16[256,1152]{1,0:T(8,128)(2,1)S(1)}, bf16[256,1152]{1,0:T(8,128)(2,1)S(1)}, u32[]{:S(2)}, u32[]{:S(2)}) %collective-permute-start.27) | collective-permute-done | bytes 589856 | tf_op jit(solution)/shard_map/ppermute | solution.py:644
  226.7 7.8 %turn.1 = (bf16[256,256]{1,0:T(8,128)(2,1)}, bf16[256,256]{1,0:T(8,128)(2,1)}, bf16[256,256]{1,0:T(8,128)(2,1)}, bf16[256,256]{1,0:T(8,128)(2,1)}, f32[256,1024]...) custom-call(s32[2]{0:T(128)} %pad_add_fusion.place_ref, ...), custom_call_target="tpu_custom_call" | custom-call | flops 2000000000 | bytes 10000000 | tf_op jit(solution)/shard_map/turn/pallas_call | solution.py:299
  237.7 6.2 %collective-permute-done.32 = bf16[256,256]{1,0:T(8,128)(2,1)S(1)} collective-permute-done((bf16[256,256]{1,0:T(8,128)(2,1)}, bf16[256,256]{1,0:T(8,128)(2,1)S(1)}, u32[]{:S(2)}, u32[]{:S(2)}) %collective-permute-start.32) | collective-permute-done | bytes 131104 | tf_op jit(solution)/shard_map/ppermute | solution.py:644
  245.0 2.6 add_convert_fusion.1
  251.2 11.5 %all-to-all-start.2 = ((bf16[64,8,1024]{2,1,0:T(8,128)(2,1)}), bf16[64,8,1024]{2,1,0:T(8,128)(2,1)S(1)}, u32[]{:S(2)}, u32[]{:S(2)}) async-start(bf16[64,8,1024]{2,1,0:T(8,128)(2,1)} %bitcast.18), calls=%async_computation.2 | async-start | bytes 2097152 | tf_op jit(solution)/shard_map/all_to_all | solution.py:746
  262.7 16.6 %back.1 = (bf16[1024,512]{1,0:T(8,128)(2,1)}, bf16[2,256,1024]{2,1,0:T(8,128)(2,1)}, bf16[2,256,1024]{2,1,0:T(8,128)(2,1)}, f32[8,1024]{1,0:T(8,128)}) custom-call(s32[2]{0:T(128)} %pad_add_fusion.place_ref, bf16[1024,256]{1,0:T(8,128)(2,1)} %get-tuple-element.149.q_ref, bf16[1024,256]{1,0:T(8,128)(2,1)} %get-tuple-element.150.k_ref, ...), custom_call_target="tpu_custom_call" | custom-call | flops 20000000000 | bytes 16000000 | tf_op jit(solution)/shard_map/back/pallas_call | solution.py:363
  279.4 2.4 collective-permute-start.36
  281.8 4.5 %projections.1 = bf16[1024,640]{1,0:T(8,128)(2,1)} custom-call(bf16[1024,1024]{1,0:T(8,128)(2,1)} %get-tuple-element.176.h_ref, bf16[1024,512]{1,0:T(8,128)(2,1)} %get-tuple-element.177.dqkv_ref, f32[1024,128]{1,0:T(8,128)} %get-tuple-element.178.sums_ref, f32[8,1024]{1,0:T(8,128)} %get-tuple-element.179.gain_ref), custom_call_target="tpu_custom_call" | custom-call | flops 1500000000 | bytes 5000000 | tf_op jit(solution)/shard_map/projections/pallas_call | solution.py:380
  286.3 9.3 %all-to-all-start.3 = ((bf16[128,8,640]{2,1,0:T(8,128)(2,1)}), bf16[128,8,640]{2,1,0:T(8,128)(2,1)S(1)}, u32[]{:S(2)}, u32[]{:S(2)}) async-start(bf16[128,8,640]{2,1,0:T(8,128)(2,1)} %bitcast.79), calls=%async_computation.4 | async-start | bytes 2621440 | tf_op jit(solution)/shard_map/all_to_all | solution.py:759
  300.2 12.2 %all-to-all-done.3 = bf16[128,8,640]{2,1,0:T(8,128)(2,1)S(1)} async-done(((bf16[128,8,640]{2,1,0:T(8,128)(2,1)}), bf16[128,8,640]{2,1,0:T(8,128)(2,1)S(1)}, u32[]{:S(2)}, u32[]{:S(2)}) %all-to-all-start.3) | async-done | bytes 1310752 | tf_op jit(solution)/shard_map/all_to_all | solution.py:759
  314.4 10.0 %collective-permute-start.39 = (bf16[512,256]{1,0:T(8,128)(2,1)S(1)}, bf16[512,256]{1,0:T(8,128)(2,1)S(1)}, u32[]{:S(2)}, u32[]{:S(2)}) collective-permute-start(bf16[512,256]{1,0:T(8,128)(2,1)S(1)} %slice_select_fusion), channel_id=1, source_target_pairs={{0,32},{32,0},{1,33},{33,1},{2,34},{34,2},{3,35},{35,3},{4,36},{36... | collective-permute-start | bytes 786440 | tf_op jit(solution)/shard_map/ppermute | solution.py:644
  326.4 2.5 finish.1
  330.4 3.4 %fusion.6 = (f32[1,256,1024]{2,1,0:T(8,128)}, bf16[1,256,1024]{2,1,0:T(8,128)(2,1)}) fusion(f32[256,1024]{1,0:T(8,128)S(1)} %copy-done.9, bf16[256,1024]{1,0:T(8,128)(2,1)S(1)} %bitcast.75, bf16[256,1024]{1,0:T(8,128)(2,1)} %collective-permute-done.37, f32[256]{0:T(256)S(1)} %broadcast_multiply_fusion, f32[1024]{0:T(1024)S(1)} %bitcast.86, ...), kind=kLoop, calls=%fused_computation.16 | loop fusion | flops 5242880 | bytes 7870465 | tf_op jit(solution)/shard_map/reshape | solution.py:778
  (185 shorter events, 56.7 us)
Async XLA Ops:
  10.2 36.1 %all-to-all-start = ((bf16[128,8,640]{2,1,0:T(8,128)(2,1)}), bf16[128,8,640]{2,1,0:T(8,128)(2,1)S(1)}, u32[]{:S(2)}, u32[]{:S(2)}) async-start(bf16[128,8,640]{2,1,0:T(8,128)(2,1)} %get-tuple-element.100), calls=%async_computation | async-start | bytes 2621440 | tf_op jit(solution)/shard_map/all_to_all | solution.py:694
  20.5 128.2 %all-gather.3.cloned.1.call-start = ((), (), s32[]{:S(2)}) async-start(), calls=%async_computation.6 | async-start | bytes 13369344 | tf_op jit(solution)/shard_map/all_gather | solution.py:699
  20.6 25.7 %collective-permute-start.2 = (bf16[256,1024]{1,0:T(8,128)(2,1)S(1)}, bf16[256,1024]{1,0:T(8,128)(2,1)S(1)}, u32[]{:S(2)}, u32[]{:S(2)}) collective-permute-start(bf16[256,1024]{1,0:T(8,128)(2,1)S(1)} %bitcast.71), channel_id=1, source_target_pairs={{0,64},{64,0},{1,65},{65,1},{2,66},{66,2},{3,67},{67,3},{4,68},{68... | collective-permute-start | bytes 1572872 | tf_op jit(solution)/shard_map/ppermute | solution.py:644
  20.9 25.4 %collective-permute-start.3 = (bf16[256,1024]{1,0:T(8,128)(2,1)S(1)}, bf16[256,1024]{1,0:T(8,128)(2,1)S(1)}, u32[]{:S(2)}, u32[]{:S(2)}) collective-permute-start(bf16[256,1024]{1,0:T(8,128)(2,1)S(1)} %bitcast.72), channel_id=1, source_target_pairs={{0,32},{32,0},{1,33},{33,1},{2,34},{34,2},{3,35},{35,3},{4,36},{36... | collective-permute-start | bytes 1572872 | tf_op jit(solution)/shard_map/ppermute | solution.py:644
  49.8 33.1 %collective-permute-start.10 = (bf16[256,1152]{1,0:T(8,128)(2,1)}, bf16[256,1152]{1,0:T(8,128)(2,1)S(1)}, u32[]{:S(2)}, u32[]{:S(2)}) collective-permute-start(bf16[256,1152]{1,0:T(8,128)(2,1)} %codes.1.refs_0_.refs_2_.gy_ref), channel_id=1, source_target_pairs={{0,3},{1,0},{2,1},{3,2},{4,7},{5,4},{6,5},{7,6},{8,11},{9,8},{10,9... | collective-permute-start | bytes 1769480 | tf_op jit(solution)/shard_map/ppermute | solution.py:644
  49.8 40.7 %collective-permute-start.11 = (bf16[256,1152]{1,0:T(8,128)(2,1)}, bf16[256,1152]{1,0:T(8,128)(2,1)S(1)}, u32[]{:S(2)}, u32[]{:S(2)}) collective-permute-start(bf16[256,1152]{1,0:T(8,128)(2,1)} %codes.1.refs_0_.refs_2_.gy_ref), channel_id=1, source_target_pairs={{0,2},{1,3},{2,0},{3,1},{4,6},{5,7},{6,4},{7,5},{8,10},{9,11},{10,... | collective-permute-start | bytes 1769480 | tf_op jit(solution)/shard_map/ppermute | solution.py:644
  52.9 37.6 %collective-permute-start.9 = (bf16[256,1152]{1,0:T(8,128)(2,1)}, bf16[256,1152]{1,0:T(8,128)(2,1)}, u32[]{:S(2)}, u32[]{:S(2)}) collective-permute-start(bf16[256,1152]{1,0:T(8,128)(2,1)} %codes.1.refs_0_.refs_2_.gy_ref), channel_id=1, source_target_pairs={{0,1},{1,2},{2,3},{3,0},{4,5},{5,6},{6,7},{7,4},{8,9},{9,10},{10,1... | collective-permute-start | bytes 1769480 | tf_op jit(solution)/shard_map/ppermute | solution.py:644
  54.1 15.0 %collective-permute-start.4 = (bf16[256,1024]{1,0:T(8,128)(2,1)}, bf16[256,1024]{1,0:T(8,128)(2,1)}, u32[]{:S(2)}, u32[]{:S(2)}) collective-permute-start(bf16[256,1024]{1,0:T(8,128)(2,1)} %copy-done.35), channel_id=1, source_target_pairs={{0,32},{32,0},{1,33},{33,1},{2,34},{34,2},{3,35},{35,3},{4,36},{36... | collective-permute-start | bytes 1572872 | tf_op jit(solution)/shard_map/ppermute | solution.py:644
  56.9 34.6 %all-to-all-start.1 = ((bf16[32,8,2048]{2,1,0:T(8,128)(2,1)}), bf16[32,8,2048]{2,1,0:T(8,128)(2,1)S(1)}, u32[]{:S(2)}, u32[]{:S(2)}) async-start(bf16[32,8,2048]{2,1,0:T(8,128)(2,1)} %broadcast_in_dim.4), calls=%async_computation.1 | async-start | bytes 2097152 | tf_op jit(solution)/shard_map/all_to_all | solution.py:709
  65.5 247.7 %reduce-scatter.2.cloned.1.call-start = ((), (), s32[]{:S(2)}) async-start(), calls=%async_computation.5 | async-start | bytes 13369344 | tf_op jit(solution)/shard_map/reduce_scatter | solution.py:734
  92.9 9.1 %collective-permute-start.18 = (bf16[256,1152]{1,0:T(8,128)(2,1)}, bf16[256,1152]{1,0:T(8,128)(2,1)S(1)}, u32[]{:S(2)}, u32[]{:S(2)}) collective-permute-start(bf16[256,1152]{1,0:T(8,128)(2,1)} %collective-permute-done.9.refs_2_.refs_6_), channel_id=1, source_target_pairs={{0,32},{32,0},{1,33},{33,1},{2,34},{34,2},{3,35},{35,3},{4,36},{36... | collective-permute-start | bytes 1769480 | tf_op jit(solution)/shard_map/ppermute | solution.py:644
  92.9 9.5 %collective-permute-start.19 = (bf16[256,1152]{1,0:T(8,128)(2,1)}, bf16[256,1152]{1,0:T(8,128)(2,1)}, u32[]{:S(2)}, u32[]{:S(2)}) collective-permute-start(bf16[256,1152]{1,0:T(8,128)(2,1)} %copy-done.11), channel_id=1, source_target_pairs={{0,32},{32,0},{1,33},{33,1},{2,34},{34,2},{3,35},{35,3},{4,36},{36... | collective-permute-start | bytes 1769480 | tf_op jit(solution)/shard_map/ppermute | solution.py:644
  93.4 11.5 %collective-permute-start.20 = (bf16[256,1152]{1,0:T(8,128)(2,1)}, bf16[256,1152]{1,0:T(8,128)(2,1)}, u32[]{:S(2)}, u32[]{:S(2)}) collective-permute-start(bf16[256,1152]{1,0:T(8,128)(2,1)} %copy-done.12), channel_id=1, source_target_pairs={{0,32},{32,0},{1,33},{33,1},{2,34},{34,2},{3,35},{35,3},{4,36},{36... | collective-permute-start | bytes 1769480 | tf_op jit(solution)/shard_map/ppermute | solution.py:644
  100.4 15.6 %collective-permute-start.16 = (bf16[256,1024]{1,0:T(8,128)(2,1)}, bf16[256,1024]{1,0:T(8,128)(2,1)S(1)}, u32[]{:S(2)}, u32[]{:S(2)}) collective-permute-start(bf16[256,1024]{1,0:T(8,128)(2,1)} %get-tuple-element.118.refs_0_), channel_id=1, source_target_pairs={{0,32},{32,0},{1,33},{33,1},{2,34},{34,2},{3,35},{35,3},{4,36},{36... | collective-permute-start | bytes 1572872 | tf_op jit(solution)/shard_map/ppermute | solution.py:644
  101.0 21.9 %collective-permute-start.13 = (bf16[256,1024]{1,0:T(8,128)(2,1)}, bf16[256,1024]{1,0:T(8,128)(2,1)S(1)}, u32[]{:S(2)}, u32[]{:S(2)}) collective-permute-start(bf16[256,1024]{1,0:T(8,128)(2,1)} %get-tuple-element.118.refs_0_), channel_id=1, source_target_pairs={{0,1},{1,2},{2,3},{3,0},{4,5},{5,6},{6,7},{7,4},{8,9},{9,10},{10,1... | collective-permute-start | bytes 1572872 | tf_op jit(solution)/shard_map/ppermute | solution.py:644
  102.0 20.8 %collective-permute-start.14 = (bf16[256,1024]{1,0:T(8,128)(2,1)}, bf16[256,1024]{1,0:T(8,128)(2,1)S(1)}, u32[]{:S(2)}, u32[]{:S(2)}) collective-permute-start(bf16[256,1024]{1,0:T(8,128)(2,1)} %get-tuple-element.118.refs_0_), channel_id=1, source_target_pairs={{0,3},{1,0},{2,1},{3,2},{4,7},{5,4},{6,5},{7,6},{8,11},{9,8},{10,9... | collective-permute-start | bytes 1572872 | tf_op jit(solution)/shard_map/ppermute | solution.py:644
  102.4 23.3 %collective-permute-start.15 = (bf16[256,1024]{1,0:T(8,128)(2,1)}, bf16[256,1024]{1,0:T(8,128)(2,1)S(1)}, u32[]{:S(2)}, u32[]{:S(2)}) collective-permute-start(bf16[256,1024]{1,0:T(8,128)(2,1)} %get-tuple-element.118.refs_0_), channel_id=1, source_target_pairs={{0,2},{1,3},{2,0},{3,1},{4,6},{5,7},{6,4},{7,5},{8,10},{9,11},{10,... | collective-permute-start | bytes 1572872 | tf_op jit(solution)/shard_map/ppermute | solution.py:644
  197.3 18.8 %collective-permute-start.25 = (bf16[256,1152]{1,0:T(8,128)(2,1)S(1)}, bf16[256,1152]{1,0:T(8,128)(2,1)S(1)}, u32[]{:S(2)}, u32[]{:S(2)}) collective-permute-start(bf16[256,1152]{1,0:T(8,128)(2,1)S(1)} %get-tuple-element.188), channel_id=1, source_target_pairs={{0,3},{1,0},{2,1},{3,2},{4,7},{5,4},{6,5},{7,6},{8,11},{9,8},{10,9... | collective-permute-start | bytes 1769480 | tf_op jit(solution)/shard_map/ppermute | solution.py:644
  197.6 18.5 %collective-permute-start.26 = (bf16[256,1152]{1,0:T(8,128)(2,1)S(1)}, bf16[256,1152]{1,0:T(8,128)(2,1)S(1)}, u32[]{:S(2)}, u32[]{:S(2)}) collective-permute-start(bf16[256,1152]{1,0:T(8,128)(2,1)S(1)} %get-tuple-element.187), channel_id=1, source_target_pairs={{0,1},{1,2},{2,3},{3,0},{4,5},{5,6},{6,7},{7,4},{8,9},{9,10},{10,1... | collective-permute-start | bytes 1769480 | tf_op jit(solution)/shard_map/ppermute | solution.py:644
  198.7 27.1 %collective-permute-start.27 = (bf16[256,1152]{1,0:T(8,128)(2,1)S(1)}, bf16[256,1152]{1,0:T(8,128)(2,1)S(1)}, u32[]{:S(2)}, u32[]{:S(2)}) collective-permute-start(bf16[256,1152]{1,0:T(8,128)(2,1)S(1)} %get-tuple-element.186), channel_id=1, source_target_pairs={{0,2},{1,3},{2,0},{3,1},{4,6},{5,7},{6,4},{7,5},{8,10},{9,11},{10,... | collective-permute-start | bytes 1769480 | tf_op jit(solution)/shard_map/ppermute | solution.py:644
  214.7 32.9 %collective-permute-start.29 = (bf16[4,256,1024]{2,1,0:T(8,128)(2,1)}, bf16[4,256,1024]{2,1,0:T(8,128)(2,1)S(1)}, u32[]{:S(2)}, u32[]{:S(2)}) collective-permute-start(bf16[4,256,1024]{2,1,0:T(8,128)(2,1)} %get-tuple-element.143), channel_id=1, source_target_pairs={{0,32},{32,0},{1,33},{33,1},{2,34},{34,2},{3,35},{35,3},{4,36},{36... | collective-permute-start | bytes 6291464 | tf_op jit(solution)/shard_map/ppermute | solution.py:644
  234.5 10.5 %collective-permute-start.28 = (bf16[2,256,1024]{2,1,0:T(8,128)(2,1)}, bf16[2,256,1024]{2,1,0:T(8,128)(2,1)S(1)}, u32[]{:S(2)}, u32[]{:S(2)}) collective-permute-start(bf16[2,256,1024]{2,1,0:T(8,128)(2,1)} %get-tuple-element.139), channel_id=1, source_target_pairs={{0,32},{32,0},{1,33},{33,1},{2,34},{34,2},{3,35},{35,3},{4,36},{36... | collective-permute-start | bytes 3145736 | tf_op jit(solution)/shard_map/ppermute | solution.py:644
  237.2 12.4 %collective-permute-start.30 = (bf16[256,256]{1,0:T(8,128)(2,1)}, bf16[256,256]{1,0:T(8,128)(2,1)S(1)}, u32[]{:S(2)}, u32[]{:S(2)}) collective-permute-start(bf16[256,256]{1,0:T(8,128)(2,1)} %get-tuple-element.145), channel_id=1, source_target_pairs={{0,64},{64,0},{1,65},{65,1},{2,66},{66,2},{3,67},{67,3},{4,68},{68... | collective-permute-start | bytes 393224 | tf_op jit(solution)/shard_map/ppermute | solution.py:644
  237.2 12.4 %collective-permute-start.31 = (bf16[256,256]{1,0:T(8,128)(2,1)}, bf16[256,256]{1,0:T(8,128)(2,1)S(1)}, u32[]{:S(2)}, u32[]{:S(2)}) collective-permute-start(bf16[256,256]{1,0:T(8,128)(2,1)} %get-tuple-element.146), channel_id=1, source_target_pairs={{0,32},{32,0},{1,33},{33,1},{2,34},{34,2},{3,35},{35,3},{4,36},{36... | collective-permute-start | bytes 393224 | tf_op jit(solution)/shard_map/ppermute | solution.py:644
  249.6 29.7 %collective-permute-start.34 = (bf16[256,1024]{1,0:T(8,128)(2,1)}, bf16[256,1024]{1,0:T(8,128)(2,1)S(1)}, u32[]{:S(2)}, u32[]{:S(2)}) collective-permute-start(bf16[256,1024]{1,0:T(8,128)(2,1)} %get-tuple-element.161), channel_id=1, source_target_pairs={{0,3},{1,0},{2,1},{3,2},{4,7},{5,4},{6,5},{7,6},{8,11},{9,8},{10,9... | collective-permute-start | bytes 1572872 | tf_op jit(solution)/shard_map/ppermute | solution.py:644
  249.7 29.6 %collective-permute-start.35 = (bf16[256,1024]{1,0:T(8,128)(2,1)S(1)}, bf16[256,1024]{1,0:T(8,128)(2,1)S(1)}, u32[]{:S(2)}, u32[]{:S(2)}) collective-permute-start(bf16[256,1024]{1,0:T(8,128)(2,1)S(1)} %get-tuple-element.162), channel_id=1, source_target_pairs={{0,1},{1,2},{2,3},{3,0},{4,5},{5,6},{6,7},{7,4},{8,9},{9,10},{10,1... | collective-permute-start | bytes 1572872 | tf_op jit(solution)/shard_map/ppermute | solution.py:644
  251.2 28.2 %all-to-all-start.2 = ((bf16[64,8,1024]{2,1,0:T(8,128)(2,1)}), bf16[64,8,1024]{2,1,0:T(8,128)(2,1)S(1)}, u32[]{:S(2)}, u32[]{:S(2)}) async-start(bf16[64,8,1024]{2,1,0:T(8,128)(2,1)} %bitcast.18), calls=%async_computation.2 | async-start | bytes 2097152 | tf_op jit(solution)/shard_map/all_to_all | solution.py:746
  279.4 18.1 %collective-permute-start.36 = (bf16[2,256,1024]{2,1,0:T(8,128)(2,1)}, bf16[2,256,1024]{2,1,0:T(8,128)(2,1)}, u32[]{:S(2)}, u32[]{:S(2)}) collective-permute-start(bf16[2,256,1024]{2,1,0:T(8,128)(2,1)} %get-tuple-element.166), channel_id=1, source_target_pairs={{0,32},{32,0},{1,33},{33,1},{2,34},{34,2},{3,35},{35,3},{4,36},{36... | collective-permute-start | bytes 3145736 | tf_op jit(solution)/shard_map/ppermute | solution.py:644
  286.3 26.0 %all-to-all-start.3 = ((bf16[128,8,640]{2,1,0:T(8,128)(2,1)}), bf16[128,8,640]{2,1,0:T(8,128)(2,1)S(1)}, u32[]{:S(2)}, u32[]{:S(2)}) async-start(bf16[128,8,640]{2,1,0:T(8,128)(2,1)} %bitcast.79), calls=%async_computation.4 | async-start | bytes 2621440 | tf_op jit(solution)/shard_map/all_to_all | solution.py:759
  296.5 32.5 %collective-permute-start.38 = (bf16[256,1024]{1,0:T(8,128)(2,1)}, bf16[256,1024]{1,0:T(8,128)(2,1)}, u32[]{:S(2)}, u32[]{:S(2)}) collective-permute-start(bf16[256,1024]{1,0:T(8,128)(2,1)} %get-tuple-element.167), channel_id=1, source_target_pairs={{0,2},{1,3},{2,0},{3,1},{4,6},{5,7},{6,4},{7,5},{8,10},{9,11},{10,... | collective-permute-start | bytes 1572872 | tf_op jit(solution)/shard_map/ppermute | solution.py:644
  299.9 29.0 %collective-permute-start.37 = (bf16[256,1024]{1,0:T(8,128)(2,1)}, bf16[256,1024]{1,0:T(8,128)(2,1)}, u32[]{:S(2)}, u32[]{:S(2)}) collective-permute-start(bf16[256,1024]{1,0:T(8,128)(2,1)} %select_bitcast_fusion), channel_id=1, source_target_pairs={{0,64},{64,0},{1,65},{65,1},{2,66},{66,2},{3,67},{67,3},{4,68},{68... | collective-permute-start | bytes 1572872 | tf_op jit(solution)/shard_map/ppermute | solution.py:644
  314.4 11.3 %collective-permute-start.39 = (bf16[512,256]{1,0:T(8,128)(2,1)S(1)}, bf16[512,256]{1,0:T(8,128)(2,1)S(1)}, u32[]{:S(2)}, u32[]{:S(2)}) collective-permute-start(bf16[512,256]{1,0:T(8,128)(2,1)S(1)} %slice_select_fusion), channel_id=1, source_target_pairs={{0,32},{32,0},{1,33},{33,1},{2,34},{34,2},{3,35},{35,3},{4,36},{36... | collective-permute-start | bytes 786440 | tf_op jit(solution)/shard_map/ppermute | solution.py:644
  (56 other events, 424.0 us)
Sparse Core Ops, SparseCore 0:
  46.5 102.1 all-gather.2
  190.6 99.3 reduce-scatter.1

commit v3 on v2

--- a/solution.py
+++ b/solution.py
@@ -691,12 +691,12 @@
         expert_gate.reshape(TOK, FF), expert_up.reshape(TOK, FF),
     )
 
+    expert_w = assemble(place, keep, swap(send, "core"), expert_down.reshape(128, D))
+    expert_w, packed, across = fence(expert_w, packed, across)
+    expert_w = lax.all_gather(expert_w, PLANE, axis=0).reshape(16, 1536, 256)
+
     arrived = lax.all_to_all(packed, AXES, split_axis=0, concat_axis=0, tiled=True).reshape(D, 640)
     beside = swap(own, "core")
-
-    expert_w = assemble(place, keep, swap(send, "core"), expert_down.reshape(128, D))
-    expert_w, arrived, across, beside = fence(expert_w, arrived, across, beside)
-    expert_w = lax.all_gather(expert_w, PLANE, axis=0).reshape(16, 1536, 256)
 
     lane = jnp.arange(128) % 32
     angles = jnp.arange(LENGTH).astype(f32)[:, None] * (rope_base ** (-2.0 * lane.astype(f32) / HEAD))[None, :]
@@ -740,8 +740,7 @@
 
     do = exchange_seq(*do)
     grad_output_sum = (keep.astype(f32) + swap(send, "core").astype(f32)).astype(bf16).reshape(64, 8, D)
-    grad_output_sum, *rest = fence(grad_output_sum, *moe_sums, *do)
-    moe_sums, do = rest[:4], rest[4:]
+    grad_output_sum, *moe_sums = fence(grad_output_sum, *moe_sums)
     moe_near = [shift(moe_sums[1], "z", -1), shift(moe_sums[2], "z", 1)]
     grad_output = lax.all_to_all(grad_output_sum, ("ylo",) + FSDP, split_axis=0, concat_axis=0, tiled=True)
     dqkv, keep, send, gain = back(place, q, k, v, do, lse, cos, sin, arrived, blocks)
@@ -754,18 +753,12 @@
     pair = (keep.astype(f32) + swap(send, "core").astype(f32)).astype(bf16)
     kept = jnp.where(ylo == 0, pair[0], pair[1])
     got = swap(jnp.where(ylo == 0, pair[1], pair[0]), "ylo")
-    got, moe_far, grad_gate, grad_up, grad_down = fence(got, shift(moe_sums[3], "z", 2), *finished)
+    got, moe_far = fence(got, shift(moe_sums[3], "z", 2))
     grad_hidden_one = kept.astype(f32) + got.astype(f32)
     first = lax.all_to_all(first.reshape(128, 8, 640), AXES, split_axis=0, concat_axis=0, tiled=True)
     grad_output = jnp.sum(grad_output.astype(f32), axis=0)
     layer_out = sum(part.astype(f32) for part in (moe_sums[0], *moe_near, moe_far))
     layer_out = (residual + layer_out).astype(bf16).reshape(1, TOK, D)
-    first = jnp.sum(first.astype(f32).reshape(4, 32, 8, 640), axis=1)
-    grad_query = first[:, :, :256].transpose(1, 0, 2).reshape(8, D)
-    grad_key = first[:, :, 256:384].transpose(1, 0, 2).reshape(8, 512)
-    grad_value = first[:, :, 384:512].transpose(1, 0, 2).reshape(8, 512)
-    small = jnp.sum(first[:, :, 512:], axis=0)
-
     inputs = own.astype(f32)
     factor_one = lax.rsqrt(jnp.mean(inputs * inputs, axis=-1, keepdims=True) + epsilon)
     normed_one = inputs * factor_one
@@ -774,6 +767,14 @@
         scaled - normed_one * jnp.mean(scaled * normed_one, axis=-1, keepdims=True)
     )
 
+    first, layer_out, grad_inputs, grad_output, grad_gate, grad_up, grad_down = fence(
+        first, layer_out, grad_inputs, grad_output, *finished
+    )
+    first = jnp.sum(first.astype(f32).reshape(4, 32, 8, 640), axis=1)
+    grad_query = first[:, :, :256].transpose(1, 0, 2).reshape(8, D)
+    grad_key = first[:, :, 256:384].transpose(1, 0, 2).reshape(8, 512)
+    grad_value = first[:, :, 384:512].transpose(1, 0, 2).reshape(8, 512)
+    small = jnp.sum(first[:, :, 512:], axis=0)
     return (
         layer_out, grad_inputs.reshape(1, TOK, D), small[:, 32], grad_query, grad_key, grad_value, grad_output,
         small[:, 33], small[:, :EXPERTS], grad_gate.reshape(1, TOK, FF), grad_up.reshape(1, TOK, FF),

time: 346 us -> 355 us (1.026)
  the two profiles are of different devices: /device:TPU:79 before, /device:TPU:1 now
where the time goes in v3:
time: 355 us; the launch traced here: 350 us
  Pallas kernels  141 us (40%)
  waiting for transfers between devices  88.3 us (25%)
  starting transfers between devices  76.8 us (22%)
  other arithmetic  18.8 us (5%)
  between operations  14.6 us (4%)
  local copies, waits for them, and re-layouts  10.5 us (3%)
    ppermute x40, waiting for transfers between devices, shift(): return lax.ppermute(values, axis, [(i, (i + by) % n) for i in range(n)])  68.8 us
    ppermute x40, starting transfers between devices, shift(): return lax.ppermute(values, axis, [(i, (i + by) % n) for i in range(n)])  43.1 us
    pallas_call x1, Pallas kernels, main(): call(main_kernel, 'experts', 25000000000, 60000000, grid=(SHARE,), in_spe...  41.7 us
    pallas_call x3, Pallas kernels, rows_of(): call(functools.partial(rows_kernel, n, with_gates), 'rows', n * 750000000...  30.2 us
    all_to_all x1, waiting for transfers between devices, on_device(): lax.all_to_all(packed, AXES, split_axis=0, concat_axis=0, tiled=True)  19.4 us
    pallas_call x1, Pallas kernels, back(): call(back_kernel, 'back', 20000000000, 16000000, in_specs=[SCALAR] + [VEC...  16.6 us
    pallas_call x1, Pallas kernels, outs(): call(outs_kernel, 'expert_outs', 6000000000, 12000000, grid=(SHARE,), in_...  14.8 us
    pallas_call x1, Pallas kernels, front(): call(front_kernel, 'front', 8000000000, 10000000, in_specs=[SCALAR] + [VE...  12 us
  transfers between devices with their start and end apart: 46, of which 15 were waited for; matrix products, arithmetic and copies ran while one was open for 6% of the time, Pallas kernels for 28%

profile of v3, /device:TPU:1, one launch (start us, length us, event | category | flops | bytes accessed | tf_op | source)
XLA Modules:
  0.0 350.3 jit_solution(13415251638846520564)
XLA Ops:
  10.0 2.4 pack.1
  17.6 3.4 collective-permute-done.1.x1_ref
  21.0 11.8 %all-to-all-start = ((bf16[128,8,640]{2,1,0:T(8,128)(2,1)}), bf16[128,8,640]{2,1,0:T(8,128)(2,1)S(1)}, u32[]{:S(2)}, u32[]{:S(2)}) async-start(bf16[128,8,640]{2,1,0:T(8,128)(2,1)} %get-tuple-element.101), calls=%async_computation | async-start | bytes 2621440 | tf_op jit(solution)/shard_map/all_to_all | solution.py:698
  34.8 2.6 codes.1.refs_0_.refs_2_.gy_ref
  37.3 2.6 collective-permute-start.10
  44.6 19.4 %all-to-all-done = bf16[128,8,640]{2,1,0:T(8,128)(2,1)S(1)} async-done(((bf16[128,8,640]{2,1,0:T(8,128)(2,1)}), bf16[128,8,640]{2,1,0:T(8,128)(2,1)S(1)}, u32[]{:S(2)}, u32[]{:S(2)}) %all-to-all-start) | async-done | bytes 1310752 | tf_op jit(solution)/shard_map/all_to_all | solution.py:698
  65.2 5.6 %all-to-all-start.1 = ((bf16[32,8,2048]{2,1,0:T(8,128)(2,1)}), bf16[32,8,2048]{2,1,0:T(8,128)(2,1)S(1)}, u32[]{:S(2)}, u32[]{:S(2)}) async-start(bf16[32,8,2048]{2,1,0:T(8,128)(2,1)} %broadcast_in_dim.4), calls=%async_computation.1 | async-start | bytes 2097152 | tf_op jit(solution)/shard_map/all_to_all | solution.py:709
  71.3 3.1 multiply_sine_fusion
  74.4 12.0 %front.1 = (bf16[1024,256]{1,0:T(8,128)(2,1)}, bf16[1024,256]{1,0:T(8,128)(2,1)}, bf16[1024,256]{1,0:T(8,128)(2,1)}, bf16[256,256]{1,0:T(8,128)(2,1)}, bf16[256,...) custom-call(s32[2]{0:T(128)} %pad_add_fusion.place_ref, ...), custom_call_target="tpu_custom_call" | custom-call | flops 8000000000 | bytes 10000000 | tf_op jit(solution)/shard_map/front/pallas_call | solution.py:234
  90.2 6.2 %collective-permute-done.7 = bf16[256,256]{1,0:T(8,128)(2,1)S(1)} collective-permute-done((bf16[256,256]{1,0:T(8,128)(2,1)}, bf16[256,256]{1,0:T(8,128)(2,1)S(1)}, u32[]{:S(2)}, u32[]{:S(2)}) %collective-permute-start.7) | collective-permute-done | bytes 131104 | tf_op jit(solution)/shard_map/ppermute | solution.py:644
  96.4 2.5 collective-permute-start.8
  98.9 3.5 collective-permute-done.5.m1_ref
  107.9 4.0 %mid.1 = (f32[256,1024]{1,0:T(8,128)}, bf16[256,1024]{1,0:T(8,128)(2,1)}) custom-call(bf16[256,1024]{1,0:T(8,128)(2,1)} %bitcast.69, bf16[256,256]{1,0:T(8,128)(2,1)} %get-tuple-element.113.m0_ref, bf16[256,256]{1,0:T(8,128)(2,1)} %copy-done.23, bf16[256,256]{1,0:T(8,128)(2,1)} %copy-done.24, bf16[256,256]{1,0:T(8,128)(2,1)} %copy-done.25, ...), custom_call_target="tpu_custom_call" | custom-call | flops 1000000000 | bytes 5000000 | tf_op jit(solution)/shard_map/mid/pallas_call | solution.py:258
  117.7 10.5 %rows.3 = (bf16[8,8,80,1024]{3,2,1,0:T(8,128)(2,1)}, f32[8,128]{1,0:T(8,128)}) custom-call(s32[1]{0:T(128)} %bitcast.9.z_ref, bf16[256,1152]{1,0:T(8,128)(2,1)} %codes.1.refs_0_.refs_2_.gy_ref, bf16[256,1152]{1,0:T(8,128)(2,1)} %collective-permute-done.17.refs_1_.refs_3_, bf16[256,1152]{1,0:T(8,128)(2,1)} %collective-permute-done.9.refs_2_.refs_6_, ...), custom_call_target="tpu_custom_call" | custom-call | flops 6000000000 | bytes 16000000 | tf_op jit(solution)/shard_map/rows/pallas_call | solution.py:472
  129.1 6.0 %rows.4 = (bf16[8,8,80,1024]{3,2,1,0:T(8,128)(2,1)}, f32[8,8,80,1]{3,2,1,0:T(8,128)}, f32[8,128]{1,0:T(8,128)}) custom-call(s32[1]{0:T(128)} %bitcast.9.z_ref, bf16[256,1024]{1,0:T(8,128)(2,1)} %get-tuple-element.119.refs_0_, bf16[256,1024]{1,0:T(8,128)(2,1)} %copy-done.29, bf16[256,1152]{1,0:T(8,128)(2,1)} %codes.1.refs_0_.refs_2_.gy_ref, ...), custom_call_target="tpu_custom_call" | custom-call | flops 1500000000 | bytes 4000000 | tf_op jit(solution)/shard_map/rows/pallas_call | solution.py:472
  135.1 4.3 %collective-permute-done.15.refs_4_ = bf16[256,1024]{1,0:T(8,128)(2,1)S(1)} collective-permute-done((bf16[256,1024]{1,0:T(8,128)(2,1)}, bf16[256,1024]{1,0:T(8,128)(2,1)S(1)}, u32[]{:S(2)}, u32[]{:S(2)}) %collective-permute-start.15) | collective-permute-done | bytes 524320 | tf_op jit(solution)/shard_map/ppermute | solution.py:644
  144.2 13.7 %rows.5 = (bf16[8,8,80,1024]{3,2,1,0:T(8,128)(2,1)}, f32[8,8,80,1]{3,2,1,0:T(8,128)}, f32[8,128]{1,0:T(8,128)}) custom-call(s32[1]{0:T(128)} %bitcast.9.z_ref, bf16[256,1024]{1,0:T(8,128)(2,1)} %copy-done.15, bf16[256,1024]{1,0:T(8,128)(2,1)} %copy-done.18, bf16[256,1024]{1,0:T(8,128)(2,1)} %copy-done.16, ...), custom_call_target="tpu_custom_call", output_to_operand_aliasing={{0}: (15, {}), {1}: (16, {})} | custom-call | flops 4499999744 | bytes 12000000 | tf_op jit(solution)/shard_map/rows/pallas_call | solution.py:472
  157.9 41.7 %experts.1 = (bf16[8,640,256]{2,1,0:T(8,128)(2,1)}, bf16[8,2,768,512]{3,2,1,0:T(8,128)(2,1)}, bf16[4,256,1152]{2,1,0:T(8,128)(2,1)}, bf16[4,256,1152]{2,1,0:T(8,128)(2,1)}) custom-call(s32[1]{0:T(128)} %bitcast.9.z_ref, bf16[8,8,80,1024]{3,2,1,0:T(8,128)(2,1)} %get-tuple-element.133.x_ref, bf16[8,8,80,1024]{3,2,1,0:T(8,128)(2,1)} %get-tuple-element.134.gy_ref, ...), custom_call_target="tpu_custom_call" | custom-call | flops 24999999488 | bytes 60000000 | tf_op jit(solution)/shard_map/experts/pallas_call | solution.py:559
  200.3 4.4 %collective-permute-done.24 = bf16[4,256,1152]{2,1,0:T(8,128)(2,1)S(1)} collective-permute-done((bf16[4,256,1152]{2,1,0:T(8,128)(2,1)}, bf16[4,256,1152]{2,1,0:T(8,128)(2,1)S(1)}, u32[]{:S(2)}, u32[]{:S(2)}) %collective-permute-start.24) | collective-permute-done | bytes 2359328 | tf_op jit(solution)/shard_map/ppermute | solution.py:644
  209.1 14.8 %expert_outs.1 = (bf16[4,256,1024]{2,1,0:T(8,128)(2,1)}, bf16[4,256,1024]{2,1,0:T(8,128)(2,1)}) custom-call(s32[1]{0:T(128)} %bitcast.9.z_ref, bf16[8,640,256]{2,1,0:T(8,128)(2,1)} %get-tuple-element.151.act_ref, bf16[16,1536,256]{2,1,0:T(8,128)(2,1)} %bitcast.92, bf16[256,1152]{1,0:T(8,128)(2,1)} %codes.1.refs_0_.refs_2_.gy_ref, ...), custom_call_target="tpu_custom_call" | custom-call | flops 6000000000 | bytes 12000000 | tf_op jit(solution)/shard_map/expert_outs/pallas_call | solution.py:607
  224.7 11.4 %collective-permute-done.26.part2_ref = bf16[256,1152]{1,0:T(8,128)(2,1)S(1)} collective-permute-done((bf16[256,1152]{1,0:T(8,128)(2,1)S(1)}, bf16[256,1152]{1,0:T(8,128)(2,1)S(1)}, u32[]{:S(2)}, u32[]{:S(2)}) %collective-permute-start.26) | collective-permute-done | bytes 589856 | tf_op jit(solution)/shard_map/ppermute | solution.py:644
  237.1 7.9 %turn.1 = (bf16[256,256]{1,0:T(8,128)(2,1)}, bf16[256,256]{1,0:T(8,128)(2,1)}, bf16[256,256]{1,0:T(8,128)(2,1)}, bf16[256,256]{1,0:T(8,128)(2,1)}, f32[256,1024]...) custom-call(s32[2]{0:T(128)} %pad_add_fusion.place_ref, ...), custom_call_target="tpu_custom_call" | custom-call | flops 2000000000 | bytes 10000000 | tf_op jit(solution)/shard_map/turn/pallas_call | solution.py:299
  248.7 6.1 %collective-permute-done.30 = bf16[256,256]{1,0:T(8,128)(2,1)} collective-permute-done((bf16[256,256]{1,0:T(8,128)(2,1)}, bf16[256,256]{1,0:T(8,128)(2,1)}, u32[]{:S(2)}, u32[]{:S(2)}) %collective-permute-start.30) | collective-permute-done | bytes 131104 | tf_op jit(solution)/shard_map/ppermute | solution.py:644
  255.8 2.6 add_convert_fusion.1
  261.8 9.1 %all-to-all-start.2 = ((bf16[64,8,1024]{2,1,0:T(8,128)(2,1)}), bf16[64,8,1024]{2,1,0:T(8,128)(2,1)S(1)}, u32[]{:S(2)}, u32[]{:S(2)}) async-start(bf16[64,8,1024]{2,1,0:T(8,128)(2,1)} %bitcast.18), calls=%async_computation.2 | async-start | bytes 2097152 | tf_op jit(solution)/shard_map/all_to_all | solution.py:745
  271.7 16.6 %back.1 = (bf16[1024,512]{1,0:T(8,128)(2,1)}, bf16[2,256,1024]{2,1,0:T(8,128)(2,1)}, bf16[2,256,1024]{2,1,0:T(8,128)(2,1)}, f32[8,1024]{1,0:T(8,128)}) custom-call(s32[2]{0:T(128)} %pad_add_fusion.place_ref, bf16[1024,256]{1,0:T(8,128)(2,1)} %get-tuple-element.105.q_ref, bf16[1024,256]{1,0:T(8,128)(2,1)} %get-tuple-element.106.k_ref, ...), custom_call_target="tpu_custom_call" | custom-call | flops 20000000000 | bytes 16000000 | tf_op jit(solution)/shard_map/back/pallas_call | solution.py:363
  288.4 4.6 %collective-permute-start.36 = (bf16[2,256,1024]{2,1,0:T(8,128)(2,1)}, bf16[2,256,1024]{2,1,0:T(8,128)(2,1)}, u32[]{:S(2)}, u32[]{:S(2)}) collective-permute-start(bf16[2,256,1024]{2,1,0:T(8,128)(2,1)} %get-tuple-element.164), channel_id=1, source_target_pairs={{0,32},{32,0},{1,33},{33,1},{2,34},{34,2},{3,35},{35,3},{4,36},{36... | collective-permute-start | bytes 3145736 | tf_op jit(solution)/shard_map/ppermute | solution.py:644
  293.7 4.4 %projections.1 = bf16[1024,640]{1,0:T(8,128)(2,1)} custom-call(bf16[1024,1024]{1,0:T(8,128)(2,1)} %get-tuple-element.104.h_ref, bf16[1024,512]{1,0:T(8,128)(2,1)} %get-tuple-element.157.dqkv_ref, f32[1024,128]{1,0:T(8,128)} %get-tuple-element.158.sums_ref, f32[8,1024]{1,0:T(8,128)} %get-tuple-element.159.gain_ref), custom_call_target="tpu_custom_call" | custom-call | flops 1500000000 | bytes 5000000 | tf_op jit(solution)/shard_map/projections/pallas_call | solution.py:380
  298.2 6.6 %all-to-all-start.3 = ((bf16[128,8,640]{2,1,0:T(8,128)(2,1)}), bf16[128,8,640]{2,1,0:T(8,128)(2,1)S(1)}, u32[]{:S(2)}, u32[]{:S(2)}) async-start(bf16[128,8,640]{2,1,0:T(8,128)(2,1)} %bitcast.78), calls=%async_computation.3 | async-start | bytes 2621440 | tf_op jit(solution)/shard_map/all_to_all | solution.py:758
  309.3 22.2 %collective-permute-done.37 = bf16[256,1024]{1,0:T(8,128)(2,1)S(1)} collective-permute-done((bf16[256,1024]{1,0:T(8,128)(2,1)S(1)}, bf16[256,1024]{1,0:T(8,128)(2,1)S(1)}, u32[]{:S(2)}, u32[]{:S(2)}) %collective-permute-start.37) | collective-permute-done | bytes 524320 | tf_op jit(solution)/shard_map/ppermute | solution.py:644
  335.5 2.4 fusion.16
  338.6 2.5 finish.1
  (168 shorter events, 64.8 us)
Async XLA Ops:
  7.2 150.7 %all-gather.3.cloned.1.call-start = ((), (), s32[]{:S(2)}) async-start(), calls=%async_computation.6 | async-start | bytes 13369344 | tf_op jit(solution)/shard_map/all_gather | solution.py:696
  7.2 13.8 %collective-permute-start.1 = (bf16[256,1024]{1,0:T(8,128)(2,1)}, bf16[256,1024]{1,0:T(8,128)(2,1)}, u32[]{:S(2)}, u32[]{:S(2)}) collective-permute-start(bf16[256,1024]{1,0:T(8,128)(2,1)} %bitcast.67), channel_id=1, source_target_pairs={{0,64},{64,0},{1,65},{65,1},{2,66},{66,2},{3,67},{67,3},{4,68},{68... | collective-permute-start | bytes 1572872 | tf_op jit(solution)/shard_map/ppermute | solution.py:644
  21.0 43.0 %all-to-all-start = ((bf16[128,8,640]{2,1,0:T(8,128)(2,1)}), bf16[128,8,640]{2,1,0:T(8,128)(2,1)S(1)}, u32[]{:S(2)}, u32[]{:S(2)}) async-start(bf16[128,8,640]{2,1,0:T(8,128)(2,1)} %get-tuple-element.101), calls=%async_computation | async-start | bytes 2621440 | tf_op jit(solution)/shard_map/all_to_all | solution.py:698
  32.8 41.5 %collective-permute-start.2 = (bf16[256,1024]{1,0:T(8,128)(2,1)S(1)}, bf16[256,1024]{1,0:T(8,128)(2,1)}, u32[]{:S(2)}, u32[]{:S(2)}) collective-permute-start(bf16[256,1024]{1,0:T(8,128)(2,1)S(1)} %bitcast.71), channel_id=1, source_target_pairs={{0,32},{32,0},{1,33},{33,1},{2,34},{34,2},{3,35},{35,3},{4,36},{36... | collective-permute-start | bytes 1572872 | tf_op jit(solution)/shard_map/ppermute | solution.py:644
  37.3 50.7 %collective-permute-start.10 = (bf16[256,1152]{1,0:T(8,128)(2,1)}, bf16[256,1152]{1,0:T(8,128)(2,1)S(1)}, u32[]{:S(2)}, u32[]{:S(2)}) collective-permute-start(bf16[256,1152]{1,0:T(8,128)(2,1)} %codes.1.refs_0_.refs_2_.gy_ref), channel_id=1, source_target_pairs={{0,3},{1,0},{2,1},{3,2},{4,7},{5,4},{6,5},{7,6},{8,11},{9,8},{10,9... | collective-permute-start | bytes 1769480 | tf_op jit(solution)/shard_map/ppermute | solution.py:644
  39.9 59.0 %collective-permute-start.11 = (bf16[256,1152]{1,0:T(8,128)(2,1)}, bf16[256,1152]{1,0:T(8,128)(2,1)}, u32[]{:S(2)}, u32[]{:S(2)}) collective-permute-start(bf16[256,1152]{1,0:T(8,128)(2,1)} %codes.1.refs_0_.refs_2_.gy_ref), channel_id=1, source_target_pairs={{0,2},{1,3},{2,0},{3,1},{4,6},{5,7},{6,4},{7,5},{8,10},{9,11},{10,... | collective-permute-start | bytes 1769480 | tf_op jit(solution)/shard_map/ppermute | solution.py:644
  41.2 33.2 %collective-permute-start.3 = (bf16[256,1024]{1,0:T(8,128)(2,1)}, bf16[256,1024]{1,0:T(8,128)(2,1)}, u32[]{:S(2)}, u32[]{:S(2)}) collective-permute-start(bf16[256,1024]{1,0:T(8,128)(2,1)} %collective-permute-done.1.x1_ref), channel_id=1, source_target_pairs={{0,32},{32,0},{1,33},{33,1},{2,34},{34,2},{3,35},{35,3},{4,36},{36... | collective-permute-start | bytes 1572872 | tf_op jit(solution)/shard_map/ppermute | solution.py:644
  43.9 55.0 %collective-permute-start.9 = (bf16[256,1152]{1,0:T(8,128)(2,1)}, bf16[256,1152]{1,0:T(8,128)(2,1)}, u32[]{:S(2)}, u32[]{:S(2)}) collective-permute-start(bf16[256,1152]{1,0:T(8,128)(2,1)} %codes.1.refs_0_.refs_2_.gy_ref), channel_id=1, source_target_pairs={{0,1},{1,2},{2,3},{3,0},{4,5},{5,6},{6,7},{7,4},{8,9},{9,10},{10,1... | collective-permute-start | bytes 1769480 | tf_op jit(solution)/shard_map/ppermute | solution.py:644
  65.2 37.2 %all-to-all-start.1 = ((bf16[32,8,2048]{2,1,0:T(8,128)(2,1)}), bf16[32,8,2048]{2,1,0:T(8,128)(2,1)S(1)}, u32[]{:S(2)}, u32[]{:S(2)}) async-start(bf16[32,8,2048]{2,1,0:T(8,128)(2,1)} %broadcast_in_dim.4), calls=%async_computation.1 | async-start | bytes 2097152 | tf_op jit(solution)/shard_map/all_to_all | solution.py:709
  70.7 262.7 %reduce-scatter.2.cloned.1.call-start = ((), (), s32[]{:S(2)}) async-start(), calls=%async_computation.5 | async-start | bytes 13369344 | tf_op jit(solution)/shard_map/reduce_scatter | solution.py:734
  88.0 14.4 %collective-permute-start.5 = (bf16[256,256]{1,0:T(8,128)(2,1)}, bf16[256,256]{1,0:T(8,128)(2,1)S(1)}, u32[]{:S(2)}, u32[]{:S(2)}) collective-permute-start(bf16[256,256]{1,0:T(8,128)(2,1)} %get-tuple-element.110), channel_id=1, source_target_pairs={{0,64},{64,0},{1,65},{65,1},{2,66},{66,2},{3,67},{67,3},{4,68},{68... | collective-permute-start | bytes 393224 | tf_op jit(solution)/shard_map/ppermute | solution.py:644
  88.1 14.3 %collective-permute-start.6 = (bf16[256,256]{1,0:T(8,128)(2,1)}, bf16[256,256]{1,0:T(8,128)(2,1)S(1)}, u32[]{:S(2)}, u32[]{:S(2)}) collective-permute-start(bf16[256,256]{1,0:T(8,128)(2,1)} %get-tuple-element.111), channel_id=1, source_target_pairs={{0,32},{32,0},{1,33},{33,1},{2,34},{34,2},{3,35},{35,3},{4,36},{36... | collective-permute-start | bytes 393224 | tf_op jit(solution)/shard_map/ppermute | solution.py:644
  104.8 12.3 %collective-permute-start.20 = (bf16[256,1152]{1,0:T(8,128)(2,1)}, bf16[256,1152]{1,0:T(8,128)(2,1)}, u32[]{:S(2)}, u32[]{:S(2)}) collective-permute-start(bf16[256,1152]{1,0:T(8,128)(2,1)} %collective-permute-done.11.refs_6_.refs_10_), channel_id=1, source_target_pairs={{0,32},{32,0},{1,33},{33,1},{2,34},{34,2},{3,35},{35,3},{4,36},{36... | collective-permute-start | bytes 1769480 | tf_op jit(solution)/shard_map/ppermute | solution.py:644
  111.9 16.4 %collective-permute-start.16 = (bf16[256,1024]{1,0:T(8,128)(2,1)}, bf16[256,1024]{1,0:T(8,128)(2,1)S(1)}, u32[]{:S(2)}, u32[]{:S(2)}) collective-permute-start(bf16[256,1024]{1,0:T(8,128)(2,1)} %get-tuple-element.119.refs_0_), channel_id=1, source_target_pairs={{0,32},{32,0},{1,33},{33,1},{2,34},{34,2},{3,35},{35,3},{4,36},{36... | collective-permute-start | bytes 1572872 | tf_op jit(solution)/shard_map/ppermute | solution.py:644
  112.4 22.7 %collective-permute-start.13 = (bf16[256,1024]{1,0:T(8,128)(2,1)}, bf16[256,1024]{1,0:T(8,128)(2,1)S(1)}, u32[]{:S(2)}, u32[]{:S(2)}) collective-permute-start(bf16[256,1024]{1,0:T(8,128)(2,1)} %get-tuple-element.119.refs_0_), channel_id=1, source_target_pairs={{0,1},{1,2},{2,3},{3,0},{4,5},{5,6},{6,7},{7,4},{8,9},{9,10},{10,1... | collective-permute-start | bytes 1572872 | tf_op jit(solution)/shard_map/ppermute | solution.py:644
  113.8 21.3 %collective-permute-start.14 = (bf16[256,1024]{1,0:T(8,128)(2,1)}, bf16[256,1024]{1,0:T(8,128)(2,1)S(1)}, u32[]{:S(2)}, u32[]{:S(2)}) collective-permute-start(bf16[256,1024]{1,0:T(8,128)(2,1)} %get-tuple-element.119.refs_0_), channel_id=1, source_target_pairs={{0,3},{1,0},{2,1},{3,2},{4,7},{5,4},{6,5},{7,6},{8,11},{9,8},{10,9... | collective-permute-start | bytes 1572872 | tf_op jit(solution)/shard_map/ppermute | solution.py:644
  115.1 24.3 %collective-permute-start.15 = (bf16[256,1024]{1,0:T(8,128)(2,1)}, bf16[256,1024]{1,0:T(8,128)(2,1)S(1)}, u32[]{:S(2)}, u32[]{:S(2)}) collective-permute-start(bf16[256,1024]{1,0:T(8,128)(2,1)} %get-tuple-element.119.refs_0_), channel_id=1, source_target_pairs={{0,2},{1,3},{2,0},{3,1},{4,6},{5,7},{6,4},{7,5},{8,10},{9,11},{10,... | collective-permute-start | bytes 1572872 | tf_op jit(solution)/shard_map/ppermute | solution.py:644
  206.2 18.6 %collective-permute-start.25 = (bf16[256,1152]{1,0:T(8,128)(2,1)S(1)}, bf16[256,1152]{1,0:T(8,128)(2,1)S(1)}, u32[]{:S(2)}, u32[]{:S(2)}) collective-permute-start(bf16[256,1152]{1,0:T(8,128)(2,1)S(1)} %get-tuple-element.186), channel_id=1, source_target_pairs={{0,3},{1,0},{2,1},{3,2},{4,7},{5,4},{6,5},{7,6},{8,11},{9,8},{10,9... | collective-permute-start | bytes 1769480 | tf_op jit(solution)/shard_map/ppermute | solution.py:644
  207.9 28.2 %collective-permute-start.26 = (bf16[256,1152]{1,0:T(8,128)(2,1)S(1)}, bf16[256,1152]{1,0:T(8,128)(2,1)S(1)}, u32[]{:S(2)}, u32[]{:S(2)}) collective-permute-start(bf16[256,1152]{1,0:T(8,128)(2,1)S(1)} %get-tuple-element.185), channel_id=1, source_target_pairs={{0,1},{1,2},{2,3},{3,0},{4,5},{5,6},{6,7},{7,4},{8,9},{9,10},{10,1... | collective-permute-start | bytes 1769480 | tf_op jit(solution)/shard_map/ppermute | solution.py:644
  207.9 28.2 %collective-permute-start.27 = (bf16[256,1152]{1,0:T(8,128)(2,1)S(1)}, bf16[256,1152]{1,0:T(8,128)(2,1)S(1)}, u32[]{:S(2)}, u32[]{:S(2)}) collective-permute-start(bf16[256,1152]{1,0:T(8,128)(2,1)S(1)} %get-tuple-element.184), channel_id=1, source_target_pairs={{0,2},{1,3},{2,0},{3,1},{4,6},{5,7},{6,4},{7,5},{8,10},{9,11},{10,... | collective-permute-start | bytes 1769480 | tf_op jit(solution)/shard_map/ppermute | solution.py:644
  223.9 34.5 %collective-permute-start.33 = (bf16[4,256,1024]{2,1,0:T(8,128)(2,1)}, bf16[4,256,1024]{2,1,0:T(8,128)(2,1)S(1)}, u32[]{:S(2)}, u32[]{:S(2)}) collective-permute-start(bf16[4,256,1024]{2,1,0:T(8,128)(2,1)} %get-tuple-element.153), channel_id=1, source_target_pairs={{0,32},{32,0},{1,33},{33,1},{2,34},{34,2},{3,35},{35,3},{4,36},{36... | collective-permute-start | bytes 6291464 | tf_op jit(solution)/shard_map/ppermute | solution.py:644
  245.0 10.8 %collective-permute-start.32 = (bf16[2,256,1024]{2,1,0:T(8,128)(2,1)}, bf16[2,256,1024]{2,1,0:T(8,128)(2,1)S(1)}, u32[]{:S(2)}, u32[]{:S(2)}) collective-permute-start(bf16[2,256,1024]{2,1,0:T(8,128)(2,1)} %get-tuple-element.149), channel_id=1, source_target_pairs={{0,32},{32,0},{1,33},{33,1},{2,34},{34,2},{3,35},{35,3},{4,36},{36... | collective-permute-start | bytes 3145736 | tf_op jit(solution)/shard_map/ppermute | solution.py:644
  247.0 23.9 %collective-permute-start.28 = (bf16[256,256]{1,0:T(8,128)(2,1)}, bf16[256,256]{1,0:T(8,128)(2,1)S(1)}, u32[]{:S(2)}, u32[]{:S(2)}) collective-permute-start(bf16[256,256]{1,0:T(8,128)(2,1)} %get-tuple-element.141), channel_id=1, source_target_pairs={{0,64},{64,0},{1,65},{65,1},{2,66},{66,2},{3,67},{67,3},{4,68},{68... | collective-permute-start | bytes 393224 | tf_op jit(solution)/shard_map/ppermute | solution.py:644
  248.0 22.9 %collective-permute-start.29 = (bf16[256,256]{1,0:T(8,128)(2,1)}, bf16[256,256]{1,0:T(8,128)(2,1)S(1)}, u32[]{:S(2)}, u32[]{:S(2)}) collective-permute-start(bf16[256,256]{1,0:T(8,128)(2,1)} %get-tuple-element.142), channel_id=1, source_target_pairs={{0,32},{32,0},{1,33},{33,1},{2,34},{34,2},{3,35},{35,3},{4,36},{36... | collective-permute-start | bytes 393224 | tf_op jit(solution)/shard_map/ppermute | solution.py:644
  254.7 16.2 %collective-permute-start.31 = (bf16[256,256]{1,0:T(8,128)(2,1)}, bf16[256,256]{1,0:T(8,128)(2,1)S(1)}, u32[]{:S(2)}, u32[]{:S(2)}) collective-permute-start(bf16[256,256]{1,0:T(8,128)(2,1)} %collective-permute-done.30), channel_id=1, source_target_pairs={{0,32},{32,0},{1,33},{33,1},{2,34},{34,2},{3,35},{35,3},{4,36},{36... | collective-permute-start | bytes 393224 | tf_op jit(solution)/shard_map/ppermute | solution.py:644
  260.3 28.0 %collective-permute-start.34 = (bf16[256,1024]{1,0:T(8,128)(2,1)}, bf16[256,1024]{1,0:T(8,128)(2,1)S(1)}, u32[]{:S(2)}, u32[]{:S(2)}) collective-permute-start(bf16[256,1024]{1,0:T(8,128)(2,1)} %get-tuple-element.155), channel_id=1, source_target_pairs={{0,3},{1,0},{2,1},{3,2},{4,7},{5,4},{6,5},{7,6},{8,11},{9,8},{10,9... | collective-permute-start | bytes 1572872 | tf_op jit(solution)/shard_map/ppermute | solution.py:644
  260.3 28.0 %collective-permute-start.35 = (bf16[256,1024]{1,0:T(8,128)(2,1)S(1)}, bf16[256,1024]{1,0:T(8,128)(2,1)S(1)}, u32[]{:S(2)}, u32[]{:S(2)}) collective-permute-start(bf16[256,1024]{1,0:T(8,128)(2,1)S(1)} %get-tuple-element.156), channel_id=1, source_target_pairs={{0,1},{1,2},{2,3},{3,0},{4,5},{5,6},{6,7},{7,4},{8,9},{9,10},{10,1... | collective-permute-start | bytes 1572872 | tf_op jit(solution)/shard_map/ppermute | solution.py:644
  261.8 26.5 %all-to-all-start.2 = ((bf16[64,8,1024]{2,1,0:T(8,128)(2,1)}), bf16[64,8,1024]{2,1,0:T(8,128)(2,1)S(1)}, u32[]{:S(2)}, u32[]{:S(2)}) async-start(bf16[64,8,1024]{2,1,0:T(8,128)(2,1)} %bitcast.18), calls=%async_computation.2 | async-start | bytes 2097152 | tf_op jit(solution)/shard_map/all_to_all | solution.py:745
  288.4 16.4 %collective-permute-start.36 = (bf16[2,256,1024]{2,1,0:T(8,128)(2,1)}, bf16[2,256,1024]{2,1,0:T(8,128)(2,1)}, u32[]{:S(2)}, u32[]{:S(2)}) collective-permute-start(bf16[2,256,1024]{2,1,0:T(8,128)(2,1)} %get-tuple-element.164), channel_id=1, source_target_pairs={{0,32},{32,0},{1,33},{33,1},{2,34},{34,2},{3,35},{35,3},{4,36},{36... | collective-permute-start | bytes 3145736 | tf_op jit(solution)/shard_map/ppermute | solution.py:644
  293.7 15.6 %collective-permute-start.38 = (bf16[256,1024]{1,0:T(8,128)(2,1)}, bf16[256,1024]{1,0:T(8,128)(2,1)}, u32[]{:S(2)}, u32[]{:S(2)}) collective-permute-start(bf16[256,1024]{1,0:T(8,128)(2,1)} %get-tuple-element.165), channel_id=1, source_target_pairs={{0,2},{1,3},{2,0},{3,1},{4,6},{5,7},{6,4},{7,5},{8,10},{9,11},{10,... | collective-permute-start | bytes 1572872 | tf_op jit(solution)/shard_map/ppermute | solution.py:644
  298.2 42.9 %all-to-all-start.3 = ((bf16[128,8,640]{2,1,0:T(8,128)(2,1)}), bf16[128,8,640]{2,1,0:T(8,128)(2,1)S(1)}, u32[]{:S(2)}, u32[]{:S(2)}) async-start(bf16[128,8,640]{2,1,0:T(8,128)(2,1)} %bitcast.78), calls=%async_computation.3 | async-start | bytes 2621440 | tf_op jit(solution)/shard_map/all_to_all | solution.py:758
  306.9 24.7 %collective-permute-start.37 = (bf16[256,1024]{1,0:T(8,128)(2,1)S(1)}, bf16[256,1024]{1,0:T(8,128)(2,1)S(1)}, u32[]{:S(2)}, u32[]{:S(2)}) collective-permute-start(bf16[256,1024]{1,0:T(8,128)(2,1)S(1)} %select_bitcast_fusion), channel_id=1, source_target_pairs={{0,64},{64,0},{1,65},{65,1},{2,66},{66,2},{3,67},{67,3},{4,68},{68... | collective-permute-start | bytes 1572872 | tf_op jit(solution)/shard_map/ppermute | solution.py:644
  (47 other events, 306.6 us)
Sparse Core Ops, SparseCore 0:
  21.1 120.1 all-gather.2
  199.8 100.7 reduce-scatter.1

commit v4 on v3

--- a/solution.py
+++ b/solution.py
@@ -404,11 +404,6 @@
     return e / jnp.sum(e, axis=-1, keepdims=True)
 
 
-def split(values):
-    high = values.astype(bf16)
-    return high, (values - high.astype(f32)).astype(bf16)
-
-
 def whole(*shape):
     return pl.BlockSpec(shape, lambda e: (0,) * len(shape))
 
@@ -445,9 +440,7 @@
     rows_ref[:, 0] = dot(place, values[...]).astype(bf16).reshape(SHARE, CAP, D)
     if with_gates:
         table = gate_table(dot(values[...], router_ref[:, :EXPERTS]), slots.astype(f32))
-        high, low = split(table)
-        both = dot(place, high) + dot(place, low)
-        gate = jnp.sum(both * own[...].astype(f32), axis=1, keepdims=True)
+        gate = jnp.sum(dot(place, table.astype(bf16)) * own[...].astype(f32), axis=1, keepdims=True)
         gates_ref[:, 0] = gate.reshape(SHARE, CAP, 1)
 
 
@@ -546,8 +539,7 @@
                 b = 2 * j + c
                 place = as_bf16(dot(codes_kept[b][:, :EXPERTS], spread[...]) == start[...])
                 out[j, :, :D] = dot(place, kept[b].reshape(SLOTS, D)).astype(bf16)
-                high, low = split(mine[...] * dgates[b].reshape(SLOTS, 1))
-                scattered = dot(place, high) + dot(place, low)
+                scattered = dot(place, (mine[...] * dgates[b].reshape(SLOTS, 1)).astype(bf16))
                 out[j, :, D:] = jnp.concatenate([scattered, jnp.zeros((TOK, 128 - EXPERTS), f32)], axis=1).astype(bf16)
             return carry
 
@@ -684,28 +676,28 @@
     own = tokens.reshape(TOK, D)
     across = swap(own, "ylo")
     gy_own = with_codes(routes.reshape(TOK, TOPK), cotangent.reshape(TOK, D))
-    gy_blocks = gather_z(gy_own)
-
     packed, keep, send = pack(
         place, query_weight, key_weight, value_weight, router_weight, norm1_gain.reshape(1, 8), norm2_gain.reshape(1, 8),
         expert_gate.reshape(TOK, FF), expert_up.reshape(TOK, FF),
     )
 
-    expert_w = assemble(place, keep, swap(send, "core"), expert_down.reshape(128, D))
-    expert_w, packed, across = fence(expert_w, packed, across)
-    expert_w = lax.all_gather(expert_w, PLANE, axis=0).reshape(16, 1536, 256)
-
-    arrived = lax.all_to_all(packed, AXES, split_axis=0, concat_axis=0, tiled=True).reshape(D, 640)
-    beside = swap(own, "core")
-
     lane = jnp.arange(128) % 32
     angles = jnp.arange(LENGTH).astype(f32)[:, None] * (rope_base ** (-2.0 * lane.astype(f32) / HEAD))[None, :]
-    cos, sin = fence(jnp.cos(angles), jnp.sin(angles))
+    output_rows = jnp.concatenate([output_weight, swap(output_weight, "ylo")], axis=1)
+    expert_w = assemble(place, keep, swap(send, "core"), expert_down.reshape(128, D))
+    packed, across, cos, sin, gy_own, output_rows, expert_w = fence(
+        packed, across, jnp.cos(angles), jnp.sin(angles), gy_own, output_rows, expert_w
+    )
+    arrived = lax.all_to_all(packed, AXES, split_axis=0, concat_axis=0, tiled=True).reshape(D, 640)
+    gy_blocks = gather_z(gy_own)
+    beside = swap(own, "core")
+
+    expert_w, arrived, beside = fence(expert_w, arrived, beside)
+    expert_w = lax.all_gather(expert_w, PLANE, axis=0).reshape(16, 1536, 256)
+
     blocks = [own, across, beside, swap(across, "core")]
     q, k, v, *mixed, lse, hidden_all, gains = front(place, blocks, arrived, cos, sin)
 
-    output_rows = jnp.concatenate([output_weight, swap(output_weight, "ylo")], axis=1)
-    output_rows, _ = fence(output_rows, arrived)
     output_own = lax.all_to_all(
         jnp.broadcast_to(output_rows[None], (32, 8, 2 * D)), FSDP, split_axis=0, concat_axis=0, tiled=True
     ).reshape(TOK, 2 * D)
@@ -753,9 +745,9 @@
     pair = (keep.astype(f32) + swap(send, "core").astype(f32)).astype(bf16)
     kept = jnp.where(ylo == 0, pair[0], pair[1])
     got = swap(jnp.where(ylo == 0, pair[1], pair[0]), "ylo")
-    got, moe_far = fence(got, shift(moe_sums[3], "z", 2))
+    first = lax.all_to_all(first.reshape(128, 8, 640), AXES, split_axis=0, concat_axis=0, tiled=True)
+    first, got, moe_far, grad_gate, grad_up, grad_down = fence(first, got, shift(moe_sums[3], "z", 2), *finished)
     grad_hidden_one = kept.astype(f32) + got.astype(f32)
-    first = lax.all_to_all(first.reshape(128, 8, 640), AXES, split_axis=0, concat_axis=0, tiled=True)
     grad_output = jnp.sum(grad_output.astype(f32), axis=0)
     layer_out = sum(part.astype(f32) for part in (moe_sums[0], *moe_near, moe_far))
     layer_out = (residual + layer_out).astype(bf16).reshape(1, TOK, D)
@@ -767,9 +759,6 @@
         scaled - normed_one * jnp.mean(scaled * normed_one, axis=-1, keepdims=True)
     )
 
-    first, layer_out, grad_inputs, grad_output, grad_gate, grad_up, grad_down = fence(
-        first, layer_out, grad_inputs, grad_output, *finished
-    )
     first = jnp.sum(first.astype(f32).reshape(4, 32, 8, 640), axis=1)
     grad_query = first[:, :, :256].transpose(1, 0, 2).reshape(8, D)
     grad_key = first[:, :, 256:384].transpose(1, 0, 2).reshape(8, 512)

time: 355 us -> 355 us (level)
  starting transfers between devices: 76.8 us -> 70.3 us
  waiting for transfers between devices: 88.3 us -> 93.7 us
    all_to_all x1, waiting for transfers between devices: 0.01 us -> 9.59 us  [on_device(): lax.all_to_all(first.reshape(128, 8, 640), AXES, split_axis=0, concat_axi...]
    unnamed x67 -> x73, local copies, waits for them, and re-layouts: 6.57 us -> 8.65 us
  transfers between devices with their start and end apart: 46 -> 46, of which waited for: 15 -> 17; matrix products, arithmetic and copies ran while one was open for 6% -> 5% of each run, Pallas kernels for 28% -> 27%
where the time goes in v4:
time: 355 us; the launch traced here: 350 us
  Pallas kernels  139 us (39%)
  waiting for transfers between devices  93.7 us (26%)
  starting transfers between devices  70.3 us (20%)
  other arithmetic  20.2 us (6%)
  between operations  14.6 us (4%)
  local copies, waits for them, and re-layouts  12.4 us (3%)
    ppermute x40, waiting for transfers between devices, shift(): return lax.ppermute(values, axis, [(i, (i + by) % n) for i in range(n)])  66.2 us
    pallas_call x1, Pallas kernels, main(): call(main_kernel, 'experts', 25000000000, 60000000, grid=(SHARE,), in_spe...  41.3 us
    ppermute x40, starting transfers between devices, shift(): return lax.ppermute(values, axis, [(i, (i + by) % n) for i in range(n)])  39.7 us
    pallas_call x3, Pallas kernels, rows_of(): call(functools.partial(rows_kernel, n, with_gates), 'rows', n * 750000000...  28.4 us
    all_to_all x1, waiting for transfers between devices, on_device(): lax.all_to_all(packed, AXES, split_axis=0, concat_axis=0, tiled=True)  17.9 us
    pallas_call x1, Pallas kernels, back(): call(back_kernel, 'back', 20000000000, 16000000, in_specs=[SCALAR] + [VEC...  16.6 us
    pallas_call x1, Pallas kernels, outs(): call(outs_kernel, 'expert_outs', 6000000000, 12000000, grid=(SHARE,), in_...  14.6 us
    pallas_call x1, Pallas kernels, front(): call(front_kernel, 'front', 8000000000, 10000000, in_specs=[SCALAR] + [VE...  11.9 us
  transfers between devices with their start and end apart: 46, of which 17 were waited for; matrix products, arithmetic and copies ran while one was open for 5% of the time, Pallas kernels for 27%

profile of v4, /device:TPU:1, one launch (start us, length us, event | category | flops | bytes accessed | tf_op | source)
XLA Modules:
  0.0 350.0 jit_solution(8170028098333548648)
XLA Ops:
  13.1 3.1 multiply_sine_fusion
  20.2 5.6 %collective-permute-done.1 = bf16[8,1024]{1,0:T(8,128)(2,1)S(1)} collective-permute-done((bf16[8,1024]{1,0:T(8,128)(2,1)}, bf16[8,1024]{1,0:T(8,128)(2,1)S(1)}, u32[]{:S(2)}, u32[]{:S(2)}) %collective-permute-start.1) | collective-permute-done | bytes 16416 | tf_op jit(solution)/shard_map/ppermute | solution.py:636
  28.7 10.8 %all-to-all-start.1 = ((bf16[128,8,640]{2,1,0:T(8,128)(2,1)}), bf16[128,8,640]{2,1,0:T(8,128)(2,1)S(1)}, u32[]{:S(2)}, u32[]{:S(2)}) async-start(bf16[128,8,640]{2,1,0:T(8,128)(2,1)} %get-tuple-element.104), calls=%async_computation.1 | async-start | bytes 2621440 | tf_op jit(solution)/shard_map/all_to_all | solution.py:691
  42.4 17.9 %all-to-all-done.1 = bf16[128,8,640]{2,1,0:T(8,128)(2,1)S(1)} async-done(((bf16[128,8,640]{2,1,0:T(8,128)(2,1)}), bf16[128,8,640]{2,1,0:T(8,128)(2,1)S(1)}, u32[]{:S(2)}, u32[]{:S(2)}) %all-to-all-start.1) | async-done | bytes 1310752 | tf_op jit(solution)/shard_map/all_to_all | solution.py:691
  62.6 4.8 %all-to-all-start = ((bf16[32,8,2048]{2,1,0:T(8,128)(2,1)}), bf16[32,8,2048]{2,1,0:T(8,128)(2,1)S(1)}, u32[]{:S(2)}, u32[]{:S(2)}) async-start(bf16[32,8,2048]{2,1,0:T(8,128)(2,1)} %broadcast_in_dim.4), calls=%async_computation | async-start | bytes 2097152 | tf_op jit(solution)/shard_map/all_to_all | solution.py:701
  67.4 2.5 collective-permute-start.10
  71.6 11.9 %front.1 = (bf16[1024,256]{1,0:T(8,128)(2,1)}, bf16[1024,256]{1,0:T(8,128)(2,1)}, bf16[1024,256]{1,0:T(8,128)(2,1)}, bf16[256,256]{1,0:T(8,128)(2,1)}, bf16[256,...) custom-call(s32[2]{0:T(128)} %pad_add_fusion.place_ref, ...), custom_call_target="tpu_custom_call" | custom-call | flops 8000000000 | bytes 10000000 | tf_op jit(solution)/shard_map/front/pallas_call | solution.py:234
  85.0 7.9 %collective-permute-done.10.refs_4_.refs_8_ = bf16[256,1152]{1,0:T(8,128)(2,1)S(1)} collective-permute-done((bf16[256,1152]{1,0:T(8,128)(2,1)S(1)}, bf16[256,1152]{1,0:T(8,128)(2,1)S(1)}, u32[]{:S(2)}, u32[]{:S(2)}) %collective-permute-start.10) | collective-permute-done | bytes 589856 | tf_op jit(solution)/shard_map/ppermute | solution.py:636
  97.7 11.4 %collective-permute-done.9.refs_2_.refs_6_ = bf16[256,1152]{1,0:T(8,128)(2,1)} collective-permute-done((bf16[256,1152]{1,0:T(8,128)(2,1)S(1)}, bf16[256,1152]{1,0:T(8,128)(2,1)}, u32[]{:S(2)}, u32[]{:S(2)}) %collective-permute-start.9) | collective-permute-done | bytes 589856 | tf_op jit(solution)/shard_map/ppermute | solution.py:636
  111.5 2.8 collective-permute-done.12.other_ref
  115.2 3.9 %mid.1 = (f32[256,1024]{1,0:T(8,128)}, bf16[256,1024]{1,0:T(8,128)(2,1)}) custom-call(bf16[256,1024]{1,0:T(8,128)(2,1)} %bitcast.70, bf16[256,256]{1,0:T(8,128)(2,1)} %get-tuple-element.114.m0_ref, bf16[256,256]{1,0:T(8,128)(2,1)} %copy-done.27, bf16[256,256]{1,0:T(8,128)(2,1)} %copy-done.28, bf16[256,256]{1,0:T(8,128)(2,1)} %copy-done.29, ...), custom_call_target="tpu_custom_call" | custom-call | flops 1000000000 | bytes 5000000 | tf_op jit(solution)/shard_map/mid/pallas_call | solution.py:258
  123.6 10.6 %rows.3 = (bf16[8,8,80,1024]{3,2,1,0:T(8,128)(2,1)}, f32[8,128]{1,0:T(8,128)}) custom-call(s32[1]{0:T(128)} %bitcast.12.z_ref, bf16[256,1152]{1,0:T(8,128)(2,1)} %codes.1.refs_0_.refs_2_.gy_ref, bf16[256,1152]{1,0:T(8,128)(2,1)} %collective-permute-done.17.refs_1_.refs_3_, bf16[256,1152]{1,0:T(8,128)(2,1)} %collective-permute-done.9.refs_2_.refs_6_, ...), custom_call_target="tpu_custom_call" | custom-call | flops 6000000000 | bytes 16000000 | tf_op jit(solution)/shard_map/rows/pallas_call | solution.py:465
  135.1 5.6 %rows.4 = (bf16[8,8,80,1024]{3,2,1,0:T(8,128)(2,1)}, f32[8,8,80,1]{3,2,1,0:T(8,128)}, f32[8,128]{1,0:T(8,128)}) custom-call(s32[1]{0:T(128)} %bitcast.12.z_ref, bf16[256,1024]{1,0:T(8,128)(2,1)} %get-tuple-element.121.refs_0_, bf16[256,1024]{1,0:T(8,128)(2,1)} %copy-done.32, bf16[256,1152]{1,0:T(8,128)(2,1)} %codes.1.refs_0_.refs_2_.gy_ref, ...), custom_call_target="tpu_custom_call" | custom-call | flops 1500000000 | bytes 4000000 | tf_op jit(solution)/shard_map/rows/pallas_call | solution.py:465
  140.6 5.4 %collective-permute-done.15.refs_4_ = bf16[256,1024]{1,0:T(8,128)(2,1)S(1)} collective-permute-done((bf16[256,1024]{1,0:T(8,128)(2,1)}, bf16[256,1024]{1,0:T(8,128)(2,1)S(1)}, u32[]{:S(2)}, u32[]{:S(2)}) %collective-permute-start.15) | collective-permute-done | bytes 524320 | tf_op jit(solution)/shard_map/ppermute | solution.py:636
  150.9 12.2 %rows.5 = (bf16[8,8,80,1024]{3,2,1,0:T(8,128)(2,1)}, f32[8,8,80,1]{3,2,1,0:T(8,128)}, f32[8,128]{1,0:T(8,128)}) custom-call(s32[1]{0:T(128)} %bitcast.12.z_ref, bf16[256,1024]{1,0:T(8,128)(2,1)} %copy-done.19, bf16[256,1024]{1,0:T(8,128)(2,1)} %copy-done.22, bf16[256,1024]{1,0:T(8,128)(2,1)} %copy-done.20, ...), custom_call_target="tpu_custom_call", output_to_operand_aliasing={{0}: (15, {}), {1}: (16, {})} | custom-call | flops 4499999744 | bytes 12000000 | tf_op jit(solution)/shard_map/rows/pallas_call | solution.py:465
  163.1 41.3 %experts.1 = (bf16[8,640,256]{2,1,0:T(8,128)(2,1)}, bf16[8,2,768,512]{3,2,1,0:T(8,128)(2,1)}, bf16[4,256,1152]{2,1,0:T(8,128)(2,1)}, bf16[4,256,1152]{2,1,0:T(8,128)(2,1)}) custom-call(s32[1]{0:T(128)} %bitcast.12.z_ref, bf16[8,8,80,1024]{3,2,1,0:T(8,128)(2,1)} %get-tuple-element.135.x_ref, bf16[8,8,80,1024]{3,2,1,0:T(8,128)(2,1)} %get-tuple-element.136.gy_ref, ...), custom_call_target="tpu_custom_call" | custom-call | flops 24999999488 | bytes 60000000 | tf_op jit(solution)/shard_map/experts/pallas_call | solution.py:551
  204.8 4.4 %collective-permute-done.24 = bf16[4,256,1152]{2,1,0:T(8,128)(2,1)S(1)} collective-permute-done((bf16[4,256,1152]{2,1,0:T(8,128)(2,1)}, bf16[4,256,1152]{2,1,0:T(8,128)(2,1)S(1)}, u32[]{:S(2)}, u32[]{:S(2)}) %collective-permute-start.24) | collective-permute-done | bytes 2359328 | tf_op jit(solution)/shard_map/ppermute | solution.py:636
  214.8 14.6 %expert_outs.1 = (bf16[4,256,1024]{2,1,0:T(8,128)(2,1)}, bf16[4,256,1024]{2,1,0:T(8,128)(2,1)}) custom-call(s32[1]{0:T(128)} %bitcast.12.z_ref, bf16[8,640,256]{2,1,0:T(8,128)(2,1)} %get-tuple-element.144.act_ref, bf16[16,1536,256]{2,1,0:T(8,128)(2,1)} %bitcast.92, bf16[256,1152]{1,0:T(8,128)(2,1)} %codes.1.refs_0_.refs_2_.gy_ref, ...), custom_call_target="tpu_custom_call" | custom-call | flops 6000000000 | bytes 12000000 | tf_op jit(solution)/shard_map/expert_outs/pallas_call | solution.py:599
  230.7 9.6 %collective-permute-done.27.part3_ref = bf16[256,1152]{1,0:T(8,128)(2,1)S(1)} collective-permute-done((bf16[256,1152]{1,0:T(8,128)(2,1)S(1)}, bf16[256,1152]{1,0:T(8,128)(2,1)S(1)}, u32[]{:S(2)}, u32[]{:S(2)}) %collective-permute-start.27) | collective-permute-done | bytes 589856 | tf_op jit(solution)/shard_map/ppermute | solution.py:636
  241.1 8.0 %turn.1 = (bf16[256,256]{1,0:T(8,128)(2,1)}, bf16[256,256]{1,0:T(8,128)(2,1)}, bf16[256,256]{1,0:T(8,128)(2,1)}, bf16[256,256]{1,0:T(8,128)(2,1)}, f32[256,1024]...) custom-call(s32[2]{0:T(128)} %pad_add_fusion.place_ref, ...), custom_call_target="tpu_custom_call" | custom-call | flops 2000000000 | bytes 10000000 | tf_op jit(solution)/shard_map/turn/pallas_call | solution.py:299
  249.1 2.6 collective-permute-start.28
  253.8 6.1 %collective-permute-done.32 = bf16[256,256]{1,0:T(8,128)(2,1)} collective-permute-done((bf16[256,256]{1,0:T(8,128)(2,1)}, bf16[256,256]{1,0:T(8,128)(2,1)}, u32[]{:S(2)}, u32[]{:S(2)}) %collective-permute-start.32) | collective-permute-done | bytes 131104 | tf_op jit(solution)/shard_map/ppermute | solution.py:636
  261.1 2.6 add_convert_fusion.1
  267.2 8.0 %all-to-all-start.2 = ((bf16[64,8,1024]{2,1,0:T(8,128)(2,1)}), bf16[64,8,1024]{2,1,0:T(8,128)(2,1)S(1)}, u32[]{:S(2)}, u32[]{:S(2)}) async-start(bf16[64,8,1024]{2,1,0:T(8,128)(2,1)} %bitcast.18), calls=%async_computation.2 | async-start | bytes 2097152 | tf_op jit(solution)/shard_map/all_to_all | solution.py:737
  275.9 16.6 %back.1 = (bf16[1024,512]{1,0:T(8,128)(2,1)}, bf16[2,256,1024]{2,1,0:T(8,128)(2,1)}, bf16[2,256,1024]{2,1,0:T(8,128)(2,1)}, f32[8,1024]{1,0:T(8,128)}) custom-call(s32[2]{0:T(128)} %pad_add_fusion.place_ref, bf16[1024,256]{1,0:T(8,128)(2,1)} %get-tuple-element.148.q_ref, bf16[1024,256]{1,0:T(8,128)(2,1)} %get-tuple-element.149.k_ref, ...), custom_call_target="tpu_custom_call" | custom-call | flops 20000000000 | bytes 16000000 | tf_op jit(solution)/shard_map/back/pallas_call | solution.py:363
  292.6 4.3 %collective-permute-start.36 = (bf16[2,256,1024]{2,1,0:T(8,128)(2,1)}, bf16[2,256,1024]{2,1,0:T(8,128)(2,1)}, u32[]{:S(2)}, u32[]{:S(2)}) collective-permute-start(bf16[2,256,1024]{2,1,0:T(8,128)(2,1)} %get-tuple-element.169), channel_id=1, source_target_pairs={{0,32},{32,0},{1,33},{33,1},{2,34},{34,2},{3,35},{35,3},{4,36},{36... | collective-permute-start | bytes 3145736 | tf_op jit(solution)/shard_map/ppermute | solution.py:636
  297.6 4.4 %projections.1 = bf16[1024,640]{1,0:T(8,128)(2,1)} custom-call(bf16[1024,1024]{1,0:T(8,128)(2,1)} %get-tuple-element.164.h_ref, bf16[1024,512]{1,0:T(8,128)(2,1)} %get-tuple-element.165.dqkv_ref, f32[1024,128]{1,0:T(8,128)} %get-tuple-element.166.sums_ref, f32[8,1024]{1,0:T(8,128)} %get-tuple-element.167.gain_ref), custom_call_target="tpu_custom_call" | custom-call | flops 1500000000 | bytes 5000000 | tf_op jit(solution)/shard_map/projections/pallas_call | solution.py:380
  302.1 6.9 %all-to-all-start.3 = ((bf16[128,8,640]{2,1,0:T(8,128)(2,1)}), bf16[128,8,640]{2,1,0:T(8,128)(2,1)S(1)}, u32[]{:S(2)}, u32[]{:S(2)}) async-start(bf16[128,8,640]{2,1,0:T(8,128)(2,1)} %bitcast.79), calls=%async_computation.3 | async-start | bytes 2621440 | tf_op jit(solution)/shard_map/all_to_all | solution.py:748
  317.7 2.5 finish.1
  320.2 9.6 %all-to-all-done.3 = bf16[128,8,640]{2,1,0:T(8,128)(2,1)S(1)} async-done(((bf16[128,8,640]{2,1,0:T(8,128)(2,1)}), bf16[128,8,640]{2,1,0:T(8,128)(2,1)S(1)}, u32[]{:S(2)}, u32[]{:S(2)}) %all-to-all-start.3) | async-done | bytes 1310752 | tf_op jit(solution)/shard_map/all_to_all | solution.py:748
  329.8 6.1 %collective-permute-done.37 = bf16[256,1024]{1,0:T(8,128)(2,1)} collective-permute-done((bf16[256,1024]{1,0:T(8,128)(2,1)}, bf16[256,1024]{1,0:T(8,128)(2,1)}, u32[]{:S(2)}, u32[]{:S(2)}) %collective-permute-start.37) | collective-permute-done | bytes 524320 | tf_op jit(solution)/shard_map/ppermute | solution.py:636
  339.5 3.4 fusion.6
  (173 shorter events, 68.0 us)
Async XLA Ops:
  10.2 15.6 %collective-permute-start.2 = (bf16[2,256,256]{2,1,0:T(8,128)(2,1)}, bf16[2,256,256]{2,1,0:T(8,128)(2,1)S(1)}, u32[]{:S(2)}, u32[]{:S(2)}) collective-permute-start(bf16[2,256,256]{2,1,0:T(8,128)(2,1)} %get-tuple-element.100), channel_id=1, source_target_pairs={{0,32},{32,0},{1,33},{33,1},{2,34},{34,2},{3,35},{35,3},{4,36},{36... | collective-permute-start | bytes 786440 | tf_op jit(solution)/shard_map/ppermute | solution.py:636
  11.6 17.0 %collective-permute-start = (bf16[256,1024]{1,0:T(8,128)(2,1)}, bf16[256,1024]{1,0:T(8,128)(2,1)}, u32[]{:S(2)}, u32[]{:S(2)}) collective-permute-start(bf16[256,1024]{1,0:T(8,128)(2,1)} %bitcast.68), channel_id=1, source_target_pairs={{0,64},{64,0},{1,65},{65,1},{2,66},{66,2},{3,67},{67,3},{4,68},{68... | collective-permute-start | bytes 1572872 | tf_op jit(solution)/shard_map/ppermute | solution.py:636
  13.0 12.8 %collective-permute-start.1 = (bf16[8,1024]{1,0:T(8,128)(2,1)}, bf16[8,1024]{1,0:T(8,128)(2,1)S(1)}, u32[]{:S(2)}, u32[]{:S(2)}) collective-permute-start(bf16[8,1024]{1,0:T(8,128)(2,1)} %param.18), channel_id=1, source_target_pairs={{0,64},{64,0},{1,65},{65,1},{2,66},{66,2},{3,67},{67,3},{4,68},{68... | collective-permute-start | bytes 49160 | tf_op jit(solution)/shard_map/ppermute | solution.py:636
  28.7 31.6 %all-to-all-start.1 = ((bf16[128,8,640]{2,1,0:T(8,128)(2,1)}), bf16[128,8,640]{2,1,0:T(8,128)(2,1)S(1)}, u32[]{:S(2)}, u32[]{:S(2)}) async-start(bf16[128,8,640]{2,1,0:T(8,128)(2,1)} %get-tuple-element.104), calls=%async_computation.1 | async-start | bytes 2621440 | tf_op jit(solution)/shard_map/all_to_all | solution.py:691
  39.5 123.6 %all-gather.3.cloned.1.call-start = ((), (), s32[]{:S(2)}) async-start(), calls=%async_computation.6 | async-start | bytes 13369344 | tf_op jit(solution)/shard_map/all_gather | solution.py:696
  62.6 46.6 %all-to-all-start = ((bf16[32,8,2048]{2,1,0:T(8,128)(2,1)}), bf16[32,8,2048]{2,1,0:T(8,128)(2,1)S(1)}, u32[]{:S(2)}, u32[]{:S(2)}) async-start(bf16[32,8,2048]{2,1,0:T(8,128)(2,1)} %broadcast_in_dim.4), calls=%async_computation | async-start | bytes 2097152 | tf_op jit(solution)/shard_map/all_to_all | solution.py:701
  67.3 246.7 %reduce-scatter.2.cloned.1.call-start = ((), (), s32[]{:S(2)}) async-start(), calls=%async_computation.5 | async-start | bytes 13369344 | tf_op jit(solution)/shard_map/reduce_scatter | solution.py:726
  67.4 25.6 %collective-permute-start.10 = (bf16[256,1152]{1,0:T(8,128)(2,1)S(1)}, bf16[256,1152]{1,0:T(8,128)(2,1)S(1)}, u32[]{:S(2)}, u32[]{:S(2)}) collective-permute-start(bf16[256,1152]{1,0:T(8,128)(2,1)S(1)} %copy-done.5), channel_id=1, source_target_pairs={{0,3},{1,0},{2,1},{3,2},{4,7},{5,4},{6,5},{7,6},{8,11},{9,8},{10,9... | collective-permute-start | bytes 1769480 | tf_op jit(solution)/shard_map/ppermute | solution.py:636
  69.9 27.0 %collective-permute-start.11 = (bf16[256,1152]{1,0:T(8,128)(2,1)S(1)}, bf16[256,1152]{1,0:T(8,128)(2,1)S(1)}, u32[]{:S(2)}, u32[]{:S(2)}) collective-permute-start(bf16[256,1152]{1,0:T(8,128)(2,1)S(1)} %copy-done.5), channel_id=1, source_target_pairs={{0,2},{1,3},{2,0},{3,1},{4,6},{5,7},{6,4},{7,5},{8,10},{9,11},{10,... | collective-permute-start | bytes 1769480 | tf_op jit(solution)/shard_map/ppermute | solution.py:636
  70.5 38.7 %collective-permute-start.9 = (bf16[256,1152]{1,0:T(8,128)(2,1)S(1)}, bf16[256,1152]{1,0:T(8,128)(2,1)}, u32[]{:S(2)}, u32[]{:S(2)}) collective-permute-start(bf16[256,1152]{1,0:T(8,128)(2,1)S(1)} %copy-done.5), channel_id=1, source_target_pairs={{0,1},{1,2},{2,3},{3,0},{4,5},{5,6},{6,7},{7,4},{8,9},{9,10},{10,1... | collective-permute-start | bytes 1769480 | tf_op jit(solution)/shard_map/ppermute | solution.py:636
  83.7 25.5 %collective-permute-start.5 = (bf16[256,256]{1,0:T(8,128)(2,1)}, bf16[256,256]{1,0:T(8,128)(2,1)S(1)}, u32[]{:S(2)}, u32[]{:S(2)}) collective-permute-start(bf16[256,256]{1,0:T(8,128)(2,1)} %get-tuple-element.110), channel_id=1, source_target_pairs={{0,64},{64,0},{1,65},{65,1},{2,66},{66,2},{3,67},{67,3},{4,68},{68... | collective-permute-start | bytes 393224 | tf_op jit(solution)/shard_map/ppermute | solution.py:636
  93.0 16.2 %collective-permute-start.6 = (bf16[256,256]{1,0:T(8,128)(2,1)}, bf16[256,256]{1,0:T(8,128)(2,1)S(1)}, u32[]{:S(2)}, u32[]{:S(2)}) collective-permute-start(bf16[256,256]{1,0:T(8,128)(2,1)} %get-tuple-element.111), channel_id=1, source_target_pairs={{0,32},{32,0},{1,33},{33,1},{2,34},{34,2},{3,35},{35,3},{4,36},{36... | collective-permute-start | bytes 393224 | tf_op jit(solution)/shard_map/ppermute | solution.py:636
  95.1 14.1 %collective-permute-start.8 = (bf16[256,256]{1,0:T(8,128)(2,1)S(1)}, bf16[256,256]{1,0:T(8,128)(2,1)S(1)}, u32[]{:S(2)}, u32[]{:S(2)}) collective-permute-start(bf16[256,256]{1,0:T(8,128)(2,1)S(1)} %collective-permute-done.7), channel_id=1, source_target_pairs={{0,32},{32,0},{1,33},{33,1},{2,34},{34,2},{3,35},{35,3},{4,36},{36... | collective-permute-start | bytes 393224 | tf_op jit(solution)/shard_map/ppermute | solution.py:636
  119.1 15.1 %collective-permute-start.16 = (bf16[256,1024]{1,0:T(8,128)(2,1)}, bf16[256,1024]{1,0:T(8,128)(2,1)S(1)}, u32[]{:S(2)}, u32[]{:S(2)}) collective-permute-start(bf16[256,1024]{1,0:T(8,128)(2,1)} %get-tuple-element.121.refs_0_), channel_id=1, source_target_pairs={{0,32},{32,0},{1,33},{33,1},{2,34},{34,2},{3,35},{35,3},{4,36},{36... | collective-permute-start | bytes 1572872 | tf_op jit(solution)/shard_map/ppermute | solution.py:636
  119.4 21.2 %collective-permute-start.13 = (bf16[256,1024]{1,0:T(8,128)(2,1)}, bf16[256,1024]{1,0:T(8,128)(2,1)S(1)}, u32[]{:S(2)}, u32[]{:S(2)}) collective-permute-start(bf16[256,1024]{1,0:T(8,128)(2,1)} %get-tuple-element.121.refs_0_), channel_id=1, source_target_pairs={{0,1},{1,2},{2,3},{3,0},{4,5},{5,6},{6,7},{7,4},{8,9},{9,10},{10,1... | collective-permute-start | bytes 1572872 | tf_op jit(solution)/shard_map/ppermute | solution.py:636
  119.8 20.8 %collective-permute-start.14 = (bf16[256,1024]{1,0:T(8,128)(2,1)}, bf16[256,1024]{1,0:T(8,128)(2,1)S(1)}, u32[]{:S(2)}, u32[]{:S(2)}) collective-permute-start(bf16[256,1024]{1,0:T(8,128)(2,1)} %get-tuple-element.121.refs_0_), channel_id=1, source_target_pairs={{0,3},{1,0},{2,1},{3,2},{4,7},{5,4},{6,5},{7,6},{8,11},{9,8},{10,9... | collective-permute-start | bytes 1572872 | tf_op jit(solution)/shard_map/ppermute | solution.py:636
  122.3 23.7 %collective-permute-start.15 = (bf16[256,1024]{1,0:T(8,128)(2,1)}, bf16[256,1024]{1,0:T(8,128)(2,1)S(1)}, u32[]{:S(2)}, u32[]{:S(2)}) collective-permute-start(bf16[256,1024]{1,0:T(8,128)(2,1)} %get-tuple-element.121.refs_0_), channel_id=1, source_target_pairs={{0,2},{1,3},{2,0},{3,1},{4,6},{5,7},{6,4},{7,5},{8,10},{9,11},{10,... | collective-permute-start | bytes 1572872 | tf_op jit(solution)/shard_map/ppermute | solution.py:636
  210.7 20.0 %collective-permute-start.25 = (bf16[256,1152]{1,0:T(8,128)(2,1)S(1)}, bf16[256,1152]{1,0:T(8,128)(2,1)S(1)}, u32[]{:S(2)}, u32[]{:S(2)}) collective-permute-start(bf16[256,1152]{1,0:T(8,128)(2,1)S(1)} %get-tuple-element.188), channel_id=1, source_target_pairs={{0,3},{1,0},{2,1},{3,2},{4,7},{5,4},{6,5},{7,6},{8,11},{9,8},{10,9... | collective-permute-start | bytes 1769480 | tf_op jit(solution)/shard_map/ppermute | solution.py:636
  213.1 17.7 %collective-permute-start.26 = (bf16[256,1152]{1,0:T(8,128)(2,1)S(1)}, bf16[256,1152]{1,0:T(8,128)(2,1)S(1)}, u32[]{:S(2)}, u32[]{:S(2)}) collective-permute-start(bf16[256,1152]{1,0:T(8,128)(2,1)S(1)} %get-tuple-element.187), channel_id=1, source_target_pairs={{0,1},{1,2},{2,3},{3,0},{4,5},{5,6},{6,7},{7,4},{8,9},{9,10},{10,1... | collective-permute-start | bytes 1769480 | tf_op jit(solution)/shard_map/ppermute | solution.py:636
  213.3 27.0 %collective-permute-start.27 = (bf16[256,1152]{1,0:T(8,128)(2,1)S(1)}, bf16[256,1152]{1,0:T(8,128)(2,1)S(1)}, u32[]{:S(2)}, u32[]{:S(2)}) collective-permute-start(bf16[256,1152]{1,0:T(8,128)(2,1)S(1)} %get-tuple-element.186), channel_id=1, source_target_pairs={{0,2},{1,3},{2,0},{3,1},{4,6},{5,7},{6,4},{7,5},{8,10},{9,11},{10,... | collective-permute-start | bytes 1769480 | tf_op jit(solution)/shard_map/ppermute | solution.py:636
  229.5 34.2 %collective-permute-start.29 = (bf16[4,256,1024]{2,1,0:T(8,128)(2,1)}, bf16[4,256,1024]{2,1,0:T(8,128)(2,1)S(1)}, u32[]{:S(2)}, u32[]{:S(2)}) collective-permute-start(bf16[4,256,1024]{2,1,0:T(8,128)(2,1)} %get-tuple-element.146), channel_id=1, source_target_pairs={{0,32},{32,0},{1,33},{33,1},{2,34},{34,2},{3,35},{35,3},{4,36},{36... | collective-permute-start | bytes 6291464 | tf_op jit(solution)/shard_map/ppermute | solution.py:636
  249.1 12.1 %collective-permute-start.28 = (bf16[2,256,1024]{2,1,0:T(8,128)(2,1)}, bf16[2,256,1024]{2,1,0:T(8,128)(2,1)S(1)}, u32[]{:S(2)}, u32[]{:S(2)}) collective-permute-start(bf16[2,256,1024]{2,1,0:T(8,128)(2,1)} %get-tuple-element.142), channel_id=1, source_target_pairs={{0,32},{32,0},{1,33},{33,1},{2,34},{34,2},{3,35},{35,3},{4,36},{36... | collective-permute-start | bytes 3145736 | tf_op jit(solution)/shard_map/ppermute | solution.py:636
  252.8 22.4 %collective-permute-start.30 = (bf16[256,256]{1,0:T(8,128)(2,1)}, bf16[256,256]{1,0:T(8,128)(2,1)S(1)}, u32[]{:S(2)}, u32[]{:S(2)}) collective-permute-start(bf16[256,256]{1,0:T(8,128)(2,1)} %get-tuple-element.152), channel_id=1, source_target_pairs={{0,64},{64,0},{1,65},{65,1},{2,66},{66,2},{3,67},{67,3},{4,68},{68... | collective-permute-start | bytes 393224 | tf_op jit(solution)/shard_map/ppermute | solution.py:636
  253.2 22.0 %collective-permute-start.31 = (bf16[256,256]{1,0:T(8,128)(2,1)}, bf16[256,256]{1,0:T(8,128)(2,1)S(1)}, u32[]{:S(2)}, u32[]{:S(2)}) collective-permute-start(bf16[256,256]{1,0:T(8,128)(2,1)} %get-tuple-element.153), channel_id=1, source_target_pairs={{0,32},{32,0},{1,33},{33,1},{2,34},{34,2},{3,35},{35,3},{4,36},{36... | collective-permute-start | bytes 393224 | tf_op jit(solution)/shard_map/ppermute | solution.py:636
  259.9 15.3 %collective-permute-start.33 = (bf16[256,256]{1,0:T(8,128)(2,1)}, bf16[256,256]{1,0:T(8,128)(2,1)S(1)}, u32[]{:S(2)}, u32[]{:S(2)}) collective-permute-start(bf16[256,256]{1,0:T(8,128)(2,1)} %collective-permute-done.32), channel_id=1, source_target_pairs={{0,32},{32,0},{1,33},{33,1},{2,34},{34,2},{3,35},{35,3},{4,36},{36... | collective-permute-start | bytes 393224 | tf_op jit(solution)/shard_map/ppermute | solution.py:636
  265.7 26.8 %collective-permute-start.34 = (bf16[256,1024]{1,0:T(8,128)(2,1)}, bf16[256,1024]{1,0:T(8,128)(2,1)S(1)}, u32[]{:S(2)}, u32[]{:S(2)}) collective-permute-start(bf16[256,1024]{1,0:T(8,128)(2,1)} %get-tuple-element.160), channel_id=1, source_target_pairs={{0,3},{1,0},{2,1},{3,2},{4,7},{5,4},{6,5},{7,6},{8,11},{9,8},{10,9... | collective-permute-start | bytes 1572872 | tf_op jit(solution)/shard_map/ppermute | solution.py:636
  265.7 26.8 %collective-permute-start.35 = (bf16[256,1024]{1,0:T(8,128)(2,1)S(1)}, bf16[256,1024]{1,0:T(8,128)(2,1)S(1)}, u32[]{:S(2)}, u32[]{:S(2)}) collective-permute-start(bf16[256,1024]{1,0:T(8,128)(2,1)S(1)} %get-tuple-element.161), channel_id=1, source_target_pairs={{0,1},{1,2},{2,3},{3,0},{4,5},{5,6},{6,7},{7,4},{8,9},{9,10},{10,1... | collective-permute-start | bytes 1572872 | tf_op jit(solution)/shard_map/ppermute | solution.py:636
  267.2 25.4 %all-to-all-start.2 = ((bf16[64,8,1024]{2,1,0:T(8,128)(2,1)}), bf16[64,8,1024]{2,1,0:T(8,128)(2,1)S(1)}, u32[]{:S(2)}, u32[]{:S(2)}) async-start(bf16[64,8,1024]{2,1,0:T(8,128)(2,1)} %bitcast.18), calls=%async_computation.2 | async-start | bytes 2097152 | tf_op jit(solution)/shard_map/all_to_all | solution.py:737
  292.6 17.2 %collective-permute-start.36 = (bf16[2,256,1024]{2,1,0:T(8,128)(2,1)}, bf16[2,256,1024]{2,1,0:T(8,128)(2,1)}, u32[]{:S(2)}, u32[]{:S(2)}) collective-permute-start(bf16[2,256,1024]{2,1,0:T(8,128)(2,1)} %get-tuple-element.169), channel_id=1, source_target_pairs={{0,32},{32,0},{1,33},{33,1},{2,34},{34,2},{3,35},{35,3},{4,36},{36... | collective-permute-start | bytes 3145736 | tf_op jit(solution)/shard_map/ppermute | solution.py:636
  297.6 22.6 %collective-permute-start.38 = (bf16[256,1024]{1,0:T(8,128)(2,1)}, bf16[256,1024]{1,0:T(8,128)(2,1)}, u32[]{:S(2)}, u32[]{:S(2)}) collective-permute-start(bf16[256,1024]{1,0:T(8,128)(2,1)} %get-tuple-element.170), channel_id=1, source_target_pairs={{0,2},{1,3},{2,0},{3,1},{4,6},{5,7},{6,4},{7,5},{8,10},{9,11},{10,... | collective-permute-start | bytes 1572872 | tf_op jit(solution)/shard_map/ppermute | solution.py:636
  302.1 27.7 %all-to-all-start.3 = ((bf16[128,8,640]{2,1,0:T(8,128)(2,1)}), bf16[128,8,640]{2,1,0:T(8,128)(2,1)S(1)}, u32[]{:S(2)}, u32[]{:S(2)}) async-start(bf16[128,8,640]{2,1,0:T(8,128)(2,1)} %bitcast.79), calls=%async_computation.3 | async-start | bytes 2621440 | tf_op jit(solution)/shard_map/all_to_all | solution.py:748
  312.7 23.2 %collective-permute-start.37 = (bf16[256,1024]{1,0:T(8,128)(2,1)}, bf16[256,1024]{1,0:T(8,128)(2,1)}, u32[]{:S(2)}, u32[]{:S(2)}) collective-permute-start(bf16[256,1024]{1,0:T(8,128)(2,1)} %select_bitcast_fusion), channel_id=1, source_target_pairs={{0,64},{64,0},{1,65},{65,1},{2,66},{66,2},{3,67},{67,3},{4,68},{68... | collective-permute-start | bytes 1572872 | tf_op jit(solution)/shard_map/ppermute | solution.py:636
  (50 other events, 353.6 us)
Sparse Core Ops, SparseCore 0:
  60.4 101.8 all-gather.2
  204.5 100.2 reduce-scatter.1

commit v5 on v4

--- a/solution.py
+++ b/solution.py
@@ -681,19 +681,18 @@
         expert_gate.reshape(TOK, FF), expert_up.reshape(TOK, FF),
     )
 
+    expert_w = assemble(place, keep, swap(send, "core"), expert_down.reshape(128, D))
     lane = jnp.arange(128) % 32
     angles = jnp.arange(LENGTH).astype(f32)[:, None] * (rope_base ** (-2.0 * lane.astype(f32) / HEAD))[None, :]
+    expert_w, packed, across, cos, sin = fence(expert_w, packed, across, jnp.cos(angles), jnp.sin(angles))
+    expert_w = lax.all_gather(expert_w, PLANE, axis=0).reshape(16, 1536, 256)
+
+    arrived = lax.all_to_all(packed, AXES, split_axis=0, concat_axis=0, tiled=True).reshape(D, 640)
     output_rows = jnp.concatenate([output_weight, swap(output_weight, "ylo")], axis=1)
-    expert_w = assemble(place, keep, swap(send, "core"), expert_down.reshape(128, D))
-    packed, across, cos, sin, gy_own, output_rows, expert_w = fence(
-        packed, across, jnp.cos(angles), jnp.sin(angles), gy_own, output_rows, expert_w
-    )
-    arrived = lax.all_to_all(packed, AXES, split_axis=0, concat_axis=0, tiled=True).reshape(D, 640)
     gy_blocks = gather_z(gy_own)
+    arrived, output_rows, *near = fence(arrived, output_rows, *gy_blocks[1:3])
+    gy_blocks[1:3] = near
     beside = swap(own, "core")
-
-    expert_w, arrived, beside = fence(expert_w, arrived, beside)
-    expert_w = lax.all_gather(expert_w, PLANE, axis=0).reshape(16, 1536, 256)
 
     blocks = [own, across, beside, swap(across, "core")]
     q, k, v, *mixed, lse, hidden_all, gains = front(place, blocks, arrived, cos, sin)
@@ -709,13 +708,16 @@
     gy_blocks = [block for pair in with_core(gy_blocks) for block in pair]
     residual, hidden_two = mid(own, mixed, output_own, output_other, gains)
 
-    h_blocks = gather_z(hidden_two)
+    near = [shift(hidden_two, "z", 1), shift(hidden_two, "z", -1)]
     turn, _ = fence(jnp.zeros((8, 128), f32), hidden_two)
     gy_rows, turn = rows_of(z, 0, gy_blocks, None, None, None, turn)
+    *near, far, turn = fence(*near, hidden_two, turn)
+    far = shift(far, "z", 2)
     rows, turn = rows_of(z, 0, (hidden_two, swap(hidden_two, "core")), gy_blocks[:2], arrived, None, turn)
-    *h_blocks, turn = fence(*h_blocks, turn)
-    h_blocks = [block for pair in with_core(h_blocks[1:]) for block in pair]
-    rows, turn = rows_of(z, 2, h_blocks, gy_blocks[2:], arrived, rows, turn)
+    near = [block for pair in with_core(near) for block in pair]
+    rows, turn = rows_of(z, 2, near, gy_blocks[2:6], arrived, rows, turn)
+    far, turn = fence(far, turn)
+    rows, turn = rows_of(z, 6, (far, swap(far, "core")), gy_blocks[6:], arrived, rows, turn)
     (gy_rows,), (rows, gate_rows) = gy_rows, rows
 
     act, expert_grads, back_own, back_other = main(z, rows, gy_rows, gate_rows, expert_w, gy_blocks)

time: 355 us -> 347 us (0.977)
  waiting for transfers between devices: 93.7 us -> 73.5 us
  starting transfers between devices: 70.3 us -> 81 us
    all_to_all x1, waiting for transfers between devices: 17.9 us -> 0.01 us  [on_device(): lax.all_to_all(packed, AXES, split_axis=0, concat_axis=0, tiled=True)]
    ppermute x40, starting transfers between devices: 39.7 us -> 46 us  [shift(): return lax.ppermute(values, axis, [(i, (i + by) % n) for i in range(n)])]
    pallas_call x3 -> x4, Pallas kernels: 28.4 us -> 30.6 us  [rows_of(): call(functools.partial(rows_kernel, n, with_gates), 'rows', n * 750000000...]
    unnamed x73 -> x81, local copies, waits for them, and re-layouts: 8.65 us -> 7.43 us
  transfers between devices with their start and end apart: 46 -> 46, of which waited for: 17 -> 15; matrix products, arithmetic and copies ran while one was open for 5% -> 5% of each run, Pallas kernels for 27% -> 29%
where the time goes in v5:
time: 347 us; the launch traced here: 342 us
  Pallas kernels  141 us (41%)
  starting transfers between devices  81 us (23%)
  waiting for transfers between devices  73.5 us (21%)
  other arithmetic  20.3 us (6%)
  between operations  14.6 us (4%)
  local copies, waits for them, and re-layouts  11.4 us (3%)
    ppermute x40, waiting for transfers between devices, shift(): return lax.ppermute(values, axis, [(i, (i + by) % n) for i in range(n)])  63.8 us
    ppermute x40, starting transfers between devices, shift(): return lax.ppermute(values, axis, [(i, (i + by) % n) for i in range(n)])  46 us
    pallas_call x1, Pallas kernels, main(): call(main_kernel, 'experts', 25000000000, 60000000, grid=(SHARE,), in_spe...  41.3 us
    pallas_call x4, Pallas kernels, rows_of(): call(functools.partial(rows_kernel, n, with_gates), 'rows', n * 750000000...  30.6 us
    pallas_call x1, Pallas kernels, back(): call(back_kernel, 'back', 20000000000, 16000000, in_specs=[SCALAR] + [VEC...  16.6 us
    pallas_call x1, Pallas kernels, outs(): call(outs_kernel, 'expert_outs', 6000000000, 12000000, grid=(SHARE,), in_...  14.6 us
    pallas_call x1, Pallas kernels, front(): call(front_kernel, 'front', 8000000000, 10000000, in_specs=[SCALAR] + [VE...  12 us
    all_to_all x1, starting transfers between devices, on_device(): lax.all_to_all(packed, AXES, split_axis=0, concat_axis=0, tiled=True)  11.8 us
  transfers between devices with their start and end apart: 46, of which 15 were waited for; matrix products, arithmetic and copies ran while one was open for 5% of the time, Pallas kernels for 29%

profile of v5, /device:TPU:1, one launch (start us, length us, event | category | flops | bytes accessed | tf_op | source)
XLA Modules:
  0.0 341.7 jit_solution(8510319837157311787)
XLA Ops:
  13.4 3.1 multiply_sine_fusion
  20.9 11.8 %all-to-all-start = ((bf16[128,8,640]{2,1,0:T(8,128)(2,1)}), bf16[128,8,640]{2,1,0:T(8,128)(2,1)S(1)}, u32[]{:S(2)}, u32[]{:S(2)}) async-start(bf16[128,8,640]{2,1,0:T(8,128)(2,1)} %get-tuple-element.105), calls=%async_computation | async-start | bytes 2621440 | tf_op jit(solution)/shard_map/all_to_all | solution.py:690
  33.5 2.5 codes.1.refs_0_.refs_2_.gy_ref
  41.3 3.2 collective-permute-done.2
  44.4 19.7 %collective-permute-done.3.refs_2_.refs_4_ = bf16[256,1152]{1,0:T(8,128)(2,1)S(1)} collective-permute-done((bf16[256,1152]{1,0:T(8,128)(2,1)}, bf16[256,1152]{1,0:T(8,128)(2,1)S(1)}, u32[]{:S(2)}, u32[]{:S(2)}) %collective-permute-start.3) | collective-permute-done | bytes 589856 | tf_op jit(solution)/shard_map/ppermute | solution.py:636
  65.4 7.1 %all-to-all-start.1 = ((bf16[32,8,2048]{2,1,0:T(8,128)(2,1)}), bf16[32,8,2048]{2,1,0:T(8,128)(2,1)S(1)}, u32[]{:S(2)}, u32[]{:S(2)}) async-start(bf16[32,8,2048]{2,1,0:T(8,128)(2,1)} %broadcast_in_dim.4), calls=%async_computation.1 | async-start | bytes 2097152 | tf_op jit(solution)/shard_map/all_to_all | solution.py:700
  72.5 3.3 collective-permute-start.11
  75.9 12.0 %front.1 = (bf16[1024,256]{1,0:T(8,128)(2,1)}, bf16[1024,256]{1,0:T(8,128)(2,1)}, bf16[1024,256]{1,0:T(8,128)(2,1)}, bf16[256,256]{1,0:T(8,128)(2,1)}, bf16[256,...) custom-call(s32[2]{0:T(128)} %pad_add_fusion.place_ref, ...), custom_call_target="tpu_custom_call" | custom-call | flops 8000000000 | bytes 10000000 | tf_op jit(solution)/shard_map/front/pallas_call | solution.py:234
  91.6 5.7 %collective-permute-done.9 = bf16[256,256]{1,0:T(8,128)(2,1)S(1)} collective-permute-done((bf16[256,256]{1,0:T(8,128)(2,1)}, bf16[256,256]{1,0:T(8,128)(2,1)S(1)}, u32[]{:S(2)}, u32[]{:S(2)}) %collective-permute-start.9) | collective-permute-done | bytes 131104 | tf_op jit(solution)/shard_map/ppermute | solution.py:636
  97.4 2.9 collective-permute-start.10
  100.8 2.5 collective-permute-done.7.m1_ref
  108.7 3.9 %mid.1 = (f32[256,1024]{1,0:T(8,128)}, bf16[256,1024]{1,0:T(8,128)(2,1)}) custom-call(bf16[256,1024]{1,0:T(8,128)(2,1)} %bitcast.71, bf16[256,256]{1,0:T(8,128)(2,1)} %get-tuple-element.117.m0_ref, bf16[256,256]{1,0:T(8,128)(2,1)} %copy-done.28, bf16[256,256]{1,0:T(8,128)(2,1)} %copy-done.29, bf16[256,256]{1,0:T(8,128)(2,1)} %copy-done.30, ...), custom_call_target="tpu_custom_call" | custom-call | flops 1000000000 | bytes 5000000 | tf_op jit(solution)/shard_map/mid/pallas_call | solution.py:258
  117.1 10.6 %rows.4 = (bf16[8,8,80,1024]{3,2,1,0:T(8,128)(2,1)}, f32[8,128]{1,0:T(8,128)}) custom-call(s32[1]{0:T(128)} %bitcast.12.z_ref, bf16[256,1152]{1,0:T(8,128)(2,1)} %codes.1.refs_0_.refs_2_.gy_ref, bf16[256,1152]{1,0:T(8,128)(2,1)} %collective-permute-done.15.refs_1_.refs_3_, bf16[256,1152]{1,0:T(8,128)(2,1)} %copy-done.10, bf16[256,1152]{1,0:T(8,128)(2,1)} %copy-done.12, ...), custom_call_target="tpu_custom_call" | custom-call | flops 6000000000 | bytes 16000000 | tf_op jit(solution)/shard_map/rows/pallas_call | solution.py:465
  130.6 5.5 %rows.5 = (bf16[8,8,80,1024]{3,2,1,0:T(8,128)(2,1)}, f32[8,8,80,1]{3,2,1,0:T(8,128)}, f32[8,128]{1,0:T(8,128)}) custom-call(s32[1]{0:T(128)} %bitcast.12.z_ref, bf16[256,1024]{1,0:T(8,128)(2,1)} %get-tuple-element.131.refs_0_, bf16[256,1024]{1,0:T(8,128)(2,1)} %copy-done.36, bf16[256,1152]{1,0:T(8,128)(2,1)} %codes.1.refs_0_.refs_2_.gy_ref, ...), custom_call_target="tpu_custom_call" | custom-call | flops 1500000000 | bytes 4000000 | tf_op jit(solution)/shard_map/rows/pallas_call | solution.py:465
  137.2 8.9 %rows.6 = (bf16[8,8,80,1024]{3,2,1,0:T(8,128)(2,1)}, f32[8,8,80,1]{3,2,1,0:T(8,128)}, f32[8,128]{1,0:T(8,128)}) custom-call(s32[1]{0:T(128)} %bitcast.12.z_ref, bf16[256,1024]{1,0:T(8,128)(2,1)} %copy-done.20, bf16[256,1024]{1,0:T(8,128)(2,1)} %copy-done.23, bf16[256,1024]{1,0:T(8,128)(2,1)} %copy-done.21, ...), custom_call_target="tpu_custom_call", output_to_operand_aliasing={{0}: (11, {}), {1}: (12, {})} | custom-call | flops 3000000000 | bytes 8000000 | tf_op jit(solution)/shard_map/rows/pallas_call | solution.py:465
  149.3 5.6 %rows.7 = (bf16[8,8,80,1024]{3,2,1,0:T(8,128)(2,1)}, f32[8,8,80,1]{3,2,1,0:T(8,128)}, f32[8,128]{1,0:T(8,128)}) custom-call(s32[1]{0:T(128)} %bitcast.12.z_ref, bf16[256,1024]{1,0:T(8,128)(2,1)} %copy-done.22, bf16[256,1024]{1,0:T(8,128)(2,1)} %copy-done.25, bf16[256,1152]{1,0:T(8,128)(2,1)} %copy-done.11, ...), custom_call_target="tpu_custom_call", output_to_operand_aliasing={{0}: (7, {}), {1}: (8, {})} | custom-call | flops 1500000000 | bytes 4000000 | tf_op jit(solution)/shard_map/rows/pallas_call | solution.py:465
  154.8 41.3 %experts.1 = (bf16[8,640,256]{2,1,0:T(8,128)(2,1)}, bf16[8,2,768,512]{3,2,1,0:T(8,128)(2,1)}, bf16[4,256,1152]{2,1,0:T(8,128)(2,1)}, bf16[4,256,1152]{2,1,0:T(8,128)(2,1)}) custom-call(s32[1]{0:T(128)} %bitcast.12.z_ref, bf16[8,8,80,1024]{3,2,1,0:T(8,128)(2,1)} %get-tuple-element.143.x_ref, bf16[8,8,80,1024]{3,2,1,0:T(8,128)(2,1)} %get-tuple-element.144.gy_ref, ...), custom_call_target="tpu_custom_call" | custom-call | flops 24999999488 | bytes 60000000 | tf_op jit(solution)/shard_map/experts/pallas_call | solution.py:551
  196.8 4.4 %collective-permute-done.24 = bf16[4,256,1152]{2,1,0:T(8,128)(2,1)S(1)} collective-permute-done((bf16[4,256,1152]{2,1,0:T(8,128)(2,1)}, bf16[4,256,1152]{2,1,0:T(8,128)(2,1)S(1)}, u32[]{:S(2)}, u32[]{:S(2)}) %collective-permute-start.24) | collective-permute-done | bytes 2359328 | tf_op jit(solution)/shard_map/ppermute | solution.py:636
  206.6 14.6 %expert_outs.1 = (bf16[4,256,1024]{2,1,0:T(8,128)(2,1)}, bf16[4,256,1024]{2,1,0:T(8,128)(2,1)}) custom-call(s32[1]{0:T(128)} %bitcast.12.z_ref, bf16[8,640,256]{2,1,0:T(8,128)(2,1)} %get-tuple-element.152.act_ref, bf16[16,1536,256]{2,1,0:T(8,128)(2,1)} %bitcast.93, bf16[256,1152]{1,0:T(8,128)(2,1)} %codes.1.refs_0_.refs_2_.gy_ref, ...), custom_call_target="tpu_custom_call" | custom-call | flops 6000000000 | bytes 12000000 | tf_op jit(solution)/shard_map/expert_outs/pallas_call | solution.py:599
  222.2 10.1 %collective-permute-done.27.part3_ref = bf16[256,1152]{1,0:T(8,128)(2,1)S(1)} collective-permute-done((bf16[256,1152]{1,0:T(8,128)(2,1)S(1)}, bf16[256,1152]{1,0:T(8,128)(2,1)S(1)}, u32[]{:S(2)}, u32[]{:S(2)}) %collective-permute-start.27) | collective-permute-done | bytes 589856 | tf_op jit(solution)/shard_map/ppermute | solution.py:636
  233.2 7.9 %turn.1 = (bf16[256,256]{1,0:T(8,128)(2,1)}, bf16[256,256]{1,0:T(8,128)(2,1)}, bf16[256,256]{1,0:T(8,128)(2,1)}, bf16[256,256]{1,0:T(8,128)(2,1)}, f32[256,1024]...) custom-call(s32[2]{0:T(128)} %pad_add_fusion.place_ref, ...), custom_call_target="tpu_custom_call" | custom-call | flops 2000000000 | bytes 10000000 | tf_op jit(solution)/shard_map/turn/pallas_call | solution.py:299
  244.4 6.1 %collective-permute-done.32 = bf16[256,256]{1,0:T(8,128)(2,1)} collective-permute-done((bf16[256,256]{1,0:T(8,128)(2,1)}, bf16[256,256]{1,0:T(8,128)(2,1)}, u32[]{:S(2)}, u32[]{:S(2)}) %collective-permute-start.32) | collective-permute-done | bytes 131104 | tf_op jit(solution)/shard_map/ppermute | solution.py:636
  251.8 2.6 add_convert_fusion.1
  257.9 9.0 %all-to-all-start.2 = ((bf16[64,8,1024]{2,1,0:T(8,128)(2,1)}), bf16[64,8,1024]{2,1,0:T(8,128)(2,1)S(1)}, u32[]{:S(2)}, u32[]{:S(2)}) async-start(bf16[64,8,1024]{2,1,0:T(8,128)(2,1)} %bitcast.18), calls=%async_computation.2 | async-start | bytes 2097152 | tf_op jit(solution)/shard_map/all_to_all | solution.py:739
  267.6 16.6 %back.1 = (bf16[1024,512]{1,0:T(8,128)(2,1)}, bf16[2,256,1024]{2,1,0:T(8,128)(2,1)}, bf16[2,256,1024]{2,1,0:T(8,128)(2,1)}, f32[8,1024]{1,0:T(8,128)}) custom-call(s32[2]{0:T(128)} %pad_add_fusion.place_ref, bf16[1024,256]{1,0:T(8,128)(2,1)} %get-tuple-element.156.q_ref, bf16[1024,256]{1,0:T(8,128)(2,1)} %get-tuple-element.157.k_ref, ...), custom_call_target="tpu_custom_call" | custom-call | flops 20000000000 | bytes 16000000 | tf_op jit(solution)/shard_map/back/pallas_call | solution.py:363
  284.4 3.2 collective-permute-start.36
  289.2 4.5 %projections.1 = bf16[1024,640]{1,0:T(8,128)(2,1)} custom-call(bf16[1024,1024]{1,0:T(8,128)(2,1)} %get-tuple-element.172.h_ref, bf16[1024,512]{1,0:T(8,128)(2,1)} %get-tuple-element.173.dqkv_ref, f32[1024,128]{1,0:T(8,128)} %get-tuple-element.174.sums_ref, f32[8,1024]{1,0:T(8,128)} %get-tuple-element.175.gain_ref), custom_call_target="tpu_custom_call" | custom-call | flops 1500000000 | bytes 5000000 | tf_op jit(solution)/shard_map/projections/pallas_call | solution.py:380
  293.6 7.1 %all-to-all-start.3 = ((bf16[128,8,640]{2,1,0:T(8,128)(2,1)}), bf16[128,8,640]{2,1,0:T(8,128)(2,1)S(1)}, u32[]{:S(2)}, u32[]{:S(2)}) async-start(bf16[128,8,640]{2,1,0:T(8,128)(2,1)} %bitcast.80), calls=%async_computation.3 | async-start | bytes 2621440 | tf_op jit(solution)/shard_map/all_to_all | solution.py:750
  309.4 2.5 finish.1
  311.9 9.6 %all-to-all-done.3 = bf16[128,8,640]{2,1,0:T(8,128)(2,1)S(1)} async-done(((bf16[128,8,640]{2,1,0:T(8,128)(2,1)}), bf16[128,8,640]{2,1,0:T(8,128)(2,1)S(1)}, u32[]{:S(2)}, u32[]{:S(2)}) %all-to-all-start.3) | async-done | bytes 1310752 | tf_op jit(solution)/shard_map/all_to_all | solution.py:750
  321.5 6.1 %collective-permute-done.37 = bf16[256,1024]{1,0:T(8,128)(2,1)} collective-permute-done((bf16[256,1024]{1,0:T(8,128)(2,1)}, bf16[256,1024]{1,0:T(8,128)(2,1)}, u32[]{:S(2)}, u32[]{:S(2)}) %collective-permute-start.37) | collective-permute-done | bytes 524320 | tf_op jit(solution)/shard_map/ppermute | solution.py:636
  331.3 3.4 %fusion.6 = (f32[1,256,1024]{2,1,0:T(8,128)}, bf16[1,256,1024]{2,1,0:T(8,128)(2,1)}) fusion(f32[256,1024]{1,0:T(8,128)S(1)} %copy-done.9, bf16[256,1024]{1,0:T(8,128)(2,1)S(1)} %bitcast.76, bf16[256,1024]{1,0:T(8,128)(2,1)} %collective-permute-done.37, f32[256]{0:T(256)S(1)} %broadcast_multiply_fusion, f32[1024]{0:T(1024)S(1)} %bitcast.87, ...), kind=kLoop, calls=%fused_computation.16 | loop fusion | flops 5242880 | bytes 7870465 | tf_op jit(solution)/shard_map/reshape | solution.py:770
  (182 shorter events, 69.7 us)
Async XLA Ops:
  7.2 147.7 %all-gather.3.cloned.1.call-start = ((), (), s32[]{:S(2)}) async-start(), calls=%async_computation.6 | async-start | bytes 13369344 | tf_op jit(solution)/shard_map/all_gather | solution.py:688
  7.2 13.7 %collective-permute-start.1 = (bf16[256,1024]{1,0:T(8,128)(2,1)}, bf16[256,1024]{1,0:T(8,128)(2,1)S(1)}, u32[]{:S(2)}, u32[]{:S(2)}) collective-permute-start(bf16[256,1024]{1,0:T(8,128)(2,1)} %bitcast.69), channel_id=1, source_target_pairs={{0,64},{64,0},{1,65},{65,1},{2,66},{66,2},{3,67},{67,3},{4,68},{68... | collective-permute-start | bytes 1572872 | tf_op jit(solution)/shard_map/ppermute | solution.py:636
  20.9 43.2 %all-to-all-start = ((bf16[128,8,640]{2,1,0:T(8,128)(2,1)}), bf16[128,8,640]{2,1,0:T(8,128)(2,1)S(1)}, u32[]{:S(2)}, u32[]{:S(2)}) async-start(bf16[128,8,640]{2,1,0:T(8,128)(2,1)} %get-tuple-element.105), calls=%async_computation | async-start | bytes 2621440 | tf_op jit(solution)/shard_map/all_to_all | solution.py:690
  36.1 28.0 %collective-permute-start.3 = (bf16[256,1152]{1,0:T(8,128)(2,1)}, bf16[256,1152]{1,0:T(8,128)(2,1)S(1)}, u32[]{:S(2)}, u32[]{:S(2)}) collective-permute-start(bf16[256,1152]{1,0:T(8,128)(2,1)} %codes.1.refs_0_.refs_2_.gy_ref), channel_id=1, source_target_pairs={{0,1},{1,2},{2,3},{3,0},{4,5},{5,6},{6,7},{7,4},{8,9},{9,10},{10,1... | collective-permute-start | bytes 1769480 | tf_op jit(solution)/shard_map/ppermute | solution.py:636
  37.6 26.5 %collective-permute-start.4 = (bf16[256,1152]{1,0:T(8,128)(2,1)}, bf16[256,1152]{1,0:T(8,128)(2,1)}, u32[]{:S(2)}, u32[]{:S(2)}) collective-permute-start(bf16[256,1152]{1,0:T(8,128)(2,1)} %codes.1.refs_0_.refs_2_.gy_ref), channel_id=1, source_target_pairs={{0,3},{1,0},{2,1},{3,2},{4,7},{5,4},{6,5},{7,6},{8,11},{9,8},{10,9... | collective-permute-start | bytes 1769480 | tf_op jit(solution)/shard_map/ppermute | solution.py:636
  39.4 36.5 %collective-permute-start.5 = (bf16[256,1024]{1,0:T(8,128)(2,1)S(1)}, bf16[256,1024]{1,0:T(8,128)(2,1)}, u32[]{:S(2)}, u32[]{:S(2)}) collective-permute-start(bf16[256,1024]{1,0:T(8,128)(2,1)S(1)} %bitcast.73), channel_id=1, source_target_pairs={{0,32},{32,0},{1,33},{33,1},{2,34},{34,2},{3,35},{35,3},{4,36},{36... | collective-permute-start | bytes 1572872 | tf_op jit(solution)/shard_map/ppermute | solution.py:636
  40.4 35.5 %collective-permute-start.6 = (bf16[256,1024]{1,0:T(8,128)(2,1)}, bf16[256,1024]{1,0:T(8,128)(2,1)}, u32[]{:S(2)}, u32[]{:S(2)}) collective-permute-start(bf16[256,1024]{1,0:T(8,128)(2,1)} %copy-done.34), channel_id=1, source_target_pairs={{0,32},{32,0},{1,33},{33,1},{2,34},{34,2},{3,35},{35,3},{4,36},{36... | collective-permute-start | bytes 1572872 | tf_op jit(solution)/shard_map/ppermute | solution.py:636
  65.4 38.0 %all-to-all-start.1 = ((bf16[32,8,2048]{2,1,0:T(8,128)(2,1)}), bf16[32,8,2048]{2,1,0:T(8,128)(2,1)S(1)}, u32[]{:S(2)}, u32[]{:S(2)}) async-start(bf16[32,8,2048]{2,1,0:T(8,128)(2,1)} %broadcast_in_dim.4), calls=%async_computation.1 | async-start | bytes 2097152 | tf_op jit(solution)/shard_map/all_to_all | solution.py:700
  72.5 233.3 %reduce-scatter.2.cloned.1.call-start = ((), (), s32[]{:S(2)}) async-start(), calls=%async_computation.5 | async-start | bytes 13369344 | tf_op jit(solution)/shard_map/reduce_scatter | solution.py:728
  72.5 28.3 %collective-permute-start.11 = (bf16[256,1152]{1,0:T(8,128)(2,1)S(1)}, bf16[256,1152]{1,0:T(8,128)(2,1)S(1)}, u32[]{:S(2)}, u32[]{:S(2)}) collective-permute-start(bf16[256,1152]{1,0:T(8,128)(2,1)S(1)} %copy-done.5), channel_id=1, source_target_pairs={{0,2},{1,3},{2,0},{3,1},{4,6},{5,7},{6,4},{7,5},{8,10},{9,11},{10,... | collective-permute-start | bytes 1769480 | tf_op jit(solution)/shard_map/ppermute | solution.py:636
  88.2 15.2 %collective-permute-start.7 = (bf16[256,256]{1,0:T(8,128)(2,1)}, bf16[256,256]{1,0:T(8,128)(2,1)S(1)}, u32[]{:S(2)}, u32[]{:S(2)}) collective-permute-start(bf16[256,256]{1,0:T(8,128)(2,1)} %get-tuple-element.112), channel_id=1, source_target_pairs={{0,64},{64,0},{1,65},{65,1},{2,66},{66,2},{3,67},{67,3},{4,68},{68... | collective-permute-start | bytes 393224 | tf_op jit(solution)/shard_map/ppermute | solution.py:636
  89.4 14.0 %collective-permute-start.8 = (bf16[256,256]{1,0:T(8,128)(2,1)}, bf16[256,256]{1,0:T(8,128)(2,1)S(1)}, u32[]{:S(2)}, u32[]{:S(2)}) collective-permute-start(bf16[256,256]{1,0:T(8,128)(2,1)} %get-tuple-element.113), channel_id=1, source_target_pairs={{0,32},{32,0},{1,33},{33,1},{2,34},{34,2},{3,35},{35,3},{4,36},{36... | collective-permute-start | bytes 393224 | tf_op jit(solution)/shard_map/ppermute | solution.py:636
  106.1 10.4 %collective-permute-start.17 = (bf16[256,1152]{1,0:T(8,128)(2,1)}, bf16[256,1152]{1,0:T(8,128)(2,1)}, u32[]{:S(2)}, u32[]{:S(2)}) collective-permute-start(bf16[256,1152]{1,0:T(8,128)(2,1)} %collective-permute-done.4.refs_4_.refs_6_), channel_id=1, source_target_pairs={{0,32},{32,0},{1,33},{33,1},{2,34},{34,2},{3,35},{35,3},{4,36},{36... | collective-permute-start | bytes 1769480 | tf_op jit(solution)/shard_map/ppermute | solution.py:636
  112.7 15.0 %collective-permute-start.13 = (bf16[256,1024]{1,0:T(8,128)(2,1)}, bf16[256,1024]{1,0:T(8,128)(2,1)S(1)}, u32[]{:S(2)}, u32[]{:S(2)}) collective-permute-start(bf16[256,1024]{1,0:T(8,128)(2,1)} %get-tuple-element.131.refs_0_), channel_id=1, source_target_pairs={{0,1},{1,2},{2,3},{3,0},{4,5},{5,6},{6,7},{7,4},{8,9},{9,10},{10,1... | collective-permute-start | bytes 1572872 | tf_op jit(solution)/shard_map/ppermute | solution.py:636
  113.1 14.6 %collective-permute-start.14 = (bf16[256,1024]{1,0:T(8,128)(2,1)}, bf16[256,1024]{1,0:T(8,128)(2,1)S(1)}, u32[]{:S(2)}, u32[]{:S(2)}) collective-permute-start(bf16[256,1024]{1,0:T(8,128)(2,1)} %get-tuple-element.131.refs_0_), channel_id=1, source_target_pairs={{0,3},{1,0},{2,1},{3,2},{4,7},{5,4},{6,5},{7,6},{8,11},{9,8},{10,9... | collective-permute-start | bytes 1572872 | tf_op jit(solution)/shard_map/ppermute | solution.py:636
  115.5 14.3 %collective-permute-start.22 = (bf16[256,1024]{1,0:T(8,128)(2,1)}, bf16[256,1024]{1,0:T(8,128)(2,1)S(1)}, u32[]{:S(2)}, u32[]{:S(2)}) collective-permute-start(bf16[256,1024]{1,0:T(8,128)(2,1)} %get-tuple-element.131.refs_0_), channel_id=1, source_target_pairs={{0,32},{32,0},{1,33},{33,1},{2,34},{34,2},{3,35},{35,3},{4,36},{36... | collective-permute-start | bytes 1572872 | tf_op jit(solution)/shard_map/ppermute | solution.py:636
  128.6 17.5 %collective-permute-start.19 = (bf16[256,1024]{1,0:T(8,128)(2,1)S(1)}, bf16[256,1024]{1,0:T(8,128)(2,1)S(1)}, u32[]{:S(2)}, u32[]{:S(2)}) collective-permute-start(bf16[256,1024]{1,0:T(8,128)(2,1)S(1)} %copy-done.35), channel_id=1, source_target_pairs={{0,2},{1,3},{2,0},{3,1},{4,6},{5,7},{6,4},{7,5},{8,10},{9,11},{10,... | collective-permute-start | bytes 1572872 | tf_op jit(solution)/shard_map/ppermute | solution.py:636
  202.7 19.5 %collective-permute-start.25 = (bf16[256,1152]{1,0:T(8,128)(2,1)S(1)}, bf16[256,1152]{1,0:T(8,128)(2,1)S(1)}, u32[]{:S(2)}, u32[]{:S(2)}) collective-permute-start(bf16[256,1152]{1,0:T(8,128)(2,1)S(1)} %get-tuple-element.196), channel_id=1, source_target_pairs={{0,3},{1,0},{2,1},{3,2},{4,7},{5,4},{6,5},{7,6},{8,11},{9,8},{10,9... | collective-permute-start | bytes 1769480 | tf_op jit(solution)/shard_map/ppermute | solution.py:636
  204.0 18.2 %collective-permute-start.26 = (bf16[256,1152]{1,0:T(8,128)(2,1)S(1)}, bf16[256,1152]{1,0:T(8,128)(2,1)S(1)}, u32[]{:S(2)}, u32[]{:S(2)}) collective-permute-start(bf16[256,1152]{1,0:T(8,128)(2,1)S(1)} %get-tuple-element.195), channel_id=1, source_target_pairs={{0,1},{1,2},{2,3},{3,0},{4,5},{5,6},{6,7},{7,4},{8,9},{9,10},{10,1... | collective-permute-start | bytes 1769480 | tf_op jit(solution)/shard_map/ppermute | solution.py:636
  204.8 27.5 %collective-permute-start.27 = (bf16[256,1152]{1,0:T(8,128)(2,1)S(1)}, bf16[256,1152]{1,0:T(8,128)(2,1)S(1)}, u32[]{:S(2)}, u32[]{:S(2)}) collective-permute-start(bf16[256,1152]{1,0:T(8,128)(2,1)S(1)} %get-tuple-element.194), channel_id=1, source_target_pairs={{0,2},{1,3},{2,0},{3,1},{4,6},{5,7},{6,4},{7,5},{8,10},{9,11},{10,... | collective-permute-start | bytes 1769480 | tf_op jit(solution)/shard_map/ppermute | solution.py:636
  221.2 33.2 %collective-permute-start.29 = (bf16[4,256,1024]{2,1,0:T(8,128)(2,1)}, bf16[4,256,1024]{2,1,0:T(8,128)(2,1)S(1)}, u32[]{:S(2)}, u32[]{:S(2)}) collective-permute-start(bf16[4,256,1024]{2,1,0:T(8,128)(2,1)} %get-tuple-element.154), channel_id=1, source_target_pairs={{0,32},{32,0},{1,33},{33,1},{2,34},{34,2},{3,35},{35,3},{4,36},{36... | collective-permute-start | bytes 6291464 | tf_op jit(solution)/shard_map/ppermute | solution.py:636
  241.1 10.7 %collective-permute-start.28 = (bf16[2,256,1024]{2,1,0:T(8,128)(2,1)}, bf16[2,256,1024]{2,1,0:T(8,128)(2,1)S(1)}, u32[]{:S(2)}, u32[]{:S(2)}) collective-permute-start(bf16[2,256,1024]{2,1,0:T(8,128)(2,1)} %get-tuple-element.150), channel_id=1, source_target_pairs={{0,32},{32,0},{1,33},{33,1},{2,34},{34,2},{3,35},{35,3},{4,36},{36... | collective-permute-start | bytes 3145736 | tf_op jit(solution)/shard_map/ppermute | solution.py:636
  242.7 24.2 %collective-permute-start.30 = (bf16[256,256]{1,0:T(8,128)(2,1)}, bf16[256,256]{1,0:T(8,128)(2,1)S(1)}, u32[]{:S(2)}, u32[]{:S(2)}) collective-permute-start(bf16[256,256]{1,0:T(8,128)(2,1)} %get-tuple-element.160), channel_id=1, source_target_pairs={{0,64},{64,0},{1,65},{65,1},{2,66},{66,2},{3,67},{67,3},{4,68},{68... | collective-permute-start | bytes 393224 | tf_op jit(solution)/shard_map/ppermute | solution.py:636
  243.7 23.2 %collective-permute-start.31 = (bf16[256,256]{1,0:T(8,128)(2,1)}, bf16[256,256]{1,0:T(8,128)(2,1)S(1)}, u32[]{:S(2)}, u32[]{:S(2)}) collective-permute-start(bf16[256,256]{1,0:T(8,128)(2,1)} %get-tuple-element.161), channel_id=1, source_target_pairs={{0,32},{32,0},{1,33},{33,1},{2,34},{34,2},{3,35},{35,3},{4,36},{36... | collective-permute-start | bytes 393224 | tf_op jit(solution)/shard_map/ppermute | solution.py:636
  250.5 16.4 %collective-permute-start.33 = (bf16[256,256]{1,0:T(8,128)(2,1)}, bf16[256,256]{1,0:T(8,128)(2,1)S(1)}, u32[]{:S(2)}, u32[]{:S(2)}) collective-permute-start(bf16[256,256]{1,0:T(8,128)(2,1)} %collective-permute-done.32), channel_id=1, source_target_pairs={{0,32},{32,0},{1,33},{33,1},{2,34},{34,2},{3,35},{35,3},{4,36},{36... | collective-permute-start | bytes 393224 | tf_op jit(solution)/shard_map/ppermute | solution.py:636
  256.4 27.9 %collective-permute-start.34 = (bf16[256,1024]{1,0:T(8,128)(2,1)}, bf16[256,1024]{1,0:T(8,128)(2,1)S(1)}, u32[]{:S(2)}, u32[]{:S(2)}) collective-permute-start(bf16[256,1024]{1,0:T(8,128)(2,1)} %get-tuple-element.168), channel_id=1, source_target_pairs={{0,3},{1,0},{2,1},{3,2},{4,7},{5,4},{6,5},{7,6},{8,11},{9,8},{10,9... | collective-permute-start | bytes 1572872 | tf_op jit(solution)/shard_map/ppermute | solution.py:636
  256.6 27.6 %collective-permute-start.35 = (bf16[256,1024]{1,0:T(8,128)(2,1)S(1)}, bf16[256,1024]{1,0:T(8,128)(2,1)S(1)}, u32[]{:S(2)}, u32[]{:S(2)}) collective-permute-start(bf16[256,1024]{1,0:T(8,128)(2,1)S(1)} %get-tuple-element.169), channel_id=1, source_target_pairs={{0,1},{1,2},{2,3},{3,0},{4,5},{5,6},{6,7},{7,4},{8,9},{9,10},{10,1... | collective-permute-start | bytes 1572872 | tf_op jit(solution)/shard_map/ppermute | solution.py:636
  257.9 26.5 %all-to-all-start.2 = ((bf16[64,8,1024]{2,1,0:T(8,128)(2,1)}), bf16[64,8,1024]{2,1,0:T(8,128)(2,1)S(1)}, u32[]{:S(2)}, u32[]{:S(2)}) async-start(bf16[64,8,1024]{2,1,0:T(8,128)(2,1)} %bitcast.18), calls=%async_computation.2 | async-start | bytes 2097152 | tf_op jit(solution)/shard_map/all_to_all | solution.py:739
  284.4 17.2 %collective-permute-start.36 = (bf16[2,256,1024]{2,1,0:T(8,128)(2,1)}, bf16[2,256,1024]{2,1,0:T(8,128)(2,1)}, u32[]{:S(2)}, u32[]{:S(2)}) collective-permute-start(bf16[2,256,1024]{2,1,0:T(8,128)(2,1)} %get-tuple-element.177), channel_id=1, source_target_pairs={{0,32},{32,0},{1,33},{33,1},{2,34},{34,2},{3,35},{35,3},{4,36},{36... | collective-permute-start | bytes 3145736 | tf_op jit(solution)/shard_map/ppermute | solution.py:636
  288.4 23.6 %collective-permute-start.38 = (bf16[256,1024]{1,0:T(8,128)(2,1)}, bf16[256,1024]{1,0:T(8,128)(2,1)}, u32[]{:S(2)}, u32[]{:S(2)}) collective-permute-start(bf16[256,1024]{1,0:T(8,128)(2,1)} %get-tuple-element.178), channel_id=1, source_target_pairs={{0,2},{1,3},{2,0},{3,1},{4,6},{5,7},{6,4},{7,5},{8,10},{9,11},{10,... | collective-permute-start | bytes 1572872 | tf_op jit(solution)/shard_map/ppermute | solution.py:636
  293.6 27.9 %all-to-all-start.3 = ((bf16[128,8,640]{2,1,0:T(8,128)(2,1)}), bf16[128,8,640]{2,1,0:T(8,128)(2,1)S(1)}, u32[]{:S(2)}, u32[]{:S(2)}) async-start(bf16[128,8,640]{2,1,0:T(8,128)(2,1)} %bitcast.80), calls=%async_computation.3 | async-start | bytes 2621440 | tf_op jit(solution)/shard_map/all_to_all | solution.py:750
  304.4 23.2 %collective-permute-start.37 = (bf16[256,1024]{1,0:T(8,128)(2,1)}, bf16[256,1024]{1,0:T(8,128)(2,1)}, u32[]{:S(2)}, u32[]{:S(2)}) collective-permute-start(bf16[256,1024]{1,0:T(8,128)(2,1)} %select_bitcast_fusion), channel_id=1, source_target_pairs={{0,64},{64,0},{1,65},{65,1},{2,66},{66,2},{3,67},{67,3},{4,68},{68... | collective-permute-start | bytes 1572872 | tf_op jit(solution)/shard_map/ppermute | solution.py:636
  (54 other events, 369.5 us)
Sparse Core Ops, SparseCore 0:
  21.0 120.0 all-gather.2
  196.3 100.3 reduce-scatter.1

commit v6 on v5

--- a/solution.py
+++ b/solution.py
@@ -691,7 +691,8 @@
     output_rows = jnp.concatenate([output_weight, swap(output_weight, "ylo")], axis=1)
     gy_blocks = gather_z(gy_own)
     arrived, output_rows, *near = fence(arrived, output_rows, *gy_blocks[1:3])
-    gy_blocks[1:3] = near
+    gy_near = [block for pair in with_core([gy_own, *near]) for block in pair]
+    gy_far = gy_blocks[3]
     beside = swap(own, "core")
 
     blocks = [own, across, beside, swap(across, "core")]
@@ -701,19 +702,22 @@
         jnp.broadcast_to(output_rows[None], (32, 8, 2 * D)), FSDP, split_axis=0, concat_axis=0, tiled=True
     ).reshape(TOK, 2 * D)
 
-    mixed = exchange_seq(*mixed)
-    output_own, *rest = fence(output_own, *mixed, *gy_blocks)
-    mixed, gy_blocks = rest[:4], rest[4:]
+    turn, mixed[0], *gy_near = fence(jnp.zeros((8, 128), f32), mixed[0], *gy_near)
+    own_mixed, across_mixed, beside_mixed, both_mixed = mixed
+    gy_rows, turn = rows_of(z, 0, gy_near, None, None, None, turn)
+    both_mixed, turn = fence(swap(both_mixed, "ylo"), turn)
+    mixed = [own_mixed, swap(across_mixed, "ylo"), swap(beside_mixed, "core"), swap(both_mixed, "core")]
+    output_own, gy_far, turn, *mixed = fence(output_own, gy_far, turn, *mixed)
     output_other = swap(output_own, "core")
-    gy_blocks = [block for pair in with_core(gy_blocks) for block in pair]
+    gy_blocks = [*gy_near, gy_far, swap(gy_far, "core")]
     residual, hidden_two = mid(own, mixed, output_own, output_other, gains)
 
     near = [shift(hidden_two, "z", 1), shift(hidden_two, "z", -1)]
-    turn, _ = fence(jnp.zeros((8, 128), f32), hidden_two)
-    gy_rows, turn = rows_of(z, 0, gy_blocks, None, None, None, turn)
+    turn, _ = fence(turn, hidden_two)
+    gy_rows, turn = rows_of(z, 6, gy_blocks[6:], None, None, gy_rows, turn)
+    rows, turn = rows_of(z, 0, (hidden_two, swap(hidden_two, "core")), gy_blocks[:2], arrived, None, turn)
     *near, far, turn = fence(*near, hidden_two, turn)
     far = shift(far, "z", 2)
-    rows, turn = rows_of(z, 0, (hidden_two, swap(hidden_two, "core")), gy_blocks[:2], arrived, None, turn)
     near = [block for pair in with_core(near) for block in pair]
     rows, turn = rows_of(z, 2, near, gy_blocks[2:6], arrived, rows, turn)
     far, turn = fence(far, turn)

time: 347 us -> 347 us (level)
  starting transfers between devices: 81 us -> 76.5 us
    ppermute x40, starting transfers between devices: 46 us -> 41.5 us  [shift(): return lax.ppermute(values, axis, [(i, (i + by) % n) for i in range(n)])]
    pallas_call x4 -> x5, Pallas kernels: 30.6 us -> 32.5 us  [rows_of(): call(functools.partial(rows_kernel, n, with_gates), 'rows', n * 750000000...]
    unnamed x81 -> x79, local copies, waits for them, and re-layouts: 7.43 us -> 8.61 us
  transfers between devices with their start and end apart: 46 -> 46, of which waited for: 15 -> 15; matrix products, arithmetic and copies ran while one was open for 5% -> 5% of each run, Pallas kernels for 29% -> 30%
where the time goes in v6:
time: 347 us; the launch traced here: 341 us
  Pallas kernels  142 us (41%)
  starting transfers between devices  76.5 us (22%)
  waiting for transfers between devices  74.5 us (21%)
  other arithmetic  20.2 us (6%)
  between operations  14.6 us (4%)
  local copies, waits for them, and re-layouts  12.4 us (4%)
    ppermute x40, waiting for transfers between devices, shift(): return lax.ppermute(values, axis, [(i, (i + by) % n) for i in range(n)])  64.8 us
    ppermute x40, starting transfers between devices, shift(): return lax.ppermute(values, axis, [(i, (i + by) % n) for i in range(n)])  41.5 us
    pallas_call x1, Pallas kernels, main(): call(main_kernel, 'experts', 25000000000, 60000000, grid=(SHARE,), in_spe...  41.3 us
    pallas_call x5, Pallas kernels, rows_of(): call(functools.partial(rows_kernel, n, with_gates), 'rows', n * 750000000...  32.5 us
    pallas_call x1, Pallas kernels, back(): call(back_kernel, 'back', 20000000000, 16000000, in_specs=[SCALAR] + [VEC...  16.6 us
    pallas_call x1, Pallas kernels, outs(): call(outs_kernel, 'expert_outs', 6000000000, 12000000, grid=(SHARE,), in_...  14.6 us
    pallas_call x1, Pallas kernels, front(): call(front_kernel, 'front', 8000000000, 10000000, in_specs=[SCALAR] + [VE...  11.9 us
    all_to_all x1, starting transfers between devices, on_device(): lax.all_to_all(packed, AXES, split_axis=0, concat_axis=0, tiled=True)  11.8 us
  transfers between devices with their start and end apart: 46, of which 15 were waited for; matrix products, arithmetic and copies ran while one was open for 5% of the time, Pallas kernels for 30%

profile of v6, /device:TPU:1, one launch (start us, length us, event | category | flops | bytes accessed | tf_op | source)
XLA Modules:
  0.0 340.8 jit_solution(7703852374095089580)
XLA Ops:
  13.4 3.1 multiply_sine_fusion
  21.0 11.8 %all-to-all-start = ((bf16[128,8,640]{2,1,0:T(8,128)(2,1)}), bf16[128,8,640]{2,1,0:T(8,128)(2,1)S(1)}, u32[]{:S(2)}, u32[]{:S(2)}) async-start(bf16[128,8,640]{2,1,0:T(8,128)(2,1)} %get-tuple-element.115), calls=%async_computation | async-start | bytes 2621440 | tf_op jit(solution)/shard_map/all_to_all | solution.py:690
  33.6 2.5 codes.1.refs_0_.refs_2_.gy_ref
  41.4 3.2 collective-permute-done.2
  46.1 18.2 %collective-permute-done.3.refs_2_.refs_4_ = bf16[256,1152]{1,0:T(8,128)(2,1)} collective-permute-done((bf16[256,1152]{1,0:T(8,128)(2,1)}, bf16[256,1152]{1,0:T(8,128)(2,1)}, u32[]{:S(2)}, u32[]{:S(2)}) %collective-permute-start.3) | collective-permute-done | bytes 589856 | tf_op jit(solution)/shard_map/ppermute | solution.py:636
  66.9 8.3 %all-to-all-start.1 = ((bf16[32,8,2048]{2,1,0:T(8,128)(2,1)}), bf16[32,8,2048]{2,1,0:T(8,128)(2,1)S(1)}, u32[]{:S(2)}, u32[]{:S(2)}) async-start(bf16[32,8,2048]{2,1,0:T(8,128)(2,1)} %broadcast_in_dim.4), calls=%async_computation.1 | async-start | bytes 2097152 | tf_op jit(solution)/shard_map/all_to_all | solution.py:701
  76.0 11.9 %front.1 = (bf16[1024,256]{1,0:T(8,128)(2,1)}, bf16[1024,256]{1,0:T(8,128)(2,1)}, bf16[1024,256]{1,0:T(8,128)(2,1)}, bf16[256,256]{1,0:T(8,128)(2,1)}, bf16[256,...) custom-call(s32[2]{0:T(128)} %pad_add_fusion.place_ref, ...), custom_call_target="tpu_custom_call" | custom-call | flops 8000000000 | bytes 10000000 | tf_op jit(solution)/shard_map/front/pallas_call | solution.py:234
  90.9 8.4 %rows.5 = (bf16[8,8,80,1024]{3,2,1,0:T(8,128)(2,1)}, f32[8,128]{1,0:T(8,128)}) custom-call(s32[1]{0:T(128)} %bitcast.12.z_ref, bf16[256,1152]{1,0:T(8,128)(2,1)} %codes.1.refs_0_.refs_2_.gy_ref, bf16[256,1152]{1,0:T(8,128)(2,1)} %collective-permute-done.9.refs_1_.refs_3_, bf16[256,1152]{1,0:T(8,128)(2,1)} %collective-permute-done.3.refs_2_.refs_4_, ...), custom_call_target="tpu_custom_call" | custom-call | flops 4499999744 | bytes 12000000 | tf_op jit(solution)/shard_map/rows/pallas_call | solution.py:465
  99.6 5.6 %collective-permute-done.12.m1_ref = bf16[256,256]{1,0:T(8,128)(2,1)S(1)} collective-permute-done((bf16[256,256]{1,0:T(8,128)(2,1)}, bf16[256,256]{1,0:T(8,128)(2,1)S(1)}, u32[]{:S(2)}, u32[]{:S(2)}) %collective-permute-start.12) | collective-permute-done | bytes 131104 | tf_op jit(solution)/shard_map/ppermute | solution.py:636
  109.0 3.9 %mid.1 = (f32[256,1024]{1,0:T(8,128)}, bf16[256,1024]{1,0:T(8,128)(2,1)}) custom-call(bf16[256,1024]{1,0:T(8,128)(2,1)} %bitcast.71, bf16[256,256]{1,0:T(8,128)(2,1)} %get-tuple-element.138.m0_ref, bf16[256,256]{1,0:T(8,128)(2,1)} %copy-done.28, bf16[256,256]{1,0:T(8,128)(2,1)} %copy-done.29, bf16[256,256]{1,0:T(8,128)(2,1)} %copy-done.30, ...), custom_call_target="tpu_custom_call" | custom-call | flops 1000000000 | bytes 5000000 | tf_op jit(solution)/shard_map/mid/pallas_call | solution.py:258
  117.1 4.0 %rows.6 = (bf16[8,8,80,1024]{3,2,1,0:T(8,128)(2,1)}, f32[8,128]{1,0:T(8,128)}) custom-call(s32[1]{0:T(128)} %bitcast.12.z_ref, bf16[256,1152]{1,0:T(8,128)(2,1)} %copy-done.5, bf16[256,1152]{1,0:T(8,128)(2,1)} %copy-done.6, f32[8,128]{1,0:T(8,128)} %get-tuple-element.148.refs_2_, ...), custom_call_target="tpu_custom_call", output_to_operand_aliasing={{0}: (4, {})} | custom-call | flops 1500000000 | bytes 4000000 | tf_op jit(solution)/shard_map/rows/pallas_call | solution.py:465
  121.9 5.6 %rows.7 = (bf16[8,8,80,1024]{3,2,1,0:T(8,128)(2,1)}, f32[8,8,80,1]{3,2,1,0:T(8,128)}, f32[8,128]{1,0:T(8,128)}) custom-call(s32[1]{0:T(128)} %bitcast.12.z_ref, bf16[256,1024]{1,0:T(8,128)(2,1)} %get-tuple-element.152.refs_0_, bf16[256,1024]{1,0:T(8,128)(2,1)} %copy-done.35, bf16[256,1152]{1,0:T(8,128)(2,1)} %codes.1.refs_0_.refs_2_.gy_ref, ...), custom_call_target="tpu_custom_call" | custom-call | flops 1500000000 | bytes 4000000 | tf_op jit(solution)/shard_map/rows/pallas_call | solution.py:465
  132.8 8.9 %rows.8 = (bf16[8,8,80,1024]{3,2,1,0:T(8,128)(2,1)}, f32[8,8,80,1]{3,2,1,0:T(8,128)}, f32[8,128]{1,0:T(8,128)}) custom-call(s32[1]{0:T(128)} %bitcast.12.z_ref, bf16[256,1024]{1,0:T(8,128)(2,1)} %copy-done.20, bf16[256,1024]{1,0:T(8,128)(2,1)} %copy-done.23, bf16[256,1024]{1,0:T(8,128)(2,1)} %copy-done.21, ...), custom_call_target="tpu_custom_call", output_to_operand_aliasing={{0}: (11, {}), {1}: (12, {})} | custom-call | flops 3000000000 | bytes 8000000 | tf_op jit(solution)/shard_map/rows/pallas_call | solution.py:465
  147.7 5.6 %rows.9 = (bf16[8,8,80,1024]{3,2,1,0:T(8,128)(2,1)}, f32[8,8,80,1]{3,2,1,0:T(8,128)}, f32[8,128]{1,0:T(8,128)}) custom-call(s32[1]{0:T(128)} %bitcast.12.z_ref, bf16[256,1024]{1,0:T(8,128)(2,1)} %copy-done.22, bf16[256,1024]{1,0:T(8,128)(2,1)} %copy-done.25, bf16[256,1152]{1,0:T(8,128)(2,1)} %copy-done.5, ...), custom_call_target="tpu_custom_call", output_to_operand_aliasing={{0}: (7, {}), {1}: (8, {})} | custom-call | flops 1500000000 | bytes 4000000 | tf_op jit(solution)/shard_map/rows/pallas_call | solution.py:465
  153.2 41.3 %experts.1 = (bf16[8,640,256]{2,1,0:T(8,128)(2,1)}, bf16[8,2,768,512]{3,2,1,0:T(8,128)(2,1)}, bf16[4,256,1152]{2,1,0:T(8,128)(2,1)}, bf16[4,256,1152]{2,1,0:T(8,128)(2,1)}) custom-call(s32[1]{0:T(128)} %bitcast.12.z_ref, bf16[8,8,80,1024]{3,2,1,0:T(8,128)(2,1)} %get-tuple-element.163.x_ref, bf16[8,8,80,1024]{3,2,1,0:T(8,128)(2,1)} %get-tuple-element.164.gy_ref, ...), custom_call_target="tpu_custom_call" | custom-call | flops 24999999488 | bytes 60000000 | tf_op jit(solution)/shard_map/experts/pallas_call | solution.py:551
  195.4 4.4 %collective-permute-done.24 = bf16[4,256,1152]{2,1,0:T(8,128)(2,1)S(1)} collective-permute-done((bf16[4,256,1152]{2,1,0:T(8,128)(2,1)}, bf16[4,256,1152]{2,1,0:T(8,128)(2,1)S(1)}, u32[]{:S(2)}, u32[]{:S(2)}) %collective-permute-start.24) | collective-permute-done | bytes 2359328 | tf_op jit(solution)/shard_map/ppermute | solution.py:636
  201.2 2.6 collective-permute-start.25
  205.0 14.6 %expert_outs.1 = (bf16[4,256,1024]{2,1,0:T(8,128)(2,1)}, bf16[4,256,1024]{2,1,0:T(8,128)(2,1)}) custom-call(s32[1]{0:T(128)} %bitcast.12.z_ref, bf16[8,640,256]{2,1,0:T(8,128)(2,1)} %get-tuple-element.172.act_ref, bf16[16,1536,256]{2,1,0:T(8,128)(2,1)} %bitcast.93, bf16[256,1152]{1,0:T(8,128)(2,1)} %codes.1.refs_0_.refs_2_.gy_ref, ...), custom_call_target="tpu_custom_call" | custom-call | flops 6000000000 | bytes 12000000 | tf_op jit(solution)/shard_map/expert_outs/pallas_call | solution.py:599
  220.9 7.8 %collective-permute-done.25.part1_ref = bf16[256,1152]{1,0:T(8,128)(2,1)S(1)} collective-permute-done((bf16[256,1152]{1,0:T(8,128)(2,1)S(1)}, bf16[256,1152]{1,0:T(8,128)(2,1)S(1)}, u32[]{:S(2)}, u32[]{:S(2)}) %collective-permute-start.25) | collective-permute-done | bytes 589856 | tf_op jit(solution)/shard_map/ppermute | solution.py:636
  228.7 3.3 collective-permute-done.26.part2_ref
  233.0 7.6 %turn.1 = (bf16[256,256]{1,0:T(8,128)(2,1)}, bf16[256,256]{1,0:T(8,128)(2,1)}, bf16[256,256]{1,0:T(8,128)(2,1)}, bf16[256,256]{1,0:T(8,128)(2,1)}, f32[256,1024]...) custom-call(s32[2]{0:T(128)} %pad_add_fusion.place_ref, ...), custom_call_target="tpu_custom_call" | custom-call | flops 2000000000 | bytes 10000000 | tf_op jit(solution)/shard_map/turn/pallas_call | solution.py:299
  244.7 6.4 %collective-permute-done.32 = bf16[256,256]{1,0:T(8,128)(2,1)} collective-permute-done((bf16[256,256]{1,0:T(8,128)(2,1)}, bf16[256,256]{1,0:T(8,128)(2,1)}, u32[]{:S(2)}, u32[]{:S(2)}) %collective-permute-start.32) | collective-permute-done | bytes 131104 | tf_op jit(solution)/shard_map/ppermute | solution.py:636
  251.9 2.6 add_convert_fusion.1
  257.9 7.8 %all-to-all-start.2 = ((bf16[64,8,1024]{2,1,0:T(8,128)(2,1)}), bf16[64,8,1024]{2,1,0:T(8,128)(2,1)S(1)}, u32[]{:S(2)}, u32[]{:S(2)}) async-start(bf16[64,8,1024]{2,1,0:T(8,128)(2,1)} %bitcast.18), calls=%async_computation.2 | async-start | bytes 2097152 | tf_op jit(solution)/shard_map/all_to_all | solution.py:743
  266.5 16.6 %back.1 = (bf16[1024,512]{1,0:T(8,128)(2,1)}, bf16[2,256,1024]{2,1,0:T(8,128)(2,1)}, bf16[2,256,1024]{2,1,0:T(8,128)(2,1)}, f32[8,1024]{1,0:T(8,128)}) custom-call(s32[2]{0:T(128)} %pad_add_fusion.place_ref, bf16[1024,256]{1,0:T(8,128)(2,1)} %get-tuple-element.176.q_ref, bf16[1024,256]{1,0:T(8,128)(2,1)} %get-tuple-element.177.k_ref, ...), custom_call_target="tpu_custom_call" | custom-call | flops 20000000000 | bytes 16000000 | tf_op jit(solution)/shard_map/back/pallas_call | solution.py:363
  283.2 4.3 %collective-permute-start.36 = (bf16[2,256,1024]{2,1,0:T(8,128)(2,1)}, bf16[2,256,1024]{2,1,0:T(8,128)(2,1)}, u32[]{:S(2)}, u32[]{:S(2)}) collective-permute-start(bf16[2,256,1024]{2,1,0:T(8,128)(2,1)} %get-tuple-element.197), channel_id=1, source_target_pairs={{0,32},{32,0},{1,33},{33,1},{2,34},{34,2},{3,35},{35,3},{4,36},{36... | collective-permute-start | bytes 3145736 | tf_op jit(solution)/shard_map/ppermute | solution.py:636
  288.3 4.5 %projections.1 = bf16[1024,640]{1,0:T(8,128)(2,1)} custom-call(bf16[1024,1024]{1,0:T(8,128)(2,1)} %get-tuple-element.192.h_ref, bf16[1024,512]{1,0:T(8,128)(2,1)} %get-tuple-element.193.dqkv_ref, f32[1024,128]{1,0:T(8,128)} %get-tuple-element.194.sums_ref, f32[8,1024]{1,0:T(8,128)} %get-tuple-element.195.gain_ref), custom_call_target="tpu_custom_call" | custom-call | flops 1500000000 | bytes 5000000 | tf_op jit(solution)/shard_map/projections/pallas_call | solution.py:380
  292.7 7.0 %all-to-all-start.3 = ((bf16[128,8,640]{2,1,0:T(8,128)(2,1)}), bf16[128,8,640]{2,1,0:T(8,128)(2,1)S(1)}, u32[]{:S(2)}, u32[]{:S(2)}) async-start(bf16[128,8,640]{2,1,0:T(8,128)(2,1)} %bitcast.80), calls=%async_computation.3 | async-start | bytes 2621440 | tf_op jit(solution)/shard_map/all_to_all | solution.py:754
  308.4 2.5 finish.1
  311.0 9.6 %all-to-all-done.3 = bf16[128,8,640]{2,1,0:T(8,128)(2,1)S(1)} async-done(((bf16[128,8,640]{2,1,0:T(8,128)(2,1)}), bf16[128,8,640]{2,1,0:T(8,128)(2,1)S(1)}, u32[]{:S(2)}, u32[]{:S(2)}) %all-to-all-start.3) | async-done | bytes 1310752 | tf_op jit(solution)/shard_map/all_to_all | solution.py:754
  320.6 6.1 %collective-permute-done.37 = bf16[256,1024]{1,0:T(8,128)(2,1)} collective-permute-done((bf16[256,1024]{1,0:T(8,128)(2,1)}, bf16[256,1024]{1,0:T(8,128)(2,1)}, u32[]{:S(2)}, u32[]{:S(2)}) %collective-permute-start.37) | collective-permute-done | bytes 524320 | tf_op jit(solution)/shard_map/ppermute | solution.py:636
  330.3 3.4 %fusion.6 = (f32[1,256,1024]{2,1,0:T(8,128)}, bf16[1,256,1024]{2,1,0:T(8,128)(2,1)}) fusion(f32[256,1024]{1,0:T(8,128)S(1)} %copy-done.9, bf16[256,1024]{1,0:T(8,128)(2,1)S(1)} %bitcast.76, bf16[256,1024]{1,0:T(8,128)(2,1)} %collective-permute-done.37, f32[256]{0:T(256)S(1)} %broadcast_multiply_fusion, f32[1024]{0:T(1024)S(1)} %bitcast.87, ...), kind=kLoop, calls=%fused_computation.16 | loop fusion | flops 5242880 | bytes 7870465 | tf_op jit(solution)/shard_map/reshape | solution.py:774
  (181 shorter events, 72.7 us)
Async XLA Ops:
  7.2 146.1 %all-gather.3.cloned.1.call-start = ((), (), s32[]{:S(2)}) async-start(), calls=%async_computation.6 | async-start | bytes 13369344 | tf_op jit(solution)/shard_map/all_gather | solution.py:688
  7.2 13.8 %collective-permute-start.1 = (bf16[256,1024]{1,0:T(8,128)(2,1)}, bf16[256,1024]{1,0:T(8,128)(2,1)}, u32[]{:S(2)}, u32[]{:S(2)}) collective-permute-start(bf16[256,1024]{1,0:T(8,128)(2,1)} %bitcast.69), channel_id=1, source_target_pairs={{0,64},{64,0},{1,65},{65,1},{2,66},{66,2},{3,67},{67,3},{4,68},{68... | collective-permute-start | bytes 1572872 | tf_op jit(solution)/shard_map/ppermute | solution.py:636
  21.0 43.4 %all-to-all-start = ((bf16[128,8,640]{2,1,0:T(8,128)(2,1)}), bf16[128,8,640]{2,1,0:T(8,128)(2,1)S(1)}, u32[]{:S(2)}, u32[]{:S(2)}) async-start(bf16[128,8,640]{2,1,0:T(8,128)(2,1)} %get-tuple-element.115), calls=%async_computation | async-start | bytes 2621440 | tf_op jit(solution)/shard_map/all_to_all | solution.py:690
  36.2 28.2 %collective-permute-start.3 = (bf16[256,1152]{1,0:T(8,128)(2,1)}, bf16[256,1152]{1,0:T(8,128)(2,1)}, u32[]{:S(2)}, u32[]{:S(2)}) collective-permute-start(bf16[256,1152]{1,0:T(8,128)(2,1)} %codes.1.refs_0_.refs_2_.gy_ref), channel_id=1, source_target_pairs={{0,1},{1,2},{2,3},{3,0},{4,5},{5,6},{6,7},{7,4},{8,9},{9,10},{10,1... | collective-permute-start | bytes 1769480 | tf_op jit(solution)/shard_map/ppermute | solution.py:636
  37.7 26.8 %collective-permute-start.4 = (bf16[256,1152]{1,0:T(8,128)(2,1)}, bf16[256,1152]{1,0:T(8,128)(2,1)S(1)}, u32[]{:S(2)}, u32[]{:S(2)}) collective-permute-start(bf16[256,1152]{1,0:T(8,128)(2,1)} %codes.1.refs_0_.refs_2_.gy_ref), channel_id=1, source_target_pairs={{0,3},{1,0},{2,1},{3,2},{4,7},{5,4},{6,5},{7,6},{8,11},{9,8},{10,9... | collective-permute-start | bytes 1769480 | tf_op jit(solution)/shard_map/ppermute | solution.py:636
  39.5 35.8 %collective-permute-start.6 = (bf16[256,1024]{1,0:T(8,128)(2,1)S(1)}, bf16[256,1024]{1,0:T(8,128)(2,1)}, u32[]{:S(2)}, u32[]{:S(2)}) collective-permute-start(bf16[256,1024]{1,0:T(8,128)(2,1)S(1)} %bitcast.73), channel_id=1, source_target_pairs={{0,32},{32,0},{1,33},{33,1},{2,34},{34,2},{3,35},{35,3},{4,36},{36... | collective-permute-start | bytes 1572872 | tf_op jit(solution)/shard_map/ppermute | solution.py:636
  40.5 35.5 %collective-permute-start.7 = (bf16[256,1024]{1,0:T(8,128)(2,1)}, bf16[256,1024]{1,0:T(8,128)(2,1)}, u32[]{:S(2)}, u32[]{:S(2)}) collective-permute-start(bf16[256,1024]{1,0:T(8,128)(2,1)} %collective-permute-done.1.x1_ref), channel_id=1, source_target_pairs={{0,32},{32,0},{1,33},{33,1},{2,34},{34,2},{3,35},{35,3},{4,36},{36... | collective-permute-start | bytes 1572872 | tf_op jit(solution)/shard_map/ppermute | solution.py:636
  44.5 43.5 %collective-permute-start.9 = (bf16[256,1152]{1,0:T(8,128)(2,1)}, bf16[256,1152]{1,0:T(8,128)(2,1)}, u32[]{:S(2)}, u32[]{:S(2)}) collective-permute-start(bf16[256,1152]{1,0:T(8,128)(2,1)} %codes.1.refs_0_.refs_2_.gy_ref), channel_id=1, source_target_pairs={{0,32},{32,0},{1,33},{33,1},{2,34},{34,2},{3,35},{35,3},{4,36},{36... | collective-permute-start | bytes 1769480 | tf_op jit(solution)/shard_map/ppermute | solution.py:636
  64.3 35.3 %collective-permute-start.5 = (bf16[256,1152]{1,0:T(8,128)(2,1)}, bf16[256,1152]{1,0:T(8,128)(2,1)S(1)}, u32[]{:S(2)}, u32[]{:S(2)}) collective-permute-start(bf16[256,1152]{1,0:T(8,128)(2,1)} %codes.1.refs_0_.refs_2_.gy_ref), channel_id=1, source_target_pairs={{0,2},{1,3},{2,0},{3,1},{4,6},{5,7},{6,4},{7,5},{8,10},{9,11},{10,... | collective-permute-start | bytes 1769480 | tf_op jit(solution)/shard_map/ppermute | solution.py:636
  64.5 25.0 %collective-permute-start.10 = (bf16[256,1152]{1,0:T(8,128)(2,1)}, bf16[256,1152]{1,0:T(8,128)(2,1)}, u32[]{:S(2)}, u32[]{:S(2)}) collective-permute-start(bf16[256,1152]{1,0:T(8,128)(2,1)} %collective-permute-done.3.refs_2_.refs_4_), channel_id=1, source_target_pairs={{0,32},{32,0},{1,33},{33,1},{2,34},{34,2},{3,35},{35,3},{4,36},{36... | collective-permute-start | bytes 1769480 | tf_op jit(solution)/shard_map/ppermute | solution.py:636
  66.9 38.3 %all-to-all-start.1 = ((bf16[32,8,2048]{2,1,0:T(8,128)(2,1)}), bf16[32,8,2048]{2,1,0:T(8,128)(2,1)S(1)}, u32[]{:S(2)}, u32[]{:S(2)}) async-start(bf16[32,8,2048]{2,1,0:T(8,128)(2,1)} %broadcast_in_dim.4), calls=%async_computation.1 | async-start | bytes 2097152 | tf_op jit(solution)/shard_map/all_to_all | solution.py:701
  75.2 229.6 %reduce-scatter.2.cloned.1.call-start = ((), (), s32[]{:S(2)}) async-start(), calls=%async_computation.5 | async-start | bytes 13369344 | tf_op jit(solution)/shard_map/reduce_scatter | solution.py:732
  75.3 14.8 %collective-permute-start.11 = (bf16[256,1152]{1,0:T(8,128)(2,1)}, bf16[256,1152]{1,0:T(8,128)(2,1)S(1)}, u32[]{:S(2)}, u32[]{:S(2)}) collective-permute-start(bf16[256,1152]{1,0:T(8,128)(2,1)} %copy-done.11), channel_id=1, source_target_pairs={{0,32},{32,0},{1,33},{33,1},{2,34},{34,2},{3,35},{35,3},{4,36},{36... | collective-permute-start | bytes 1769480 | tf_op jit(solution)/shard_map/ppermute | solution.py:636
  88.0 17.2 %collective-permute-start.12 = (bf16[256,256]{1,0:T(8,128)(2,1)}, bf16[256,256]{1,0:T(8,128)(2,1)S(1)}, u32[]{:S(2)}, u32[]{:S(2)}) collective-permute-start(bf16[256,256]{1,0:T(8,128)(2,1)} %get-tuple-element.135), channel_id=1, source_target_pairs={{0,64},{64,0},{1,65},{65,1},{2,66},{66,2},{3,67},{67,3},{4,68},{68... | collective-permute-start | bytes 393224 | tf_op jit(solution)/shard_map/ppermute | solution.py:636
  89.5 15.8 %collective-permute-start.13 = (bf16[256,256]{1,0:T(8,128)(2,1)}, bf16[256,256]{1,0:T(8,128)(2,1)S(1)}, u32[]{:S(2)}, u32[]{:S(2)}) collective-permute-start(bf16[256,256]{1,0:T(8,128)(2,1)} %get-tuple-element.136), channel_id=1, source_target_pairs={{0,32},{32,0},{1,33},{33,1},{2,34},{34,2},{3,35},{35,3},{4,36},{36... | collective-permute-start | bytes 393224 | tf_op jit(solution)/shard_map/ppermute | solution.py:636
  113.3 15.2 %collective-permute-start.16 = (bf16[256,1024]{1,0:T(8,128)(2,1)}, bf16[256,1024]{1,0:T(8,128)(2,1)S(1)}, u32[]{:S(2)}, u32[]{:S(2)}) collective-permute-start(bf16[256,1024]{1,0:T(8,128)(2,1)} %get-tuple-element.152.refs_0_), channel_id=1, source_target_pairs={{0,1},{1,2},{2,3},{3,0},{4,5},{5,6},{6,7},{7,4},{8,9},{9,10},{10,1... | collective-permute-start | bytes 1572872 | tf_op jit(solution)/shard_map/ppermute | solution.py:636
  114.8 13.7 %collective-permute-start.17 = (bf16[256,1024]{1,0:T(8,128)(2,1)}, bf16[256,1024]{1,0:T(8,128)(2,1)S(1)}, u32[]{:S(2)}, u32[]{:S(2)}) collective-permute-start(bf16[256,1024]{1,0:T(8,128)(2,1)} %get-tuple-element.152.refs_0_), channel_id=1, source_target_pairs={{0,3},{1,0},{2,1},{3,2},{4,7},{5,4},{6,5},{7,6},{8,11},{9,8},{10,9... | collective-permute-start | bytes 1572872 | tf_op jit(solution)/shard_map/ppermute | solution.py:636
  129.5 14.6 %collective-permute-start.20 = (bf16[256,1024]{1,0:T(8,128)(2,1)S(1)}, bf16[256,1024]{1,0:T(8,128)(2,1)S(1)}, u32[]{:S(2)}, u32[]{:S(2)}) collective-permute-start(bf16[256,1024]{1,0:T(8,128)(2,1)S(1)} %copy-done.34), channel_id=1, source_target_pairs={{0,2},{1,3},{2,0},{3,1},{4,6},{5,7},{6,4},{7,5},{8,10},{9,11},{10,... | collective-permute-start | bytes 1572872 | tf_op jit(solution)/shard_map/ppermute | solution.py:636
  201.2 27.4 %collective-permute-start.25 = (bf16[256,1152]{1,0:T(8,128)(2,1)S(1)}, bf16[256,1152]{1,0:T(8,128)(2,1)S(1)}, u32[]{:S(2)}, u32[]{:S(2)}) collective-permute-start(bf16[256,1152]{1,0:T(8,128)(2,1)S(1)} %get-tuple-element.216), channel_id=1, source_target_pairs={{0,3},{1,0},{2,1},{3,2},{4,7},{5,4},{6,5},{7,6},{8,11},{9,8},{10,9... | collective-permute-start | bytes 1769480 | tf_op jit(solution)/shard_map/ppermute | solution.py:636
  203.8 28.2 %collective-permute-start.26 = (bf16[256,1152]{1,0:T(8,128)(2,1)S(1)}, bf16[256,1152]{1,0:T(8,128)(2,1)S(1)}, u32[]{:S(2)}, u32[]{:S(2)}) collective-permute-start(bf16[256,1152]{1,0:T(8,128)(2,1)S(1)} %get-tuple-element.215), channel_id=1, source_target_pairs={{0,1},{1,2},{2,3},{3,0},{4,5},{5,6},{6,7},{7,4},{8,9},{9,10},{10,1... | collective-permute-start | bytes 1769480 | tf_op jit(solution)/shard_map/ppermute | solution.py:636
  203.8 28.2 %collective-permute-start.27 = (bf16[256,1152]{1,0:T(8,128)(2,1)S(1)}, bf16[256,1152]{1,0:T(8,128)(2,1)S(1)}, u32[]{:S(2)}, u32[]{:S(2)}) collective-permute-start(bf16[256,1152]{1,0:T(8,128)(2,1)S(1)} %get-tuple-element.214), channel_id=1, source_target_pairs={{0,2},{1,3},{2,0},{3,1},{4,6},{5,7},{6,4},{7,5},{8,10},{9,11},{10,... | collective-permute-start | bytes 1769480 | tf_op jit(solution)/shard_map/ppermute | solution.py:636
  219.7 34.8 %collective-permute-start.29 = (bf16[4,256,1024]{2,1,0:T(8,128)(2,1)}, bf16[4,256,1024]{2,1,0:T(8,128)(2,1)S(1)}, u32[]{:S(2)}, u32[]{:S(2)}) collective-permute-start(bf16[4,256,1024]{2,1,0:T(8,128)(2,1)} %get-tuple-element.174), channel_id=1, source_target_pairs={{0,32},{32,0},{1,33},{33,1},{2,34},{34,2},{3,35},{35,3},{4,36},{36... | collective-permute-start | bytes 6291464 | tf_op jit(solution)/shard_map/ppermute | solution.py:636
  243.0 22.8 %collective-permute-start.30 = (bf16[256,256]{1,0:T(8,128)(2,1)}, bf16[256,256]{1,0:T(8,128)(2,1)S(1)}, u32[]{:S(2)}, u32[]{:S(2)}) collective-permute-start(bf16[256,256]{1,0:T(8,128)(2,1)} %get-tuple-element.180), channel_id=1, source_target_pairs={{0,64},{64,0},{1,65},{65,1},{2,66},{66,2},{3,67},{67,3},{4,68},{68... | collective-permute-start | bytes 393224 | tf_op jit(solution)/shard_map/ppermute | solution.py:636
  244.0 21.8 %collective-permute-start.31 = (bf16[256,256]{1,0:T(8,128)(2,1)}, bf16[256,256]{1,0:T(8,128)(2,1)S(1)}, u32[]{:S(2)}, u32[]{:S(2)}) collective-permute-start(bf16[256,256]{1,0:T(8,128)(2,1)} %get-tuple-element.181), channel_id=1, source_target_pairs={{0,32},{32,0},{1,33},{33,1},{2,34},{34,2},{3,35},{35,3},{4,36},{36... | collective-permute-start | bytes 393224 | tf_op jit(solution)/shard_map/ppermute | solution.py:636
  251.0 14.8 %collective-permute-start.33 = (bf16[256,256]{1,0:T(8,128)(2,1)}, bf16[256,256]{1,0:T(8,128)(2,1)S(1)}, u32[]{:S(2)}, u32[]{:S(2)}) collective-permute-start(bf16[256,256]{1,0:T(8,128)(2,1)} %collective-permute-done.32), channel_id=1, source_target_pairs={{0,32},{32,0},{1,33},{33,1},{2,34},{34,2},{3,35},{35,3},{4,36},{36... | collective-permute-start | bytes 393224 | tf_op jit(solution)/shard_map/ppermute | solution.py:636
  256.5 26.7 %collective-permute-start.34 = (bf16[256,1024]{1,0:T(8,128)(2,1)}, bf16[256,1024]{1,0:T(8,128)(2,1)S(1)}, u32[]{:S(2)}, u32[]{:S(2)}) collective-permute-start(bf16[256,1024]{1,0:T(8,128)(2,1)} %get-tuple-element.188), channel_id=1, source_target_pairs={{0,3},{1,0},{2,1},{3,2},{4,7},{5,4},{6,5},{7,6},{8,11},{9,8},{10,9... | collective-permute-start | bytes 1572872 | tf_op jit(solution)/shard_map/ppermute | solution.py:636
  256.5 26.7 %collective-permute-start.35 = (bf16[256,1024]{1,0:T(8,128)(2,1)S(1)}, bf16[256,1024]{1,0:T(8,128)(2,1)S(1)}, u32[]{:S(2)}, u32[]{:S(2)}) collective-permute-start(bf16[256,1024]{1,0:T(8,128)(2,1)S(1)} %get-tuple-element.189), channel_id=1, source_target_pairs={{0,1},{1,2},{2,3},{3,0},{4,5},{5,6},{6,7},{7,4},{8,9},{9,10},{10,1... | collective-permute-start | bytes 1572872 | tf_op jit(solution)/shard_map/ppermute | solution.py:636
  257.9 25.2 %all-to-all-start.2 = ((bf16[64,8,1024]{2,1,0:T(8,128)(2,1)}), bf16[64,8,1024]{2,1,0:T(8,128)(2,1)S(1)}, u32[]{:S(2)}, u32[]{:S(2)}) async-start(bf16[64,8,1024]{2,1,0:T(8,128)(2,1)} %bitcast.18), calls=%async_computation.2 | async-start | bytes 2097152 | tf_op jit(solution)/shard_map/all_to_all | solution.py:743
  283.2 17.4 %collective-permute-start.36 = (bf16[2,256,1024]{2,1,0:T(8,128)(2,1)}, bf16[2,256,1024]{2,1,0:T(8,128)(2,1)}, u32[]{:S(2)}, u32[]{:S(2)}) collective-permute-start(bf16[2,256,1024]{2,1,0:T(8,128)(2,1)} %get-tuple-element.197), channel_id=1, source_target_pairs={{0,32},{32,0},{1,33},{33,1},{2,34},{34,2},{3,35},{35,3},{4,36},{36... | collective-permute-start | bytes 3145736 | tf_op jit(solution)/shard_map/ppermute | solution.py:636
  288.3 22.7 %collective-permute-start.38 = (bf16[256,1024]{1,0:T(8,128)(2,1)}, bf16[256,1024]{1,0:T(8,128)(2,1)}, u32[]{:S(2)}, u32[]{:S(2)}) collective-permute-start(bf16[256,1024]{1,0:T(8,128)(2,1)} %get-tuple-element.198), channel_id=1, source_target_pairs={{0,2},{1,3},{2,0},{3,1},{4,6},{5,7},{6,4},{7,5},{8,10},{9,11},{10,... | collective-permute-start | bytes 1572872 | tf_op jit(solution)/shard_map/ppermute | solution.py:636
  292.7 27.8 %all-to-all-start.3 = ((bf16[128,8,640]{2,1,0:T(8,128)(2,1)}), bf16[128,8,640]{2,1,0:T(8,128)(2,1)S(1)}, u32[]{:S(2)}, u32[]{:S(2)}) async-start(bf16[128,8,640]{2,1,0:T(8,128)(2,1)} %bitcast.80), calls=%async_computation.3 | async-start | bytes 2621440 | tf_op jit(solution)/shard_map/all_to_all | solution.py:754
  303.4 23.2 %collective-permute-start.37 = (bf16[256,1024]{1,0:T(8,128)(2,1)}, bf16[256,1024]{1,0:T(8,128)(2,1)}, u32[]{:S(2)}, u32[]{:S(2)}) collective-permute-start(bf16[256,1024]{1,0:T(8,128)(2,1)} %select_bitcast_fusion), channel_id=1, source_target_pairs={{0,64},{64,0},{1,65},{65,1},{2,66},{66,2},{3,67},{67,3},{4,68},{68... | collective-permute-start | bytes 1572872 | tf_op jit(solution)/shard_map/ppermute | solution.py:636
  (53 other events, 296.6 us)
Sparse Core Ops, SparseCore 0:
  21.1 119.9 all-gather.2
  194.7 100.7 reduce-scatter.1

commit v7 on v2

--- a/solution.py
+++ b/solution.py
@@ -520,8 +520,8 @@
         x = x_ref[0, blocks].reshape(step * CAP, D)
         gate = gate_ref[0, blocks].reshape(step * CAP, 1)
         da = dot(gy_ref[0, blocks].reshape(step * CAP, D), down_w, NT)
-        g = dot(x, gate_w)
-        u = dot(x, up_w)
+        both = dot(x, both_w)
+        g, u = both[:, :HALF], both[:, HALF:]
         s = jax.nn.sigmoid(g)
         silu = g * s
         act = silu * u
@@ -546,8 +546,7 @@
                 b = 2 * j + c
                 place = as_bf16(dot(codes_kept[b][:, :EXPERTS], spread[...]) == start[...])
                 out[j, :, :D] = dot(place, kept[b].reshape(SLOTS, D)).astype(bf16)
-                high, low = split(mine[...] * dgates[b].reshape(SLOTS, 1))
-                scattered = dot(place, high) + dot(place, low)
+                scattered = dot(place, (mine[...] * dgates[b].reshape(SLOTS, 1)).astype(bf16))
                 out[j, :, D:] = jnp.concatenate([scattered, jnp.zeros((TOK, 128 - EXPERTS), f32)], axis=1).astype(bf16)
             return carry
 

time: 346 us -> 345 us (level)
  the two profiles are of different devices: /device:TPU:79 before, /device:TPU:1 now
where the time goes in v7:
time: 345 us; the launch traced here: 338 us
  Pallas kernels  140 us (41%)
  starting transfers between devices  84 us (24%)
  waiting for transfers between devices  69.2 us (20%)
  other arithmetic  20 us (6%)
  between operations  14.6 us (4%)
  local copies, waits for them, and re-layouts  9.82 us (3%)
    ppermute x40, waiting for transfers between devices, shift(): return lax.ppermute(values, axis, [(i, (i + by) % n) for i in range(n)])  53.5 us
    ppermute x40, starting transfers between devices, shift(): return lax.ppermute(values, axis, [(i, (i + by) % n) for i in range(n)])  50.8 us
    pallas_call x1, Pallas kernels, main(): call(main_kernel, 'experts', 25000000000, 60000000, grid=(SHARE,), in_spe...  41.3 us
    pallas_call x3, Pallas kernels, rows_of(): call(functools.partial(rows_kernel, n, with_gates), 'rows', n * 750000000...  30.3 us
    pallas_call x1, Pallas kernels, back(): call(back_kernel, 'back', 20000000000, 16000000, in_specs=[SCALAR] + [VEC...  16.6 us
    pallas_call x1, Pallas kernels, outs(): call(outs_kernel, 'expert_outs', 6000000000, 12000000, grid=(SHARE,), in_...  14.7 us
    all_to_all x1, waiting for transfers between devices, on_device(): lax.all_to_all(first.reshape(128, 8, 640), AXES, split_axis=0, concat_axi...  12.4 us
    pallas_call x1, Pallas kernels, front(): call(front_kernel, 'front', 8000000000, 10000000, in_specs=[SCALAR] + [VE...  12.1 us
  transfers between devices with their start and end apart: 46, of which 18 were waited for; matrix products, arithmetic and copies ran while one was open for 6% of the time, Pallas kernels for 29%

profile of v7, /device:TPU:1, one launch (start us, length us, event | category | flops | bytes accessed | tf_op | source)
XLA Modules:
  0.0 338.2 jit_solution(16625537253225083170)
XLA Ops:
  10.2 11.5 %all-to-all-start = ((bf16[128,8,640]{2,1,0:T(8,128)(2,1)}), bf16[128,8,640]{2,1,0:T(8,128)(2,1)S(1)}, u32[]{:S(2)}, u32[]{:S(2)}) async-start(bf16[128,8,640]{2,1,0:T(8,128)(2,1)} %get-tuple-element.100), calls=%async_computation | async-start | bytes 2621440 | tf_op jit(solution)/shard_map/all_to_all | solution.py:693
  28.6 19.9 %collective-permute-done.2.x1_ref = bf16[256,1024]{1,0:T(8,128)(2,1)S(1)} collective-permute-done((bf16[256,1024]{1,0:T(8,128)(2,1)S(1)}, bf16[256,1024]{1,0:T(8,128)(2,1)S(1)}, u32[]{:S(2)}, u32[]{:S(2)}) %collective-permute-start.2) | collective-permute-done | bytes 524320 | tf_op jit(solution)/shard_map/ppermute | solution.py:643
  49.5 2.5 codes.1.refs_0_.refs_2_.gy_ref
  52.0 3.1 collective-permute-start.10
  60.0 8.6 %all-to-all-start.1 = ((bf16[32,8,2048]{2,1,0:T(8,128)(2,1)}), bf16[32,8,2048]{2,1,0:T(8,128)(2,1)S(1)}, u32[]{:S(2)}, u32[]{:S(2)}) async-start(bf16[32,8,2048]{2,1,0:T(8,128)(2,1)} %broadcast_in_dim.4), calls=%async_computation.1 | async-start | bytes 2097152 | tf_op jit(solution)/shard_map/all_to_all | solution.py:708
  69.2 3.1 multiply_sine_fusion
  72.3 12.1 %front.1 = (bf16[1024,256]{1,0:T(8,128)(2,1)}, bf16[1024,256]{1,0:T(8,128)(2,1)}, bf16[1024,256]{1,0:T(8,128)(2,1)}, bf16[256,256]{1,0:T(8,128)(2,1)}, bf16[256,...) custom-call(s32[2]{0:T(128)} %pad_add_fusion.place_ref, ...), custom_call_target="tpu_custom_call" | custom-call | flops 8000000000 | bytes 10000000 | tf_op jit(solution)/shard_map/front/pallas_call | solution.py:234
  85.9 6.7 %collective-permute-start.6 = (bf16[256,256]{1,0:T(8,128)(2,1)}, bf16[256,256]{1,0:T(8,128)(2,1)S(1)}, u32[]{:S(2)}, u32[]{:S(2)}) collective-permute-start(bf16[256,256]{1,0:T(8,128)(2,1)} %get-tuple-element.109), channel_id=1, source_target_pairs={{0,32},{32,0},{1,33},{33,1},{2,34},{34,2},{3,35},{35,3},{4,36},{36... | collective-permute-start | bytes 393224 | tf_op jit(solution)/shard_map/ppermute | solution.py:643
  100.1 3.8 %mid.1 = (f32[256,1024]{1,0:T(8,128)}, bf16[256,1024]{1,0:T(8,128)(2,1)}) custom-call(bf16[256,1024]{1,0:T(8,128)(2,1)} %bitcast.69, bf16[256,256]{1,0:T(8,128)(2,1)} %get-tuple-element.111.m0_ref, bf16[256,256]{1,0:T(8,128)(2,1)} %copy-done.29, bf16[256,256]{1,0:T(8,128)(2,1)} %copy-done.30, bf16[256,256]{1,0:T(8,128)(2,1)} %copy-done.31, ...), custom_call_target="tpu_custom_call" | custom-call | flops 1000000000 | bytes 5000000 | tf_op jit(solution)/shard_map/mid/pallas_call | solution.py:258
  104.5 2.7 collective-permute-start.14
  107.9 10.4 %rows.3 = (bf16[8,8,80,1024]{3,2,1,0:T(8,128)(2,1)}, f32[8,128]{1,0:T(8,128)}) custom-call(s32[1]{0:T(128)} %bitcast.12.z_ref, bf16[256,1152]{1,0:T(8,128)(2,1)} %codes.1.refs_0_.refs_2_.gy_ref, bf16[256,1152]{1,0:T(8,128)(2,1)} %collective-permute-done.17.refs_1_.refs_3_, bf16[256,1152]{1,0:T(8,128)(2,1)} %collective-permute-done.9.refs_2_.refs_6_, ...), custom_call_target="tpu_custom_call" | custom-call | flops 6000000000 | bytes 16000000 | tf_op jit(solution)/shard_map/rows/pallas_call | solution.py:472
  119.1 6.1 %rows.4 = (bf16[8,8,80,1024]{3,2,1,0:T(8,128)(2,1)}, f32[8,8,80,1]{3,2,1,0:T(8,128)}, f32[8,128]{1,0:T(8,128)}) custom-call(s32[1]{0:T(128)} %bitcast.12.z_ref, bf16[256,1024]{1,0:T(8,128)(2,1)} %get-tuple-element.118.refs_0_, bf16[256,1024]{1,0:T(8,128)(2,1)} %copy-done.37, bf16[256,1152]{1,0:T(8,128)(2,1)} %codes.1.refs_0_.refs_2_.gy_ref, ...), custom_call_target="tpu_custom_call" | custom-call | flops 1500000000 | bytes 4000000 | tf_op jit(solution)/shard_map/rows/pallas_call | solution.py:472
  125.2 4.2 %collective-permute-done.14.refs_2_ = bf16[256,1024]{1,0:T(8,128)(2,1)S(1)} collective-permute-done((bf16[256,1024]{1,0:T(8,128)(2,1)}, bf16[256,1024]{1,0:T(8,128)(2,1)S(1)}, u32[]{:S(2)}, u32[]{:S(2)}) %collective-permute-start.14) | collective-permute-done | bytes 524320 | tf_op jit(solution)/shard_map/ppermute | solution.py:643
  135.4 13.8 %rows.5 = (bf16[8,8,80,1024]{3,2,1,0:T(8,128)(2,1)}, f32[8,8,80,1]{3,2,1,0:T(8,128)}, f32[8,128]{1,0:T(8,128)}) custom-call(s32[1]{0:T(128)} %bitcast.12.z_ref, bf16[256,1024]{1,0:T(8,128)(2,1)} %copy-done.21, bf16[256,1024]{1,0:T(8,128)(2,1)} %copy-done.24, bf16[256,1024]{1,0:T(8,128)(2,1)} %copy-done.22, ...), custom_call_target="tpu_custom_call", output_to_operand_aliasing={{0}: (15, {}), {1}: (16, {})} | custom-call | flops 4499999744 | bytes 12000000 | tf_op jit(solution)/shard_map/rows/pallas_call | solution.py:472
  151.7 41.3 %experts.1 = (bf16[8,640,256]{2,1,0:T(8,128)(2,1)}, bf16[8,2,768,512]{3,2,1,0:T(8,128)(2,1)}, bf16[4,256,1152]{2,1,0:T(8,128)(2,1)}, bf16[4,256,1152]{2,1,0:T(8,128)(2,1)}) custom-call(s32[1]{0:T(128)} %bitcast.12.z_ref, bf16[8,8,80,1024]{3,2,1,0:T(8,128)(2,1)} %get-tuple-element.132.x_ref, bf16[8,8,80,1024]{3,2,1,0:T(8,128)(2,1)} %get-tuple-element.133.gy_ref, ...), custom_call_target="tpu_custom_call" | custom-call | flops 24999999488 | bytes 60000000 | tf_op jit(solution)/shard_map/experts/pallas_call | solution.py:558
  193.9 4.4 %collective-permute-done.24 = bf16[4,256,1152]{2,1,0:T(8,128)(2,1)S(1)} collective-permute-done((bf16[4,256,1152]{2,1,0:T(8,128)(2,1)}, bf16[4,256,1152]{2,1,0:T(8,128)(2,1)S(1)}, u32[]{:S(2)}, u32[]{:S(2)}) %collective-permute-start.24) | collective-permute-done | bytes 2359328 | tf_op jit(solution)/shard_map/ppermute | solution.py:643
  199.8 2.7 collective-permute-start.25
  204.1 14.7 %expert_outs.1 = (bf16[4,256,1024]{2,1,0:T(8,128)(2,1)}, bf16[4,256,1024]{2,1,0:T(8,128)(2,1)}) custom-call(s32[1]{0:T(128)} %bitcast.12.z_ref, bf16[8,640,256]{2,1,0:T(8,128)(2,1)} %get-tuple-element.141.act_ref, bf16[16,1536,256]{2,1,0:T(8,128)(2,1)} %bitcast.92, bf16[256,1152]{1,0:T(8,128)(2,1)} %codes.1.refs_0_.refs_2_.gy_ref, ...), custom_call_target="tpu_custom_call" | custom-call | flops 6000000000 | bytes 12000000 | tf_op jit(solution)/shard_map/expert_outs/pallas_call | solution.py:606
  219.9 7.3 %collective-permute-done.25.part1_ref = bf16[256,1152]{1,0:T(8,128)(2,1)S(1)} collective-permute-done((bf16[256,1152]{1,0:T(8,128)(2,1)S(1)}, bf16[256,1152]{1,0:T(8,128)(2,1)S(1)}, u32[]{:S(2)}, u32[]{:S(2)}) %collective-permute-start.25) | collective-permute-done | bytes 589856 | tf_op jit(solution)/shard_map/ppermute | solution.py:643
  230.4 7.8 %turn.1 = (bf16[256,256]{1,0:T(8,128)(2,1)}, bf16[256,256]{1,0:T(8,128)(2,1)}, bf16[256,256]{1,0:T(8,128)(2,1)}, bf16[256,256]{1,0:T(8,128)(2,1)}, f32[256,1024]...) custom-call(s32[2]{0:T(128)} %pad_add_fusion.place_ref, ...), custom_call_target="tpu_custom_call" | custom-call | flops 2000000000 | bytes 10000000 | tf_op jit(solution)/shard_map/turn/pallas_call | solution.py:299
  238.2 2.9 collective-permute-start.28
  243.2 6.0 %collective-permute-done.32 = bf16[256,256]{1,0:T(8,128)(2,1)S(1)} collective-permute-done((bf16[256,256]{1,0:T(8,128)(2,1)}, bf16[256,256]{1,0:T(8,128)(2,1)S(1)}, u32[]{:S(2)}, u32[]{:S(2)}) %collective-permute-start.32) | collective-permute-done | bytes 131104 | tf_op jit(solution)/shard_map/ppermute | solution.py:643
  250.3 2.6 add_convert_fusion.1
  256.5 7.3 %all-to-all-start.2 = ((bf16[64,8,1024]{2,1,0:T(8,128)(2,1)}), bf16[64,8,1024]{2,1,0:T(8,128)(2,1)S(1)}, u32[]{:S(2)}, u32[]{:S(2)}) async-start(bf16[64,8,1024]{2,1,0:T(8,128)(2,1)} %bitcast.18), calls=%async_computation.2 | async-start | bytes 2097152 | tf_op jit(solution)/shard_map/all_to_all | solution.py:745
  263.9 16.6 %back.1 = (bf16[1024,512]{1,0:T(8,128)(2,1)}, bf16[2,256,1024]{2,1,0:T(8,128)(2,1)}, bf16[2,256,1024]{2,1,0:T(8,128)(2,1)}, f32[8,1024]{1,0:T(8,128)}) custom-call(s32[2]{0:T(128)} %pad_add_fusion.place_ref, bf16[1024,256]{1,0:T(8,128)(2,1)} %get-tuple-element.149.q_ref, bf16[1024,256]{1,0:T(8,128)(2,1)} %get-tuple-element.150.k_ref, ...), custom_call_target="tpu_custom_call" | custom-call | flops 20000000000 | bytes 16000000 | tf_op jit(solution)/shard_map/back/pallas_call | solution.py:363
  280.5 6.2 %collective-permute-start.36 = (bf16[2,256,1024]{2,1,0:T(8,128)(2,1)}, bf16[2,256,1024]{2,1,0:T(8,128)(2,1)}, u32[]{:S(2)}, u32[]{:S(2)}) collective-permute-start(bf16[2,256,1024]{2,1,0:T(8,128)(2,1)} %get-tuple-element.166), channel_id=1, source_target_pairs={{0,32},{32,0},{1,33},{33,1},{2,34},{34,2},{3,35},{35,3},{4,36},{36... | collective-permute-start | bytes 3145736 | tf_op jit(solution)/shard_map/ppermute | solution.py:643
  286.8 4.5 %projections.1 = bf16[1024,640]{1,0:T(8,128)(2,1)} custom-call(bf16[1024,1024]{1,0:T(8,128)(2,1)} %get-tuple-element.176.h_ref, bf16[1024,512]{1,0:T(8,128)(2,1)} %get-tuple-element.177.dqkv_ref, f32[1024,128]{1,0:T(8,128)} %get-tuple-element.178.sums_ref, f32[8,1024]{1,0:T(8,128)} %get-tuple-element.179.gain_ref), custom_call_target="tpu_custom_call" | custom-call | flops 1500000000 | bytes 5000000 | tf_op jit(solution)/shard_map/projections/pallas_call | solution.py:380
  291.2 5.1 %all-to-all-start.3 = ((bf16[128,8,640]{2,1,0:T(8,128)(2,1)}), bf16[128,8,640]{2,1,0:T(8,128)(2,1)S(1)}, u32[]{:S(2)}, u32[]{:S(2)}) async-start(bf16[128,8,640]{2,1,0:T(8,128)(2,1)} %bitcast.79), calls=%async_computation.4 | async-start | bytes 2621440 | tf_op jit(solution)/shard_map/all_to_all | solution.py:758
  297.2 3.3 collective-permute-start.38
  305.3 12.4 %all-to-all-done.3 = bf16[128,8,640]{2,1,0:T(8,128)(2,1)S(1)} async-done(((bf16[128,8,640]{2,1,0:T(8,128)(2,1)}), bf16[128,8,640]{2,1,0:T(8,128)(2,1)S(1)}, u32[]{:S(2)}, u32[]{:S(2)}) %all-to-all-start.3) | async-done | bytes 1310752 | tf_op jit(solution)/shard_map/all_to_all | solution.py:758
  322.8 2.5 finish.1
  327.7 3.4 %fusion.6 = (f32[1,256,1024]{2,1,0:T(8,128)}, bf16[1,256,1024]{2,1,0:T(8,128)(2,1)}) fusion(f32[256,1024]{1,0:T(8,128)S(1)} %copy-done.9, bf16[256,1024]{1,0:T(8,128)(2,1)S(1)} %bitcast.75, bf16[256,1024]{1,0:T(8,128)(2,1)} %collective-permute-done.37, f32[256]{0:T(256)S(1)} %broadcast_multiply_fusion, f32[1024]{0:T(1024)S(1)} %bitcast.86, ...), kind=kLoop, calls=%fused_computation.16 | loop fusion | flops 5242880 | bytes 7870465 | tf_op jit(solution)/shard_map/reshape | solution.py:777
  (185 shorter events, 64.1 us)
Async XLA Ops:
  10.2 38.3 %all-to-all-start = ((bf16[128,8,640]{2,1,0:T(8,128)(2,1)}), bf16[128,8,640]{2,1,0:T(8,128)(2,1)S(1)}, u32[]{:S(2)}, u32[]{:S(2)}) async-start(bf16[128,8,640]{2,1,0:T(8,128)(2,1)} %get-tuple-element.100), calls=%async_computation | async-start | bytes 2621440 | tf_op jit(solution)/shard_map/all_to_all | solution.py:693
  21.7 129.9 %all-gather.3.cloned.1.call-start = ((), (), s32[]{:S(2)}) async-start(), calls=%async_computation.6 | async-start | bytes 13369344 | tf_op jit(solution)/shard_map/all_gather | solution.py:698
  21.8 26.7 %collective-permute-start.2 = (bf16[256,1024]{1,0:T(8,128)(2,1)S(1)}, bf16[256,1024]{1,0:T(8,128)(2,1)S(1)}, u32[]{:S(2)}, u32[]{:S(2)}) collective-permute-start(bf16[256,1024]{1,0:T(8,128)(2,1)S(1)} %bitcast.71), channel_id=1, source_target_pairs={{0,64},{64,0},{1,65},{65,1},{2,66},{66,2},{3,67},{67,3},{4,68},{68... | collective-permute-start | bytes 1572872 | tf_op jit(solution)/shard_map/ppermute | solution.py:643
  23.3 25.2 %collective-permute-start.3 = (bf16[256,1024]{1,0:T(8,128)(2,1)S(1)}, bf16[256,1024]{1,0:T(8,128)(2,1)S(1)}, u32[]{:S(2)}, u32[]{:S(2)}) collective-permute-start(bf16[256,1024]{1,0:T(8,128)(2,1)S(1)} %bitcast.72), channel_id=1, source_target_pairs={{0,32},{32,0},{1,33},{33,1},{2,34},{34,2},{3,35},{35,3},{4,36},{36... | collective-permute-start | bytes 1572872 | tf_op jit(solution)/shard_map/ppermute | solution.py:643
  52.0 33.9 %collective-permute-start.10 = (bf16[256,1152]{1,0:T(8,128)(2,1)}, bf16[256,1152]{1,0:T(8,128)(2,1)S(1)}, u32[]{:S(2)}, u32[]{:S(2)}) collective-permute-start(bf16[256,1152]{1,0:T(8,128)(2,1)} %codes.1.refs_0_.refs_2_.gy_ref), channel_id=1, source_target_pairs={{0,3},{1,0},{2,1},{3,2},{4,7},{5,4},{6,5},{7,6},{8,11},{9,8},{10,9... | collective-permute-start | bytes 1769480 | tf_op jit(solution)/shard_map/ppermute | solution.py:643
  55.1 38.1 %collective-permute-start.11 = (bf16[256,1152]{1,0:T(8,128)(2,1)}, bf16[256,1152]{1,0:T(8,128)(2,1)S(1)}, u32[]{:S(2)}, u32[]{:S(2)}) collective-permute-start(bf16[256,1152]{1,0:T(8,128)(2,1)} %codes.1.refs_0_.refs_2_.gy_ref), channel_id=1, source_target_pairs={{0,2},{1,3},{2,0},{3,1},{4,6},{5,7},{6,4},{7,5},{8,10},{9,11},{10,... | collective-permute-start | bytes 1769480 | tf_op jit(solution)/shard_map/ppermute | solution.py:643
  55.2 39.1 %collective-permute-start.9 = (bf16[256,1152]{1,0:T(8,128)(2,1)}, bf16[256,1152]{1,0:T(8,128)(2,1)}, u32[]{:S(2)}, u32[]{:S(2)}) collective-permute-start(bf16[256,1152]{1,0:T(8,128)(2,1)} %codes.1.refs_0_.refs_2_.gy_ref), channel_id=1, source_target_pairs={{0,1},{1,2},{2,3},{3,0},{4,5},{5,6},{6,7},{7,4},{8,9},{9,10},{10,1... | collective-permute-start | bytes 1769480 | tf_op jit(solution)/shard_map/ppermute | solution.py:643
  56.2 16.0 %collective-permute-start.4 = (bf16[256,1024]{1,0:T(8,128)(2,1)}, bf16[256,1024]{1,0:T(8,128)(2,1)}, u32[]{:S(2)}, u32[]{:S(2)}) collective-permute-start(bf16[256,1024]{1,0:T(8,128)(2,1)} %copy-done.35), channel_id=1, source_target_pairs={{0,32},{32,0},{1,33},{33,1},{2,34},{34,2},{3,35},{35,3},{4,36},{36... | collective-permute-start | bytes 1572872 | tf_op jit(solution)/shard_map/ppermute | solution.py:643
  60.0 35.1 %all-to-all-start.1 = ((bf16[32,8,2048]{2,1,0:T(8,128)(2,1)}), bf16[32,8,2048]{2,1,0:T(8,128)(2,1)S(1)}, u32[]{:S(2)}, u32[]{:S(2)}) async-start(bf16[32,8,2048]{2,1,0:T(8,128)(2,1)} %broadcast_in_dim.4), calls=%async_computation.1 | async-start | bytes 2097152 | tf_op jit(solution)/shard_map/all_to_all | solution.py:708
  68.6 249.9 %reduce-scatter.2.cloned.1.call-start = ((), (), s32[]{:S(2)}) async-start(), calls=%async_computation.5 | async-start | bytes 13369344 | tf_op jit(solution)/shard_map/reduce_scatter | solution.py:733
  84.4 9.9 %collective-permute-start.5 = (bf16[256,256]{1,0:T(8,128)(2,1)}, bf16[256,256]{1,0:T(8,128)(2,1)S(1)}, u32[]{:S(2)}, u32[]{:S(2)}) collective-permute-start(bf16[256,256]{1,0:T(8,128)(2,1)} %get-tuple-element.108), channel_id=1, source_target_pairs={{0,64},{64,0},{1,65},{65,1},{2,66},{66,2},{3,67},{67,3},{4,68},{68... | collective-permute-start | bytes 393224 | tf_op jit(solution)/shard_map/ppermute | solution.py:643
  85.9 8.4 %collective-permute-start.6 = (bf16[256,256]{1,0:T(8,128)(2,1)}, bf16[256,256]{1,0:T(8,128)(2,1)S(1)}, u32[]{:S(2)}, u32[]{:S(2)}) collective-permute-start(bf16[256,256]{1,0:T(8,128)(2,1)} %get-tuple-element.109), channel_id=1, source_target_pairs={{0,32},{32,0},{1,33},{33,1},{2,34},{34,2},{3,35},{35,3},{4,36},{36... | collective-permute-start | bytes 393224 | tf_op jit(solution)/shard_map/ppermute | solution.py:643
  97.2 10.0 %collective-permute-start.19 = (bf16[256,1152]{1,0:T(8,128)(2,1)}, bf16[256,1152]{1,0:T(8,128)(2,1)}, u32[]{:S(2)}, u32[]{:S(2)}) collective-permute-start(bf16[256,1152]{1,0:T(8,128)(2,1)} %copy-done.11), channel_id=1, source_target_pairs={{0,32},{32,0},{1,33},{33,1},{2,34},{34,2},{3,35},{35,3},{4,36},{36... | collective-permute-start | bytes 1769480 | tf_op jit(solution)/shard_map/ppermute | solution.py:643
  97.3 10.0 %collective-permute-start.20 = (bf16[256,1152]{1,0:T(8,128)(2,1)}, bf16[256,1152]{1,0:T(8,128)(2,1)}, u32[]{:S(2)}, u32[]{:S(2)}) collective-permute-start(bf16[256,1152]{1,0:T(8,128)(2,1)} %copy-done.12), channel_id=1, source_target_pairs={{0,32},{32,0},{1,33},{33,1},{2,34},{34,2},{3,35},{35,3},{4,36},{36... | collective-permute-start | bytes 1769480 | tf_op jit(solution)/shard_map/ppermute | solution.py:643
  103.9 14.4 %collective-permute-start.16 = (bf16[256,1024]{1,0:T(8,128)(2,1)}, bf16[256,1024]{1,0:T(8,128)(2,1)S(1)}, u32[]{:S(2)}, u32[]{:S(2)}) collective-permute-start(bf16[256,1024]{1,0:T(8,128)(2,1)} %get-tuple-element.118.refs_0_), channel_id=1, source_target_pairs={{0,32},{32,0},{1,33},{33,1},{2,34},{34,2},{3,35},{35,3},{4,36},{36... | collective-permute-start | bytes 1572872 | tf_op jit(solution)/shard_map/ppermute | solution.py:643
  104.5 20.8 %collective-permute-start.13 = (bf16[256,1024]{1,0:T(8,128)(2,1)}, bf16[256,1024]{1,0:T(8,128)(2,1)S(1)}, u32[]{:S(2)}, u32[]{:S(2)}) collective-permute-start(bf16[256,1024]{1,0:T(8,128)(2,1)} %get-tuple-element.118.refs_0_), channel_id=1, source_target_pairs={{0,1},{1,2},{2,3},{3,0},{4,5},{5,6},{6,7},{7,4},{8,9},{9,10},{10,1... | collective-permute-start | bytes 1572872 | tf_op jit(solution)/shard_map/ppermute | solution.py:643
  104.5 24.9 %collective-permute-start.14 = (bf16[256,1024]{1,0:T(8,128)(2,1)}, bf16[256,1024]{1,0:T(8,128)(2,1)S(1)}, u32[]{:S(2)}, u32[]{:S(2)}) collective-permute-start(bf16[256,1024]{1,0:T(8,128)(2,1)} %get-tuple-element.118.refs_0_), channel_id=1, source_target_pairs={{0,3},{1,0},{2,1},{3,2},{4,7},{5,4},{6,5},{7,6},{8,11},{9,8},{10,9... | collective-permute-start | bytes 1572872 | tf_op jit(solution)/shard_map/ppermute | solution.py:643
  107.2 23.1 %collective-permute-start.15 = (bf16[256,1024]{1,0:T(8,128)(2,1)}, bf16[256,1024]{1,0:T(8,128)(2,1)S(1)}, u32[]{:S(2)}, u32[]{:S(2)}) collective-permute-start(bf16[256,1024]{1,0:T(8,128)(2,1)} %get-tuple-element.118.refs_0_), channel_id=1, source_target_pairs={{0,2},{1,3},{2,0},{3,1},{4,6},{5,7},{6,4},{7,5},{8,10},{9,11},{10,... | collective-permute-start | bytes 1572872 | tf_op jit(solution)/shard_map/ppermute | solution.py:643
  199.8 27.5 %collective-permute-start.25 = (bf16[256,1152]{1,0:T(8,128)(2,1)S(1)}, bf16[256,1152]{1,0:T(8,128)(2,1)S(1)}, u32[]{:S(2)}, u32[]{:S(2)}) collective-permute-start(bf16[256,1152]{1,0:T(8,128)(2,1)S(1)} %get-tuple-element.188), channel_id=1, source_target_pairs={{0,3},{1,0},{2,1},{3,2},{4,7},{5,4},{6,5},{7,6},{8,11},{9,8},{10,9... | collective-permute-start | bytes 1769480 | tf_op jit(solution)/shard_map/ppermute | solution.py:643
  202.4 24.8 %collective-permute-start.26 = (bf16[256,1152]{1,0:T(8,128)(2,1)S(1)}, bf16[256,1152]{1,0:T(8,128)(2,1)S(1)}, u32[]{:S(2)}, u32[]{:S(2)}) collective-permute-start(bf16[256,1152]{1,0:T(8,128)(2,1)S(1)} %get-tuple-element.187), channel_id=1, source_target_pairs={{0,1},{1,2},{2,3},{3,0},{4,5},{5,6},{6,7},{7,4},{8,9},{9,10},{10,1... | collective-permute-start | bytes 1769480 | tf_op jit(solution)/shard_map/ppermute | solution.py:643
  202.4 27.1 %collective-permute-start.27 = (bf16[256,1152]{1,0:T(8,128)(2,1)S(1)}, bf16[256,1152]{1,0:T(8,128)(2,1)S(1)}, u32[]{:S(2)}, u32[]{:S(2)}) collective-permute-start(bf16[256,1152]{1,0:T(8,128)(2,1)S(1)} %get-tuple-element.186), channel_id=1, source_target_pairs={{0,2},{1,3},{2,0},{3,1},{4,6},{5,7},{6,4},{7,5},{8,10},{9,11},{10,... | collective-permute-start | bytes 1769480 | tf_op jit(solution)/shard_map/ppermute | solution.py:643
  218.7 34.2 %collective-permute-start.29 = (bf16[4,256,1024]{2,1,0:T(8,128)(2,1)}, bf16[4,256,1024]{2,1,0:T(8,128)(2,1)S(1)}, u32[]{:S(2)}, u32[]{:S(2)}) collective-permute-start(bf16[4,256,1024]{2,1,0:T(8,128)(2,1)} %get-tuple-element.143), channel_id=1, source_target_pairs={{0,32},{32,0},{1,33},{33,1},{2,34},{34,2},{3,35},{35,3},{4,36},{36... | collective-permute-start | bytes 6291464 | tf_op jit(solution)/shard_map/ppermute | solution.py:643
  238.2 12.2 %collective-permute-start.28 = (bf16[2,256,1024]{2,1,0:T(8,128)(2,1)}, bf16[2,256,1024]{2,1,0:T(8,128)(2,1)S(1)}, u32[]{:S(2)}, u32[]{:S(2)}) collective-permute-start(bf16[2,256,1024]{2,1,0:T(8,128)(2,1)} %get-tuple-element.139), channel_id=1, source_target_pairs={{0,32},{32,0},{1,33},{33,1},{2,34},{34,2},{3,35},{35,3},{4,36},{36... | collective-permute-start | bytes 3145736 | tf_op jit(solution)/shard_map/ppermute | solution.py:643
  242.0 12.9 %collective-permute-start.30 = (bf16[256,256]{1,0:T(8,128)(2,1)}, bf16[256,256]{1,0:T(8,128)(2,1)S(1)}, u32[]{:S(2)}, u32[]{:S(2)}) collective-permute-start(bf16[256,256]{1,0:T(8,128)(2,1)} %get-tuple-element.145), channel_id=1, source_target_pairs={{0,64},{64,0},{1,65},{65,1},{2,66},{66,2},{3,67},{67,3},{4,68},{68... | collective-permute-start | bytes 393224 | tf_op jit(solution)/shard_map/ppermute | solution.py:643
  242.5 12.4 %collective-permute-start.31 = (bf16[256,256]{1,0:T(8,128)(2,1)}, bf16[256,256]{1,0:T(8,128)(2,1)S(1)}, u32[]{:S(2)}, u32[]{:S(2)}) collective-permute-start(bf16[256,256]{1,0:T(8,128)(2,1)} %get-tuple-element.146), channel_id=1, source_target_pairs={{0,32},{32,0},{1,33},{33,1},{2,34},{34,2},{3,35},{35,3},{4,36},{36... | collective-permute-start | bytes 393224 | tf_op jit(solution)/shard_map/ppermute | solution.py:643
  254.9 25.5 %collective-permute-start.34 = (bf16[256,1024]{1,0:T(8,128)(2,1)}, bf16[256,1024]{1,0:T(8,128)(2,1)S(1)}, u32[]{:S(2)}, u32[]{:S(2)}) collective-permute-start(bf16[256,1024]{1,0:T(8,128)(2,1)} %get-tuple-element.161), channel_id=1, source_target_pairs={{0,3},{1,0},{2,1},{3,2},{4,7},{5,4},{6,5},{7,6},{8,11},{9,8},{10,9... | collective-permute-start | bytes 1572872 | tf_op jit(solution)/shard_map/ppermute | solution.py:643
  255.3 25.2 %collective-permute-start.35 = (bf16[256,1024]{1,0:T(8,128)(2,1)S(1)}, bf16[256,1024]{1,0:T(8,128)(2,1)S(1)}, u32[]{:S(2)}, u32[]{:S(2)}) collective-permute-start(bf16[256,1024]{1,0:T(8,128)(2,1)S(1)} %get-tuple-element.162), channel_id=1, source_target_pairs={{0,1},{1,2},{2,3},{3,0},{4,5},{5,6},{6,7},{7,4},{8,9},{9,10},{10,1... | collective-permute-start | bytes 1572872 | tf_op jit(solution)/shard_map/ppermute | solution.py:643
  256.5 24.0 %all-to-all-start.2 = ((bf16[64,8,1024]{2,1,0:T(8,128)(2,1)}), bf16[64,8,1024]{2,1,0:T(8,128)(2,1)S(1)}, u32[]{:S(2)}, u32[]{:S(2)}) async-start(bf16[64,8,1024]{2,1,0:T(8,128)(2,1)} %bitcast.18), calls=%async_computation.2 | async-start | bytes 2097152 | tf_op jit(solution)/shard_map/all_to_all | solution.py:745
  280.5 21.0 %collective-permute-start.36 = (bf16[2,256,1024]{2,1,0:T(8,128)(2,1)}, bf16[2,256,1024]{2,1,0:T(8,128)(2,1)}, u32[]{:S(2)}, u32[]{:S(2)}) collective-permute-start(bf16[2,256,1024]{2,1,0:T(8,128)(2,1)} %get-tuple-element.166), channel_id=1, source_target_pairs={{0,32},{32,0},{1,33},{33,1},{2,34},{34,2},{3,35},{35,3},{4,36},{36... | collective-permute-start | bytes 3145736 | tf_op jit(solution)/shard_map/ppermute | solution.py:643
  291.2 26.5 %all-to-all-start.3 = ((bf16[128,8,640]{2,1,0:T(8,128)(2,1)}), bf16[128,8,640]{2,1,0:T(8,128)(2,1)S(1)}, u32[]{:S(2)}, u32[]{:S(2)}) async-start(bf16[128,8,640]{2,1,0:T(8,128)(2,1)} %bitcast.79), calls=%async_computation.4 | async-start | bytes 2621440 | tf_op jit(solution)/shard_map/all_to_all | solution.py:758
  297.2 29.0 %collective-permute-start.38 = (bf16[256,1024]{1,0:T(8,128)(2,1)}, bf16[256,1024]{1,0:T(8,128)(2,1)}, u32[]{:S(2)}, u32[]{:S(2)}) collective-permute-start(bf16[256,1024]{1,0:T(8,128)(2,1)} %get-tuple-element.167), channel_id=1, source_target_pairs={{0,2},{1,3},{2,0},{3,1},{4,6},{5,7},{6,4},{7,5},{8,10},{9,11},{10,... | collective-permute-start | bytes 1572872 | tf_op jit(solution)/shard_map/ppermute | solution.py:643
  304.0 22.2 %collective-permute-start.37 = (bf16[256,1024]{1,0:T(8,128)(2,1)}, bf16[256,1024]{1,0:T(8,128)(2,1)}, u32[]{:S(2)}, u32[]{:S(2)}) collective-permute-start(bf16[256,1024]{1,0:T(8,128)(2,1)} %select_bitcast_fusion), channel_id=1, source_target_pairs={{0,64},{64,0},{1,65},{65,1},{2,66},{66,2},{3,67},{67,3},{4,68},{68... | collective-permute-start | bytes 1572872 | tf_op jit(solution)/shard_map/ppermute | solution.py:643
  (56 other events, 387.2 us)
Sparse Core Ops, SparseCore 0:
  48.7 102.9 all-gather.2
  193.1 100.2 reduce-scatter.1
